TPU v7x, 32 devices: a whole 2x2x4 slice. The times are simulated.
32 devices in a mesh: gx: 2 (over x), gy: 8 (over z, y), gz: 2 (over core).
Axes of the slice: x: 2, y: 2, z: 4, core: 2. Of those that a mesh axis runs over, the one named last changes fastest.
Arguments:
- tensor: float32 [64, 256, 512], P('gx', 'gy', 'gz'), may hold values from -6 to 6
- core: float32 [256, 256, 128], P('gx', 'gy', 'gz'), may hold values from -6 to 6
- factor_one: float32 [64, 256], P('gx'), may hold values from -0.375 to 0.375
- factor_two: float32 [256, 256], P('gy'), may hold values from -0.375 to 0.375
- factor_three: float32 [512, 128], P('gz'), may hold values from -0.5 to 0.5
Outputs:
- residual: float32 [64, 256, 512], P('gx', 'gy', 'gz')
- grad_one: float32 [64, 256], P('gx')
- grad_two: float32 [256, 256], P('gy')
- grad_three: float32 [512, 128], P('gz')
All inputs are finite; a program needn't handle non-finite values.
Results may differ from a plain program's by a relative error of at most 0.00007.
Values sent between devices are 32-bit elements; how exact they have to be, the bound alone decides.
No kernel may reach another device: no remote copies, remote signals or barrier semaphores. Data moves between devices by JAX's collectives and lax.ppermute only.
A program may use at most 64 MiB of HBM per device.

v0:
```python
import jax
import jax.numpy as jnp
from jax import lax
from jax.sharding import PartitionSpec as P

highest = lax.Precision.HIGHEST


def local(tensor, core, factor_one, factor_two, factor_three):
    rows_one, rows_two, rows_three = tensor.shape
    total_one = rows_one * lax.axis_size("gx")
    total_two = rows_two * lax.axis_size("gy")
    total_three = rows_three * lax.axis_size("gz")
    core_rows = lax.all_gather(core, "gx", axis=0, tiled=True)
    after_one = jnp.einsum("ar,rst->ast", factor_one, core_rows, precision=highest)
    after_two = jnp.einsum(
        "bs,ast->abt",
        factor_two,
        lax.all_gather(after_one, "gy", axis=1, tiled=True),
        precision=highest,
    )
    after_full = lax.all_gather(after_two, "gz", axis=2, tiled=True)
    approx = jnp.einsum("abt,ct->abc", after_full, factor_three, precision=highest)
    residual = approx - tensor
    folded = jnp.einsum("abc,ct->abt", residual, factor_three, precision=highest)
    wide_one = jnp.einsum("abt,bs->ast", folded, factor_two, precision=highest)
    partial_one = lax.psum_scatter(wide_one, "gy", scatter_dimension=1, tiled=True)
    share_one = lax.psum_scatter(partial_one, "gz", scatter_dimension=2, tiled=True)
    wide_two = jnp.einsum("abt,ar->rbt", folded, factor_one, precision=highest)
    partial_two = lax.psum_scatter(wide_two, "gx", scatter_dimension=0, tiled=True)
    share_two = lax.psum_scatter(partial_two, "gz", scatter_dimension=2, tiled=True)
    core_cols = lax.all_gather(core, "gy", axis=1, tiled=True)
    term_one = jnp.einsum("ast,rst->ar", share_one, core_rows, precision=highest)
    term_two = jnp.einsum("rbt,rst->bs", share_two, core_cols, precision=highest)
    term_three = jnp.einsum("abc,abt->ct", residual, after_full, precision=highest)
    grad_one = lax.psum(term_one, ("gy", "gz"))
    grad_two = lax.psum(term_two, ("gx", "gz"))
    grad_three = lax.psum(term_three, ("gx", "gy"))
    grad_one = grad_one / jnp.sqrt(jnp.float32(total_two * total_three))
    grad_two = grad_two / jnp.sqrt(jnp.float32(total_one * total_three))
    grad_three = grad_three / jnp.sqrt(jnp.float32(total_one * total_two))
    return (residual, grad_one, grad_two, grad_three)


def solution(mesh):
    placed = (P("gx", "gy", "gz"), P("gx", "gy", "gz"), P("gx", None), P("gy", None), P("gz", None))
    return jax.shard_map(
        local,
        mesh=mesh,
        in_specs=placed,
        out_specs=(P("gx", "gy", "gz"), P("gx", None), P("gy", None), P("gz", None)),
        check_vma=False,
    )
```

profile of v0, /device:TPU:0, one launch (start us, length us, event | category | flops | bytes accessed | tf_op | source)
XLA Modules:
  0.0 581.1 jit_solution(2893012608638847270)
XLA Ops:
  8.0 37.4 %all-gather.4.cloned.1.call-done = f32[256,32,64]{0,2,1:T(8,128)} async-done(((f32[128,32,64]{0,2,1:T(8,128)}), f32[256,32,64]{0,2,1:T(8,128)}) %all-gather.4.cloned.1.call-update) | async-done | bytes 2097168 | tf_op jit(solution)/shard_map/all_gather | solution.py:14
  45.4 4.5 fusion.8
  51.1 73.5 %all-gather.6.cloned.1.call-done = f32[32,256,64]{2,1,0:T(8,128)} async-done(((f32[32,32,64]{2,1,0:T(8,128)}), f32[32,256,64]{2,1,0:T(8,128)}) %all-gather.6.cloned.1.call-update) | async-done | bytes 2097168 | tf_op jit(solution)/shard_map/all_gather | solution.py:19
  124.6 4.7 convolution_bitcast_fusion.1
  130.2 3.3 all_gather.14
  134.8 2.2 convolution_subtract_fusion
  139.0 5.1 fusion.4
  144.1 5.5 copy.15
  149.8 1.9 copy.16
  151.7 5.0 convolution_bitcast_fusion
  157.9 2.5 convolution_bitcast_fusion.2
  160.4 75.7 %reduce-scatter.7.cloned.1.call-done = f32[32,32,128]{2,0,1:T(8,128)} async-done(((f32[32,256,128]{2,0,1:T(8,128)}), f32[32,32,128]{2,0,1:T(8,128)}) %reduce-scatter.7.cloned.1.call-update) | async-done | bytes 524304 | tf_op jit(solution)/shard_map/reduce_scatter | solution.py:27
  236.1 2.9 copy.17
  239.0 1.8 reshape.14
  240.9 1.6 copy.12
  242.5 49.9 %reduce-scatter.9.cloned.1.call-done = f32[128,32,128]{0,1,2:T(8,128)} async-done(((f32[256,32,128]{0,1,2:T(8,128)}), f32[128,32,128]{0,1,2:T(8,128)}) %reduce-scatter.9.cloned.1.call-update) | async-done | bytes 2097168 | tf_op jit(solution)/shard_map/reduce_scatter | solution.py:30
  292.5 110.0 %all-reduce.2.cloned.1.call-done = f32[256,128]{1,0:T(8,128)} async-done(((f32[256,128]{1,0:T(8,128)}), f32[256,128]{1,0:T(8,128)}) %all-reduce.2.cloned.1.call-update) | async-done | bytes 131088 | tf_op jit(solution)/shard_map/psum | solution.py:38
  404.1 7.6 %reduce-scatter.13.cloned.1.call-done = f32[64,1024]{1,0:T(8,128)} async-done(((f32[128,1024]{1,0:T(8,128)}), f32[64,1024]{1,0:T(8,128)}) %reduce-scatter.13.cloned.1.call-update) | async-done | bytes 262160
  412.9 2.3 convolution_bitcast_fusion.4
  415.2 63.8 %psum.21 = f32[32,256]{1,0:T(8,128)S(1)} all-reduce(f32[32,256]{1,0:T(8,128)S(1)} %convolution_bitcast_fusion.4), channel_id=1, replica_groups=mesh['gx'=2,'gy'=8,'gz'=2] {'gy','gz'}, use_global_device_ids=true, to_apply=%region_2.0 | all-reduce | flops 8192 | bytes 65536 | tf_op jit(solution)/shard_map/psum | solution.py:36
  479.6 60.9 %all-gather.8.cloned.1.call-done = f32[128,256,64]{0,1,2:T(8,128)} async-done(((f32[128,32,64]{0,1,2:T(8,128)}), f32[128,256,64]{0,1,2:T(8,128)}) %all-gather.8.cloned.1.call-update) | async-done | bytes 8388624 | tf_op jit(solution)/shard_map/all_gather | solution.py:32
  540.6 10.2 %reduce-scatter.11.cloned.1.call-done = f32[128,32,64]{0,1,2:T(8,128)} async-done(((f32[128,32,128]{0,1,2:T(8,128)}), f32[128,32,64]{0,1,2:T(8,128)}) %reduce-scatter.11.cloned.1.call-update) | async-done | bytes 1048592 | tf_op jit(solution)/shard_map/reduce_scatter | solution.py:31
  550.8 11.1 %convolution_bitcast_fusion.3 = f32[32,256]{1,0:T(8,128)S(1)} fusion(f32[128,32,64]{0,1,2:T(8,128)} %reduce-scatter.11.cloned.1.call-done, f32[128,256,64]{0,1,2:T(8,128)} %all-gather.8.cloned.1.call-done), kind=kOutput, calls=%fused_computation.4 | convolution fusion | flops 805306368 | bytes 9469952 | tf_op jit(solution)/shard_map/rbt,rst->bs/dot_general | solution.py:34
  561.8 11.8 %psum.22 = f32[32,256]{1,0:T(8,128)S(1)} all-reduce(f32[32,256]{1,0:T(8,128)S(1)} %convolution_bitcast_fusion.3), channel_id=1, replica_groups=mesh['gx'=2,'gy'=8,'gz'=2] {'gx','gz'}, use_global_device_ids=true, to_apply=%region_5.0 | all-reduce | flops 8192 | bytes 65536 | tf_op jit(solution)/shard_map/psum | solution.py:37
  (38 shorter events, 11.8 us)
Async XLA Ops:
  7.2 127.7 %copy-start = (f32[256,128]{1,0:T(8,128)S(1)}, f32[256,128]{1,0:T(8,128)}, u32[]{:S(2)}) copy-start(f32[256,128]{1,0:T(8,128)} %param.9) | copy-start | bytes 393220
  7.2 38.2 %all-gather.4.cloned.1.call-start = ((), (), s32[]{:S(2)}) async-start(), calls=%async_computation.4 | async-start | bytes 3145728 | tf_op jit(solution)/shard_map/all_gather | solution.py:14
  7.9 116.6 %copy-start.5 = (f32[32,256]{1,0:T(8,128)S(1)}, f32[32,256]{1,0:T(8,128)}, u32[]{:S(2)}) copy-start(f32[32,256]{1,0:T(8,128)} %param.8) | copy-start | bytes 98308
  7.9 116.6 %all-gather.6.cloned.1.call-start = ((), (), s32[]{:S(2)}) async-start(), calls=%async_computation.5 | async-start | bytes 4718592 | tf_op jit(solution)/shard_map/all_gather | solution.py:19
  51.0 185.1 %reduce-scatter.7.cloned.1.call-start = ((), (), s32[]{:S(2)}) async-start(), calls=%async_computation.6 | async-start | bytes 4718592 | tf_op jit(solution)/shard_map/reduce_scatter | solution.py:27
  137.0 1.0 copy-start.3
  149.6 2.1 copy-start.6
  149.6 142.9 %reduce-scatter.9.cloned.1.call-start = ((), (), s32[]{:S(2)}) async-start(), calls=%async_computation.7 | async-start | bytes 6291456 | tf_op jit(solution)/shard_map/reduce_scatter | solution.py:30
  156.7 1.2 copy-start.4
  156.7 245.8 %all-reduce.2.cloned.1.call-start = ((), (), s32[]{:S(2)}) async-start(), calls=%async_computation.10 | async-start | bytes 262144 | tf_op jit(solution)/shard_map/psum | solution.py:38
  160.4 251.2 %reduce-scatter.13.cloned.1.call-start = ((), (), s32[]{:S(2)}) async-start(), calls=%async_computation.11 | async-start | bytes 786432
  239.0 1.9 copy-start.2
  240.8 299.8 %all-gather.8.cloned.1.call-start = ((), (), s32[]{:S(2)}) async-start(), calls=%async_computation.9 | async-start | bytes 9437184 | tf_op jit(solution)/shard_map/all_gather | solution.py:32
  242.5 170.4 %copy-start.1 = (f32[256,32,64]{0,2,1:T(8,128)S(1)}, f32[256,32,64]{0,2,1:T(8,128)}, u32[]{:S(2)}) copy-start(f32[256,32,64]{0,2,1:T(8,128)} %all-gather.4.cloned.1.call-done) | copy-start | bytes 6291460
  242.5 308.3 %reduce-scatter.11.cloned.1.call-start = ((), (), s32[]{:S(2)}) async-start(), calls=%async_computation.8 | async-start | bytes 3145728 | tf_op jit(solution)/shard_map/reduce_scatter | solution.py:31
Sparse Core Ops, SparseCore 0:
  9.6 35.7 all-gather.3
  51.1 73.3 all-gather.5
  149.7 86.3 reduce-scatter.6
  238.4 54.0 reduce-scatter.8
  298.3 104.1 all-reduce.1
  404.6 6.9 reduce-scatter.12
  414.1 126.4 all-gather.7
  542.9 7.8 reduce-scatter.10
where the time goes:
time: 582 us; the launch traced here: 581 us
  waiting for transfers between devices  426 us (73%)
  blocking collectives  78.9 us (14%)
  matrix products  38.3 us (7%)
  local copies, waits for them, and re-layouts  20.4 us (4%)
  between operations  14.3 us (2%)
    psum x1, waiting for transfers between devices, local(): grad_three = lax.psum(term_three, ('gx', 'gy'))  110 us
    reduce_scatter x1, waiting for transfers between devices, local(): lax.psum_scatter(wide_one, 'gy', scatter_dimension=1, tiled=True)  75.7 us
    all_gather x1, waiting for transfers between devices, local(): lax.all_gather(after_one, 'gy', axis=1, tiled=True)  73.5 us
    psum x1, blocking collectives, local(): grad_one = lax.psum(term_one, ('gy', 'gz'))  63.8 us
    all_gather x1, waiting for transfers between devices, local(): core_cols = lax.all_gather(core, 'gy', axis=1, tiled=True)  60.9 us
    reduce_scatter x1, waiting for transfers between devices, local(): lax.psum_scatter(wide_two, 'gx', scatter_dimension=0, tiled=True)  49.9 us
    all_gather x1, waiting for transfers between devices, local(): core_rows = lax.all_gather(core, 'gx', axis=0, tiled=True)  37.4 us
    psum x1, blocking collectives, local(): grad_two = lax.psum(term_two, ('gx', 'gz'))  11.8 us
  transfers between devices with their start and end apart: 8, of which 8 were waited for; matrix products, arithmetic and copies ran while one was open for 4% of the time, Pallas kernels for 0%

commit v1 on v0

v1 whole, which is shorter than its diff:
```python
import jax
import jax.numpy as jnp
from jax import lax
from jax.sharding import PartitionSpec as P

highest = lax.Precision.HIGHEST


def dot(spec, left, right):
    return jnp.einsum(spec, left, right, precision=highest)


def swap(x, axis):
    return lax.ppermute(x, axis, [(0, 1), (1, 0)])


def part(x, index):
    return lax.dynamic_index_in_dim(x, index, 0, keepdims=False)


def in_order(axis, mine, other):
    first = lax.axis_index(axis) == 0
    return jnp.stack([jnp.where(first, mine, other), jnp.where(first, other, mine)])


def trade(x, axis):
    if lax.axis_size(axis) != 2:
        return lax.all_to_all(x, axis, 0, 0, tiled=True)
    me = lax.axis_index(axis)
    return in_order(axis, part(x, me), swap(part(x, 1 - me), axis))


def gather(x, axis):
    if lax.axis_size(axis) != 2:
        return lax.all_gather(x, axis)
    return in_order(axis, x, swap(x, axis))


def reduce_scatter(x, axis):
    if lax.axis_size(axis) != 2:
        return lax.psum_scatter(x, axis, scatter_dimension=0)
    me = lax.axis_index(axis)
    return part(x, me) + swap(part(x, 1 - me), axis)


def total(x, axis):
    if lax.axis_size(axis) != 2:
        return lax.psum(x, axis)
    return x + swap(x, axis)


def local(tensor, core, factor_one, factor_two, factor_three):
    nx, ny, nz = lax.axis_size("gx"), lax.axis_size("gy"), lax.axis_size("gz")
    i, j, k = tensor.shape
    r, s, t = core.shape
    e, q, full_t, full_s, full_r = i // (ny * nz), s // nz, t * nz, s * ny, r * nx
    half_j, half_s = j // nz, full_s // nz

    own = trade(core.reshape(r, nz, q, t).transpose(1, 0, 2, 3), "gz")
    own = own.transpose(1, 2, 0, 3).reshape(r, q, full_t)
    rows = trade(factor_one.reshape(i, nx, r).transpose(1, 0, 2), "gx").reshape(nx * i, r)

    folded_tensor = dot("abc,ct->abt", tensor, factor_three)
    folded_tensor = reduce_scatter(folded_tensor.reshape(nz, ny, e * j, full_t), "gz")
    mine_two = part(factor_two.reshape(nz, half_j, full_s), lax.axis_index("gz"))
    mine_two = mine_two.reshape(half_j, ny, nz, q).transpose(2, 0, 1, 3).reshape(nz * half_j, half_s)
    early = jnp.concatenate(
        [folded_tensor, jnp.broadcast_to(mine_two.reshape(1, -1, full_t), (ny, nz * half_j * half_s // full_t, full_t))],
        axis=1,
    )
    early = lax.all_to_all(early, "gy", 0, 0, tiled=True)
    folded_tensor = early[:, : e * j].reshape(ny, e, j, full_t).transpose(1, 0, 2, 3).reshape(e, ny * j, full_t)
    all_two = gather(early[:, e * j :].reshape(ny, nz, half_j, half_s), "gz")
    all_two = all_two.transpose(1, 0, 3, 2, 4).reshape(ny * j, full_s)
    gram = total(dot("ct,cu->tu", factor_three, factor_three), "gz")

    after_one = dot("ar,rst->ast", rows, own).reshape(nx, i, q, full_t)
    after_one = reduce_scatter(after_one, "gx").reshape(nz * ny, e, q, full_t)
    after_one = lax.all_to_all(after_one, ("gz", "gy"), 0, 0, tiled=True)
    after_one = after_one.transpose(1, 0, 2, 3).reshape(e, full_s, full_t)

    after_two = dot("bs,ast->abt", all_two, after_one)
    moved = after_two.reshape(e, ny, j, full_t).transpose(1, 0, 2, 3)
    moved = lax.all_to_all(moved, "gy", 0, 0, tiled=True).reshape(ny * e, j, full_t)

    folded = dot("abt,tu->abu", after_two, gram) - folded_tensor
    wide_one = dot("abt,bs->ast", folded, all_two)
    term_two = dot("abt,ast->bs", folded, after_one)

    after_full = gather(moved, "gz").reshape(i, j, full_t)
    residual = dot("abt,ct->abc", after_full, factor_three) - tensor
    term_three = dot("abc,abt->ct", residual, after_full)

    late = jnp.concatenate(
        [
            wide_one.reshape(e, nz * ny, q, full_t).transpose(1, 0, 2, 3).reshape(nz * ny, e * q, full_t),
            term_two.reshape(ny, j, nz, half_s).transpose(2, 0, 1, 3).reshape(nz * ny, -1, full_t),
            term_three.reshape(ny, nz, -1, full_t).transpose(1, 0, 2, 3).reshape(nz * ny, -1, full_t),
        ],
        axis=1,
    )
    late = lax.all_to_all(late, ("gz", "gy"), 0, 0, tiled=True)
    edge_one, edge_two = e * q, e * q + j * half_s // full_t
    share_one = late[:, :edge_one].reshape(i, q, full_t)
    share_two = late[:, edge_one:edge_two].sum(axis=0)
    share_three = late[:, edge_two:].reshape(nz, ny, -1, full_t).sum(axis=1)
    every_core = gather(own, "gx")
    term_one = dot("ast,xrst->axr", share_one, every_core).reshape(i, nz, full_r // nz).transpose(1, 0, 2)
    term_one = reduce_scatter(term_one, "gz")

    share_two = total(share_two, "gx").reshape(j, half_s)
    share_three = total(share_three, "gx")
    share_three = trade(share_three, "gz").reshape(-1, full_t)
    grad_two = gather(share_two, "gz").reshape(nz, j, ny, q).transpose(1, 2, 0, 3).reshape(j, full_s)

    last = jnp.concatenate([term_one.reshape(-1, full_t), share_three], axis=0)
    last = lax.all_to_all(jnp.broadcast_to(last[None], (ny,) + last.shape), "gy", 0, 0, tiled=True)
    rows_one = i * (full_r // nz) // full_t
    grad_one = last[:, :rows_one].sum(axis=0).reshape(i, full_r // nz)
    grad_one = gather(grad_one, "gz").transpose(1, 0, 2).reshape(i, full_r)
    grad_three = last[:, rows_one:].reshape(k, full_t)

    grad_one = grad_one / jnp.sqrt(jnp.float32(j * ny * k * nz))
    grad_two = grad_two / jnp.sqrt(jnp.float32(i * nx * k * nz))
    grad_three = grad_three / jnp.sqrt(jnp.float32(i * nx * j * ny))
    return (residual, grad_one, grad_two, grad_three)


def solution(mesh):
    placed = (P("gx", "gy", "gz"), P("gx", "gy", "gz"), P("gx", None), P("gy", None), P("gz", None))
    return jax.shard_map(
        local,
        mesh=mesh,
        in_specs=placed,
        out_specs=(P("gx", "gy", "gz"), P("gx", None), P("gy", None), P("gz", None)),
        check_vma=False,
    )
```

time: 582 us -> 125 us (0.21)
  waiting for transfers between devices: 426 us -> 50.1 us
  blocking collectives: 78.9 us -> 0 us
  starting transfers between devices: 0.51 us -> 33 us
  matrix products: 38.3 us -> 18 us
  between operations: 14.3 us -> 1.07 us
  local copies, waits for them, and re-layouts: 20.4 us -> 12.3 us
  other arithmetic: 2.81 us -> 9.33 us
    all_gather x3 -> x0, waiting for transfers between devices: 172 us -> none  [the longest x1 73.5 us: local(): lax.all_gather(after_one, 'gy', axis=1, tiled=True)]
    reduce_scatter x3 -> x0, waiting for transfers between devices: 136 us -> none  [the longest x1 75.7 us: local(): lax.psum_scatter(wide_one, 'gy', scatter_dimension=1, tiled=True)]
    psum x1 -> x0, waiting for transfers between devices: 110 us -> none  [local(): grad_three = lax.psum(term_three, ('gx', 'gy'))]
    psum x2 -> x0, blocking collectives: 75.6 us -> none  [the longest x1 63.8 us: local(): grad_one = lax.psum(term_one, ('gy', 'gz'))]
    all_to_all x0 -> x5, waiting for transfers between devices: none -> 36.5 us  [the longest x1 16.9 us: local(): late = lax.all_to_all(late, ('gz', 'gy'), 0, 0, tiled=True)]
    all_to_all x0 -> x5, starting transfers between devices: none -> 23 us  [the longest x1 6.36 us: local(): early = lax.all_to_all(early, 'gy', 0, 0, tiled=True)]
    dot_general x9 -> x10, matrix products: 38.3 us -> 18 us  [dot(): return jnp.einsum(spec, left, right, precision=highest)]
    ppermute x0 -> x14, waiting for transfers between devices: none -> 13.6 us  [swap(): return lax.ppermute(x, axis, [(0, 1), (1, 0)])]
  transfers between devices with their start and end apart: 8 -> 19, of which waited for: 8 -> 14; matrix products, arithmetic and copies ran while one was open for 4% -> 26% of each run, Pallas kernels for 0% -> 0%
where the time goes in v1:
time: 125 us; the launch traced here: 124 us
  waiting for transfers between devices  50.1 us (40%)
  starting transfers between devices  33 us (26%)
  matrix products  18 us (14%)
  local copies, waits for them, and re-layouts  12.3 us (10%)
  other arithmetic  9.33 us (7%)
    dot_general x10, matrix products, dot(): return jnp.einsum(spec, left, right, precision=highest)  18 us
    all_to_all x1, waiting for transfers between devices, local(): late = lax.all_to_all(late, ('gz', 'gy'), 0, 0, tiled=True)  16.9 us
    ppermute x14, waiting for transfers between devices, swap(): return lax.ppermute(x, axis, [(0, 1), (1, 0)])  13.6 us
    ppermute x14, starting transfers between devices, swap(): return lax.ppermute(x, axis, [(0, 1), (1, 0)])  10 us
    all_to_all x1, waiting for transfers between devices, local(): after_one = lax.all_to_all(after_one, ('gz', 'gy'), 0, 0, tiled=True)  8.47 us
    all_to_all x1, starting transfers between devices, local(): early = lax.all_to_all(early, 'gy', 0, 0, tiled=True)  6.36 us
    all_to_all x1, waiting for transfers between devices, local(): lax.all_to_all(moved, 'gy', 0, 0, tiled=True).reshape(ny * e, j, full_t)  5.41 us
    all_to_all x1, starting transfers between devices, local(): after_one = lax.all_to_all(after_one, ('gz', 'gy'), 0, 0, tiled=True)  4.5 us
  transfers between devices with their start and end apart: 19, of which 14 were waited for; matrix products, arithmetic and copies ran while one was open for 26% of the time, Pallas kernels for 0%

profile of v1, /device:TPU:0, one launch (start us, length us, event | category | flops | bytes accessed | tf_op | source)
XLA Modules:
  0.0 123.8 jit_solution(10091388087060622924)
XLA Ops:
  1.5 2.2 %fusion.23 = f32[32,32,128]{2,1,0:T(8,128)S(1)} fusion(f32[32,32,256]{2,1,0:T(8,128)} %param.5, f32[256,128]{1,0:T(8,128)S(1)} %copy-done), kind=kOutput, calls=%fused_computation.45 | convolution fusion | flops 402653184 | bytes 1703936 | tf_op jit(solution)/shard_map/abc,ct->abt/dot_general | solution.py:10
  6.9 2.9 %collective-permute-start = (f32[32,128]{1,0:T(8,128)}, f32[32,128]{1,0:T(8,128)}, u32[]{:S(2)}, u32[]{:S(2)}) collective-permute-start(f32[32,128]{1,0:T(8,128)} %bitcast.1), channel_id=1, source_target_pairs={{0,16},{16,0},{1,17},{17,1},{2,18},{18,2},{3,19},{19,3},{4,20},{20... | collective-permute-start | bytes 49160 | tf_op jit(solution)/shard_map/ppermute | solution.py:14
  13.5 6.4 %all-to-all-start.1 = ((f32[8,96,128]{2,1,0:T(8,128)}), f32[8,96,128]{2,1,0:T(8,128)S(1)}, u32[]{:S(2)}, u32[]{:S(2)}) async-start(f32[8,96,128]{2,1,0:T(8,128)} %pad_maximum_fusion.3), calls=%async_computation.1 | async-start | bytes 786432 | tf_op jit(solution)/shard_map/all_to_all | solution.py:71
  20.0 1.2 %fusion.27 = f32[2,32,16,128]{3,1,2,0:T(8,128)S(1)} fusion(f32[128,16,128,1]{0,2,1,3:T(8,128)S(1)} %bitcast.187, f32[1,32,128]{2,1,0:T(8,128)S(1)} %get-tuple-element.39, f32[1,32,128]{2,1,0:T(8,128)S(1)} %get-tuple-element.38), kind=kOutput, calls=%fused_computation.53 | convolution fusion | flops 201334784 | bytes 1605632 | tf_op jit(solution)/shard_map/ar,rst->ast/dot_general | solution.py:10
  21.5 1.6 %collective-permute-start.2 = (f32[32,16,128]{2,1,0:T(8,128)S(1)}, f32[32,16,128]{2,1,0:T(8,128)S(1)}, u32[]{:S(2)}, u32[]{:S(2)}) collective-permute-start(f32[32,16,128]{2,1,0:T(8,128)S(1)} %bitcast.213), channel_id=1, source_target_pairs={{0,16},{16,0},{1,17},{17,1},{2,18},{18,2},{3,19},{19,3},{4,20},{20... | collective-permute-start | bytes 786440 | tf_op jit(solution)/shard_map/ppermute | solution.py:14
  23.1 5.3 %collective-permute-done.2 = f32[32,16,128]{2,1,0:T(8,128)S(1)} collective-permute-done((f32[32,16,128]{2,1,0:T(8,128)S(1)}, f32[32,16,128]{2,1,0:T(8,128)S(1)}, u32[]{:S(2)}, u32[]{:S(2)}) %collective-permute-start.2) | collective-permute-done | bytes 262176 | tf_op jit(solution)/shard_map/ppermute | solution.py:14
  29.2 1.3 %all-to-all-done.1 = f32[8,96,128]{2,1,0:T(8,128)S(1)} async-done(((f32[8,96,128]{2,1,0:T(8,128)}), f32[8,96,128]{2,1,0:T(8,128)S(1)}, u32[]{:S(2)}, u32[]{:S(2)}) %all-to-all-start.1) | async-done | bytes 393248 | tf_op jit(solution)/shard_map/all_to_all | solution.py:71
  30.6 4.5 %all-to-all-start = ((f32[16,2,16,128]{3,2,1,0:T(8,128)}), f32[16,2,16,128]{3,2,1,0:T(8,128)S(1)}, u32[]{:S(2)}, u32[]{:S(2)}) async-start(f32[16,2,16,128]{3,2,1,0:T(8,128)} %bitcast.17), calls=%async_computation | async-start | bytes 524288 | tf_op jit(solution)/shard_map/all_to_all | solution.py:79
  37.0 8.5 %all-to-all-done = f32[16,2,16,128]{3,2,1,0:T(8,128)S(1)} async-done(((f32[16,2,16,128]{3,2,1,0:T(8,128)}), f32[16,2,16,128]{3,2,1,0:T(8,128)S(1)}, u32[]{:S(2)}, u32[]{:S(2)}) %all-to-all-start) | async-done | bytes 262176 | tf_op jit(solution)/shard_map/all_to_all | solution.py:79
  46.9 4.2 %all-to-all-start.2 = ((f32[8,2,32,128]{3,2,1,0:T(8,128)}), f32[8,2,32,128]{3,2,1,0:T(8,128)}, u32[]{:S(2)}, u32[]{:S(2)}) async-start(f32[8,2,32,128]{3,2,1,0:T(8,128)} %copy.116), calls=%async_computation.2 | async-start | bytes 524288 | tf_op jit(solution)/shard_map/all_to_all | solution.py:84
  52.0 1.6 %collective-permute-start.7 = (f32[128,16,128]{2,0,1:T(8,128)S(1)}, f32[128,16,128]{2,0,1:T(8,128)}, u32[]{:S(2)}, u32[]{:S(2)}) collective-permute-start(f32[128,16,128]{2,0,1:T(8,128)S(1)} %copy.128), channel_id=1, source_target_pairs={{0,16},{16,0},{1,17},{17,1},{2,18},{18,2},{3,19},{19,3},{4,20},{20... | collective-permute-start | bytes 3145736 | tf_op jit(solution)/shard_map/ppermute | solution.py:14
  54.2 5.4 %all-to-all-done.2 = f32[8,2,32,128]{3,2,1,0:T(8,128)} async-done(((f32[8,2,32,128]{3,2,1,0:T(8,128)}), f32[8,2,32,128]{3,2,1,0:T(8,128)}, u32[]{:S(2)}, u32[]{:S(2)}) %all-to-all-start.2) | async-done | bytes 262176 | tf_op jit(solution)/shard_map/all_to_all | solution.py:84
  62.4 2.2 %convolution_subtract_fusion = f32[32,32,256]{2,1,0:T(8,128)S(1)} fusion(f32[32,32,256]{2,1,0:T(8,128)} %param.5, f32[32,32,128]{2,1,0:T(8,128)S(1)} %bitcast.189, f32[256,128]{1,0:T(8,128)S(1)} %copy-done), kind=kOutput, calls=%fused_computation.6 | convolution fusion | flops 402915328 | bytes 2752512 | tf_op jit(solution)/shard_map/abt,ct->abc/dot_general | solution.py:10
  64.6 4.4 %copy.124 = f32[256,32,32]{2,1,0:T(8,128)} copy(f32[256,32,32]{0,2,1:T(8,128)S(1)} %bitcast.191) | data formatting | bytes 2097152 | tf_op jit(solution)/shard_map/abc,abt->ct/dot_general | solution.py:10
  69.0 7.8 %fusion.6 = f32[2,8,16,128]{3,2,0,1:T(8,128)S(1)} fusion(f32[32,32,128,1,1]{2,1,0,4,3:T(8,128)S(1)} %bitcast.190, f32[8,2,16,32,32]{4,3,2,1,0:T(8,128)} %bitcast.186), kind=kOutput, calls=%fused_computation.10 | convolution fusion | flops 402653184 | bytes 1703936 | tf_op jit(solution)/shard_map/abc,abt->ct/dot_general | solution.py:10
  77.8 4.5 %all-to-all-start.3 = ((f32[16,80,128]{2,1,0:T(8,128)}), f32[16,80,128]{2,1,0:T(8,128)}, u32[]{:S(2)}, u32[]{:S(2)}) async-start(f32[16,80,128]{2,1,0:T(8,128)} %pad_maximum_fusion.1), calls=%async_computation.3 | async-start | bytes 1310720 | tf_op jit(solution)/shard_map/all_to_all | solution.py:102
  82.3 1.4 %select_bitcast_fusion.1 = (f32[1,128,16,128]{3,1,2,0:T(8,128)S(1)}, f32[1,128,16,128]{3,1,2,0:T(8,128)S(1)}) fusion(f32[128,16,128]{2,0,1:T(8,128)S(1)} %copy.128, f32[128,16,128]{2,0,1:T(8,128)} %collective-permute-done.7, pred[]{:T(512)S(6)} %eq.5), kind=kLoop, calls=%fused_computation.14 | loop fusion | flops 524288 | bytes 4194305 | tf_op jit(solution)/shard_map/stack | solution.py:23
  83.7 16.9 %all-to-all-done.3 = f32[16,80,128]{2,1,0:T(8,128)} async-done(((f32[16,80,128]{2,1,0:T(8,128)}), f32[16,80,128]{2,1,0:T(8,128)}, u32[]{:S(2)}, u32[]{:S(2)}) %all-to-all-start.3) | async-done | bytes 655392 | tf_op jit(solution)/shard_map/all_to_all | solution.py:102
  101.5 1.6 %collective-permute-start.9 = (f32[2,16,128]{2,1,0:T(8,128)S(1)}, f32[2,16,128]{2,1,0:T(8,128)S(1)}, u32[]{:S(2)}, u32[]{:S(2)}) collective-permute-start(f32[2,16,128]{2,1,0:T(8,128)S(1)} %bitcast_reduce_fusion), channel_id=1, source_target_pairs={{0,16},{16,0},{1,17},{17,1},{2,18},{18,2},{3,19},{19,3},{4,20},{20... | collective-permute-start | bytes 49160 | tf_op jit(solution)/shard_map/ppermute | solution.py:14
  104.1 1.9 %fusion.9 = f32[32,2,128]{2,0,1:T(8,128)S(1)} fusion(f32[1,128,16,128]{3,1,2,0:T(8,128)S(1)} %get-tuple-element.21, f32[1,128,16,128]{3,1,2,0:T(8,128)S(1)} %get-tuple-element.20, f32[32,16,128]{2,1,0:T(8,128)S(1)} %bitcast.198), kind=kOutput, calls=%fused_computation.11 | convolution fusion | flops 201850880 | bytes 2392064 | tf_op jit(solution)/shard_map/ast,xrst->axr/dot_general | solution.py:10
  108.3 3.4 %all-to-all-start.4 = ((f32[8,64,128]{2,1,0:T(8,128)}), f32[8,64,128]{2,1,0:T(8,128)S(1)}, u32[]{:S(2)}, u32[]{:S(2)}) async-start(f32[8,64,128]{2,1,0:T(8,128)} %broadcast_in_dim.15), calls=%async_computation.4 | async-start | bytes 524288 | tf_op jit(solution)/shard_map/all_to_all | solution.py:117
  112.3 3.2 %collective-permute-done.12 = f32[32,128]{1,0:T(8,128)S(1)} collective-permute-done((f32[32,128]{1,0:T(8,128)S(1)}, f32[32,128]{1,0:T(8,128)S(1)}, u32[]{:S(2)}, u32[]{:S(2)}) %collective-permute-start.12) | collective-permute-done | bytes 16416 | tf_op jit(solution)/shard_map/ppermute | solution.py:14
  115.5 1.2 collective-permute-done.13
  116.9 4.4 %all-to-all-done.4 = f32[8,64,128]{2,1,0:T(8,128)S(1)} async-done(((f32[8,64,128]{2,1,0:T(8,128)}), f32[8,64,128]{2,1,0:T(8,128)S(1)}, u32[]{:S(2)}, u32[]{:S(2)}) %all-to-all-start.4) | async-done | bytes 262176 | tf_op jit(solution)/shard_map/all_to_all | solution.py:117
  (86 shorter events, 24.8 us)
Async XLA Ops:
  0.6 0.9 copy-start
  0.6 19.2 %copy-start.2 = (f32[128,32,64]{0,2,1:T(8,128)S(1)}, f32[128,32,64]{0,2,1:T(8,128)}, u32[]{:S(2)}) copy-start(f32[128,32,64]{0,2,1:T(8,128)} %param.6) | copy-start | bytes 3145732
  3.8 8.9 %collective-permute-start.3 = (f32[8,64,128]{2,1,0:T(8,128)S(1)}, f32[8,64,128]{2,1,0:T(8,128)S(1)}, u32[]{:S(2)}, u32[]{:S(2)}) collective-permute-start(f32[8,64,128]{2,1,0:T(8,128)S(1)} %dynamic-slice_bitcast_fusion.1), channel_id=1, source_target_pairs={{0,1},{1,0},{2,3},{3,2},{4,5},{5,4},{6,7},{7,6},{8,9},{9,8},{10,11... | collective-permute-start | bytes 786440 | tf_op jit(solution)/shard_map/ppermute | solution.py:14
  5.4 14.5 %collective-permute-start.1 = (f32[128,16,64]{0,2,1:T(8,128)S(1)}, f32[128,16,64]{0,2,1:T(8,128)S(1)}, u32[]{:S(2)}, u32[]{:S(2)}) collective-permute-start(f32[128,16,64]{0,2,1:T(8,128)S(1)} %dynamic-slice_bitcast_fusion), channel_id=1, source_target_pairs={{0,1},{1,0},{2,3},{3,2},{4,5},{5,4},{6,7},{7,6},{8,9},{9,8},{10,11... | collective-permute-start | bytes 1572872 | tf_op jit(solution)/shard_map/ppermute | solution.py:14
  6.9 5.0 %collective-permute-start = (f32[32,128]{1,0:T(8,128)}, f32[32,128]{1,0:T(8,128)}, u32[]{:S(2)}, u32[]{:S(2)}) collective-permute-start(f32[32,128]{1,0:T(8,128)} %bitcast.1), channel_id=1, source_target_pairs={{0,16},{16,0},{1,17},{17,1},{2,18},{18,2},{3,19},{19,3},{4,20},{20... | collective-permute-start | bytes 49160 | tf_op jit(solution)/shard_map/ppermute | solution.py:14
  13.5 17.1 %all-to-all-start.1 = ((f32[8,96,128]{2,1,0:T(8,128)}), f32[8,96,128]{2,1,0:T(8,128)S(1)}, u32[]{:S(2)}, u32[]{:S(2)}) async-start(f32[8,96,128]{2,1,0:T(8,128)} %pad_maximum_fusion.3), calls=%async_computation.1 | async-start | bytes 786432 | tf_op jit(solution)/shard_map/all_to_all | solution.py:71
  21.5 6.9 %collective-permute-start.2 = (f32[32,16,128]{2,1,0:T(8,128)S(1)}, f32[32,16,128]{2,1,0:T(8,128)S(1)}, u32[]{:S(2)}, u32[]{:S(2)}) collective-permute-start(f32[32,16,128]{2,1,0:T(8,128)S(1)} %bitcast.213), channel_id=1, source_target_pairs={{0,16},{16,0},{1,17},{17,1},{2,18},{18,2},{3,19},{19,3},{4,20},{20... | collective-permute-start | bytes 786440 | tf_op jit(solution)/shard_map/ppermute | solution.py:14
  30.6 14.9 %all-to-all-start = ((f32[16,2,16,128]{3,2,1,0:T(8,128)}), f32[16,2,16,128]{3,2,1,0:T(8,128)S(1)}, u32[]{:S(2)}, u32[]{:S(2)}) async-start(f32[16,2,16,128]{3,2,1,0:T(8,128)} %bitcast.17), calls=%async_computation | async-start | bytes 524288 | tf_op jit(solution)/shard_map/all_to_all | solution.py:79
  35.1 1.5 %collective-permute-start.4 = (f32[8,2,16,128]{3,2,1,0:T(8,128)S(1)}, f32[8,2,16,128]{3,2,1,0:T(8,128)S(1)}, u32[]{:S(2)}, u32[]{:S(2)}) collective-permute-start(f32[8,2,16,128]{3,2,1,0:T(8,128)S(1)} %bitcast.208), channel_id=1, source_target_pairs={{0,1},{1,0},{2,3},{3,2},{4,5},{5,4},{6,7},{7,6},{8,9},{9,8},{10,11... | collective-permute-start | bytes 393224 | tf_op jit(solution)/shard_map/ppermute | solution.py:14
  46.9 12.7 %all-to-all-start.2 = ((f32[8,2,32,128]{3,2,1,0:T(8,128)}), f32[8,2,32,128]{3,2,1,0:T(8,128)}, u32[]{:S(2)}, u32[]{:S(2)}) async-start(f32[8,2,32,128]{3,2,1,0:T(8,128)} %copy.116), calls=%async_computation.2 | async-start | bytes 524288 | tf_op jit(solution)/shard_map/all_to_all | solution.py:84
  51.5 2.0 %collective-permute-start.6 = (f32[128,128]{1,0:T(8,128)S(1)}, f32[128,128]{1,0:T(8,128)S(1)}, u32[]{:S(2)}, u32[]{:S(2)}) collective-permute-start(f32[128,128]{1,0:T(8,128)S(1)} %fusion.35), channel_id=1, source_target_pairs={{0,1},{1,0},{2,3},{3,2},{4,5},{5,4},{6,7},{7,6},{8,9},{9,8},{10,11... | collective-permute-start | bytes 196616 | tf_op jit(solution)/shard_map/ppermute | solution.py:14
  52.0 30.3 %collective-permute-start.7 = (f32[128,16,128]{2,0,1:T(8,128)S(1)}, f32[128,16,128]{2,0,1:T(8,128)}, u32[]{:S(2)}, u32[]{:S(2)}) collective-permute-start(f32[128,16,128]{2,0,1:T(8,128)S(1)} %copy.128), channel_id=1, source_target_pairs={{0,16},{16,0},{1,17},{17,1},{2,18},{18,2},{3,19},{19,3},{4,20},{20... | collective-permute-start | bytes 3145736 | tf_op jit(solution)/shard_map/ppermute | solution.py:14
  59.6 1.7 %collective-permute-start.5 = (f32[16,32,128]{2,1,0:T(8,128)}, f32[16,32,128]{2,1,0:T(8,128)S(1)}, u32[]{:S(2)}, u32[]{:S(2)}) collective-permute-start(f32[16,32,128]{2,1,0:T(8,128)} %bitcast.33), channel_id=1, source_target_pairs={{0,1},{1,0},{2,3},{3,2},{4,5},{5,4},{6,7},{7,6},{8,9},{9,8},{10,11... | collective-permute-start | bytes 786440 | tf_op jit(solution)/shard_map/ppermute | solution.py:14
  64.6 12.2 %copy-start.1 = (f32[32,32,256]{2,1,0:T(8,128)}, f32[32,32,256]{2,1,0:T(8,128)S(1)}, u32[]{:S(2)}) copy-start(f32[32,32,256]{2,1,0:T(8,128)S(1)} %convolution_subtract_fusion) | copy-start | bytes 3145732
  77.8 22.8 %all-to-all-start.3 = ((f32[16,80,128]{2,1,0:T(8,128)}), f32[16,80,128]{2,1,0:T(8,128)}, u32[]{:S(2)}, u32[]{:S(2)}) async-start(f32[16,80,128]{2,1,0:T(8,128)} %pad_maximum_fusion.1), calls=%async_computation.3 | async-start | bytes 1310720 | tf_op jit(solution)/shard_map/all_to_all | solution.py:102
  101.5 4.7 %collective-permute-start.9 = (f32[2,16,128]{2,1,0:T(8,128)S(1)}, f32[2,16,128]{2,1,0:T(8,128)S(1)}, u32[]{:S(2)}, u32[]{:S(2)}) collective-permute-start(f32[2,16,128]{2,1,0:T(8,128)S(1)} %bitcast_reduce_fusion), channel_id=1, source_target_pairs={{0,16},{16,0},{1,17},{17,1},{2,18},{18,2},{3,19},{19,3},{4,20},{20... | collective-permute-start | bytes 49160 | tf_op jit(solution)/shard_map/ppermute | solution.py:14
  106.1 1.2 %collective-permute-start.8 = (f32[32,128]{1,0:T(8,128)S(1)}, f32[32,128]{1,0:T(8,128)S(1)}, u32[]{:S(2)}, u32[]{:S(2)}) collective-permute-start(f32[32,128]{1,0:T(8,128)S(1)} %dynamic-slice_bitcast_fusion.2), channel_id=1, source_target_pairs={{0,1},{1,0},{2,3},{3,2},{4,5},{5,4},{6,7},{7,6},{8,9},{9,8},{10,11... | collective-permute-start | bytes 49160 | tf_op jit(solution)/shard_map/ppermute | solution.py:14
  106.2 1.4 %collective-permute-start.10 = (f32[16,128]{1,0:T(8,128)S(1)}, f32[16,128]{1,0:T(8,128)S(1)}, u32[]{:S(2)}, u32[]{:S(2)}) collective-permute-start(f32[16,128]{1,0:T(8,128)S(1)} %dynamic-slice_bitcast_fusion.3), channel_id=1, source_target_pairs={{0,1},{1,0},{2,3},{3,2},{4,5},{5,4},{6,7},{7,6},{8,9},{9,8},{10,11... | collective-permute-start | bytes 24584 | tf_op jit(solution)/shard_map/ppermute | solution.py:14
  108.3 13.1 %all-to-all-start.4 = ((f32[8,64,128]{2,1,0:T(8,128)}), f32[8,64,128]{2,1,0:T(8,128)S(1)}, u32[]{:S(2)}, u32[]{:S(2)}) async-start(f32[8,64,128]{2,1,0:T(8,128)} %broadcast_in_dim.15), calls=%async_computation.4 | async-start | bytes 524288 | tf_op jit(solution)/shard_map/all_to_all | solution.py:117
  111.7 3.8 %collective-permute-start.12 = (f32[32,128]{1,0:T(8,128)S(1)}, f32[32,128]{1,0:T(8,128)S(1)}, u32[]{:S(2)}, u32[]{:S(2)}) collective-permute-start(f32[32,128]{1,0:T(8,128)S(1)} %get-tuple-element.24), channel_id=1, source_target_pairs={{0,16},{16,0},{1,17},{17,1},{2,18},{18,2},{3,19},{19,3},{4,20},{20... | collective-permute-start | bytes 49160 | tf_op jit(solution)/shard_map/ppermute | solution.py:14
  115.5 1.2 collective-permute-start.13
  122.0 1.2 collective-permute-start.11

commit v2 on v1

v2 whole, which is shorter than its diff:
```python
import jax
import jax.numpy as jnp
from jax import lax
from jax.experimental import pallas as pl
from jax.experimental.pallas import tpu as pltpu
from jax.sharding import PartitionSpec as P

highest = lax.Precision.HIGHEST


def dot(spec, left, right):
    return jnp.einsum(spec, left, right, precision=highest)


def swap(x, axis):
    return lax.ppermute(x, axis, [(0, 1), (1, 0)])


def part(x, index):
    return lax.dynamic_index_in_dim(x, index, 0, keepdims=False)


def in_order(axis, mine, other):
    first = lax.axis_index(axis) == 0
    return jnp.stack([jnp.where(first, mine, other), jnp.where(first, other, mine)])


def trade(x, axis):
    if lax.axis_size(axis) != 2:
        return lax.all_to_all(x, axis, 0, 0, tiled=True)
    me = lax.axis_index(axis)
    return in_order(axis, part(x, me), swap(part(x, 1 - me), axis))


def gather(x, axis):
    if lax.axis_size(axis) != 2:
        return lax.all_gather(x, axis)
    return in_order(axis, x, swap(x, axis))


def reduce_scatter(x, axis):
    if lax.axis_size(axis) != 2:
        return lax.psum_scatter(x, axis, scatter_dimension=0)
    me = lax.axis_index(axis)
    return part(x, me) + swap(part(x, 1 - me), axis)


def total(x, axis):
    if lax.axis_size(axis) != 2:
        return lax.psum(x, axis)
    return x + swap(x, axis)


def fit(place, tensor, moved, factor_three, nz):
    i, j, k = tensor.shape
    full_t = moved.shape[1]
    if nz != 2:
        after_full = gather(moved, "gz").reshape(i * j, full_t)
        mine, other = after_full, after_full
    else:
        mine, other = moved, swap(moved, "gz")
    steps = 4
    block = i * j // steps
    each = mine.shape[0] // block

    def body(place_ref, tensor_ref, mine_ref, other_ref, factor_ref, residual_ref, sum_ref):
        step = pl.program_id(0)
        mine_here = step // each == place_ref[0]
        after = jnp.where(mine_here, mine_ref[...], other_ref[...])
        left = (
            lax.dot_general(after, factor_ref[...], (((1,), (1,)), ((), ())), precision=highest, preferred_element_type=jnp.float32)
            - tensor_ref[...]
        )
        residual_ref[...] = left
        term = lax.dot_general(left, after, (((0,), (0,)), ((), ())), precision=highest, preferred_element_type=jnp.float32)

        @pl.when(step == 0)
        def _():
            sum_ref[...] = term

        @pl.when(step > 0)
        def _():
            sum_ref[...] += term

    residual, term = pl.pallas_call(
        body,
        grid_spec=pltpu.PrefetchScalarGridSpec(
            num_scalar_prefetch=1,
            grid=(steps,),
            in_specs=[
                pl.BlockSpec((block, k), lambda n, place: (n, 0)),
                pl.BlockSpec((block, full_t), lambda n, place: (n % each, 0)),
                pl.BlockSpec((block, full_t), lambda n, place: (n % each, 0)),
                pl.BlockSpec((k, full_t), lambda n, place: (0, 0)),
            ],
            out_specs=[
                pl.BlockSpec((block, k), lambda n, place: (n, 0)),
                pl.BlockSpec((k, full_t), lambda n, place: (0, 0)),
            ],
        ),
        out_shape=[jax.ShapeDtypeStruct((i * j, k), jnp.float32), jax.ShapeDtypeStruct((k, full_t), jnp.float32)],
        compiler_params=pltpu.CompilerParams(vmem_limit_bytes=32 * 1024 * 1024),
        cost_estimate=pl.CostEstimate(flops=24 * i * j * k * full_t, bytes_accessed=8 * i * j * k, transcendentals=0),
    )(place, tensor.reshape(i * j, k), mine, other, factor_three)
    return residual.reshape(i, j, k), term


def local(tensor, core, factor_one, factor_two, factor_three):
    nx, ny, nz = lax.axis_size("gx"), lax.axis_size("gy"), lax.axis_size("gz")
    i, j, k = tensor.shape
    r, s, t = core.shape
    e, q, full_t, full_s, full_r = i // (ny * nz), s // nz, t * nz, s * ny, r * nx
    half_j, half_s = j // nz, full_s // nz

    own = trade(core.reshape(r, nz, q, t).transpose(1, 0, 2, 3), "gz")
    own = own.transpose(1, 2, 0, 3).reshape(r, q, full_t)
    rows = trade(factor_one.reshape(i, nx, r).transpose(1, 0, 2), "gx").reshape(nx * i, r)

    rows_last = lax.axis_index("gz").reshape(1).astype(jnp.int32)

    folded_tensor = dot("abc,ct->abt", tensor, factor_three).reshape(i, nz, half_j, full_t)
    folded_tensor = reduce_scatter(folded_tensor.transpose(1, 0, 2, 3), "gz").reshape(nz * ny, e * half_j, full_t)
    gram = total(dot("ct,cu->tu", factor_three, factor_three), "gz")

    after_one = dot("ar,rst->ast", rows, own).reshape(nx, i, q, full_t)
    after_one = reduce_scatter(after_one, "gx").reshape(nz * ny, e * q, full_t)

    mine_two = part(factor_two.reshape(nz, half_j, full_s), lax.axis_index("gz"))
    mine_two = mine_two.reshape(half_j, ny, nz, q).transpose(2, 0, 1, 3).reshape(1, -1, full_t)
    mine_two = jnp.broadcast_to(mine_two, (nz * ny,) + mine_two.shape[1:])
    early = jnp.concatenate([after_one, folded_tensor, mine_two], axis=1)
    early = lax.all_to_all(early, ("gz", "gy"), 0, 0, tiled=True)
    cut, cut_two = e * q, e * q + e * half_j
    after_one = early[:, :cut].reshape(nz * ny, e, q, full_t).transpose(1, 0, 2, 3).reshape(e, full_s, full_t)
    folded_tensor = early[:, cut:cut_two].reshape(nz, ny, e, half_j, full_t).transpose(2, 1, 0, 3, 4).reshape(e, ny * j, full_t)
    all_two = early[:, cut_two:].reshape(nz, ny, nz, half_j, half_s).transpose(1, 0, 3, 2, 4).reshape(ny * j, full_s)

    after_two = dot("bs,ast->abt", all_two, after_one)
    moved = after_two.reshape(e, ny, j, full_t).transpose(1, 0, 2, 3)
    moved = lax.all_to_all(moved, "gy", 0, 0, tiled=True).reshape(ny * e * j, full_t)

    folded = dot("abt,tu->abu", after_two, gram) - folded_tensor
    wide_one = dot("abt,bs->ast", folded, all_two)
    term_two = dot("abt,ast->bs", folded, after_one).reshape(ny * j, nz, half_s)
    term_two = reduce_scatter(term_two.transpose(1, 0, 2), "gz")

    residual, term_three = fit(rows_last, tensor, moved, factor_three, nz)

    late = jnp.concatenate(
        [
            wide_one.reshape(e, nz * ny, q, full_t).transpose(1, 0, 2, 3).reshape(nz * ny, e * q, full_t),
            term_two.reshape(ny, nz, -1, full_t).transpose(1, 0, 2, 3).reshape(nz * ny, -1, full_t),
            term_three.reshape(ny, nz, -1, full_t).transpose(1, 0, 2, 3).reshape(nz * ny, -1, full_t),
        ],
        axis=1,
    )
    late = lax.all_to_all(late, ("gz", "gy"), 0, 0, tiled=True)
    cut = e * q
    share_one = late[:, :cut].reshape(i, q, full_t)
    sums = total(late[:, cut:].reshape(nz, ny, -1, full_t).sum(axis=1), "gx")
    cut = half_j * half_s // full_t
    share_two, share_three = sums[:, :cut], sums[:, cut:]
    every_core = gather(own, "gx")
    term_one = dot("ast,xrst->axr", share_one, every_core).reshape(i, nz, full_r // nz).transpose(1, 0, 2)
    term_one = reduce_scatter(term_one, "gz")

    share_two = share_two.reshape(nz, half_j, ny, q).transpose(1, 2, 0, 3).reshape(half_j, full_s)
    grad_two = gather(share_two, "gz").reshape(j, full_s)

    last = jnp.concatenate([term_one.reshape(nz, -1, full_t), share_three], axis=1)
    last = jnp.broadcast_to(last[:, None], (nz, ny) + last.shape[1:])
    last = lax.all_to_all(last.reshape((nz * ny,) + last.shape[2:]), ("gz", "gy"), 0, 0, tiled=True)
    last = last.reshape((nz, ny) + last.shape[1:])
    cut = (i // nz) * (full_r // nz) // full_t
    grad_one = last[:, :, :cut].sum(axis=1).reshape(nz, i // nz, full_r // nz)
    grad_one = gather(grad_one.transpose(1, 0, 2).reshape(i // nz, full_r), "gz").reshape(i, full_r)
    grad_three = last[:, :, cut:].transpose(1, 0, 2, 3).reshape(k, full_t)

    grad_one = grad_one / jnp.sqrt(jnp.float32(j * ny * k * nz))
    grad_two = grad_two / jnp.sqrt(jnp.float32(i * nx * k * nz))
    grad_three = grad_three / jnp.sqrt(jnp.float32(i * nx * j * ny))
    return (residual, grad_one, grad_two, grad_three)


def solution(mesh):
    placed = (P("gx", "gy", "gz"), P("gx", "gy", "gz"), P("gx", None), P("gy", None), P("gz", None))
    return jax.shard_map(
        local,
        mesh=mesh,
        in_specs=placed,
        out_specs=(P("gx", "gy", "gz"), P("gx", None), P("gy", None), P("gz", None)),
        check_vma=False,
    )
```

time: 125 us -> 120 us (0.960)
  starting transfers between devices: 33 us -> 23.2 us
  waiting for transfers between devices: 50.1 us -> 59.5 us
  matrix products: 18 us -> 8.63 us
  Pallas kernels: 0 us -> 5.24 us
    all_to_all x4 -> x3, waiting for transfers between devices: 19.6 us -> 34 us  [the longest x1 19.5 us: local(): early = lax.all_to_all(early, ('gz', 'gy'), 0, 0, tiled=True)]
    dot_general x10 -> x8, matrix products: 18 us -> 8.63 us  [dot(): return jnp.einsum(spec, left, right, precision=highest)]
    all_to_all x4 -> x3, starting transfers between devices: 18.5 us -> 12.9 us  [the longest x1 5.98 us: local(): early = lax.all_to_all(early, ('gz', 'gy'), 0, 0, tiled=True)]
    pallas_call x0 -> x1, Pallas kernels: none -> 5.24 us  [fit(): pl.pallas_call(body, grid_spec=pltpu.PrefetchScalarGridSpec(num_scalar_pr...]
    dot_general x1 -> x0, local copies, waits for them, and re-layouts: 4.38 us -> none  [dot(): return jnp.einsum(spec, left, right, precision=highest)]
    ppermute x14 -> x12, starting transfers between devices: 10 us -> 6.06 us  [swap(): return lax.ppermute(x, axis, [(0, 1), (1, 0)])]
    slice x2 -> x3, local copies, waits for them, and re-layouts: 0.03 us -> 2.84 us  [the longest x1 1.86 us: local(): early[:, cut:cut_two].reshape(nz, ny, e, half_j, full_t)]
    ppermute x14 -> x12, waiting for transfers between devices: 13.6 us -> 11.1 us  [swap(): return lax.ppermute(x, axis, [(0, 1), (1, 0)])]
  transfers between devices with their start and end apart: 19 -> 16, of which waited for: 14 -> 7; matrix products, arithmetic and copies ran while one was open for 26% -> 19% of each run, Pallas kernels for 0% -> 4%
where the time goes in v2:
time: 120 us; the launch traced here: 119 us
  waiting for transfers between devices  59.5 us (50%)
  starting transfers between devices  23.2 us (19%)
  local copies, waits for them, and re-layouts  12.6 us (10%)
  other arithmetic  8.74 us (7%)
  matrix products  8.63 us (7%)
  Pallas kernels  5.24 us (4%)
    all_to_all x1, waiting for transfers between devices, local(): early = lax.all_to_all(early, ('gz', 'gy'), 0, 0, tiled=True)  19.5 us
    all_to_all x1, waiting for transfers between devices, local(): late = lax.all_to_all(late, ('gz', 'gy'), 0, 0, tiled=True)  14.4 us
    ppermute x12, waiting for transfers between devices, swap(): return lax.ppermute(x, axis, [(0, 1), (1, 0)])  11.1 us
    all_to_all x1, waiting for transfers between devices, local(): lax.all_to_all(last.reshape((nz * ny,) + last.shape[2:]), ('gz', 'gy'), 0...  8.66 us
    dot_general x8, matrix products, dot(): return jnp.einsum(spec, left, right, precision=highest)  8.63 us
    ppermute x12, starting transfers between devices, swap(): return lax.ppermute(x, axis, [(0, 1), (1, 0)])  6.06 us
    all_to_all x1, starting transfers between devices, local(): early = lax.all_to_all(early, ('gz', 'gy'), 0, 0, tiled=True)  5.98 us
    all_to_all x1, waiting for transfers between devices, local(): lax.all_to_all(moved, 'gy', 0, 0, tiled=True).reshape(ny * e * j, full_t)  5.81 us
  transfers between devices with their start and end apart: 16, of which 7 were waited for; matrix products, arithmetic and copies ran while one was open for 19% of the time, Pallas kernels for 4%

profile of v2, /device:TPU:0, one launch (start us, length us, event | category | flops | bytes accessed | tf_op | source)
XLA Modules:
  0.0 118.9 jit_solution(16590211900755221444)
XLA Ops:
  1.6 3.0 %collective-permute-start = (f32[32,128]{1,0:T(8,128)S(1)}, f32[32,128]{1,0:T(8,128)S(1)}, u32[]{:S(2)}, u32[]{:S(2)}) collective-permute-start(f32[32,128]{1,0:T(8,128)S(1)} %bitcast.208), channel_id=1, source_target_pairs={{0,16},{16,0},{1,17},{17,1},{2,18},{18,2},{3,19},{19,3},{4,20},{20... | collective-permute-start | bytes 49160 | tf_op jit(solution)/shard_map/ppermute | solution.py:16
  4.6 1.1 dynamic-slice_bitcast_fusion
  5.8 1.0 fusion.15
  8.0 1.1 fusion.7
  9.2 1.2 %fusion.19 = f32[2,32,16,128]{3,1,2,0:T(8,128)S(1)} fusion(f32[128,16,128,1]{0,2,1,3:T(8,128)S(1)} %bitcast.178, f32[1,32,128]{2,1,0:T(8,128)S(1)} %get-tuple-element.26, f32[1,32,128]{2,1,0:T(8,128)S(1)} %get-tuple-element.25), kind=kOutput, calls=%fused_computation.39 | convolution fusion | flops 201334784 | bytes 1605632 | tf_op jit(solution)/shard_map/ar,rst->ast/dot_general | solution.py:12
  12.1 1.0 bitcast_add_fusion
  13.1 6.9 %collective-permute-done.2 = f32[32,16,128]{2,1,0:T(8,128)} collective-permute-done((f32[32,16,128]{2,1,0:T(8,128)}, f32[32,16,128]{2,1,0:T(8,128)}, u32[]{:S(2)}, u32[]{:S(2)}) %collective-permute-start.2) | collective-permute-done | bytes 262176 | tf_op jit(solution)/shard_map/ppermute | solution.py:16
  20.0 1.1 bitcast_add_fusion.1
  22.0 6.0 %all-to-all-start = ((f32[16,96,128]{2,1,0:T(8,128)}), f32[16,96,128]{2,1,0:T(8,128)}, u32[]{:S(2)}, u32[]{:S(2)}) async-start(f32[16,96,128]{2,1,0:T(8,128)} %pad_maximum_fusion.1), calls=%async_computation | async-start | bytes 1572864 | tf_op jit(solution)/shard_map/all_to_all | solution.py:132
  29.8 19.5 %all-to-all-done = f32[16,96,128]{2,1,0:T(8,128)} async-done(((f32[16,96,128]{2,1,0:T(8,128)}), f32[16,96,128]{2,1,0:T(8,128)}, u32[]{:S(2)}, u32[]{:S(2)}) %all-to-all-start) | async-done | bytes 786464 | tf_op jit(solution)/shard_map/all_to_all | solution.py:132
  49.3 1.9 %fusion.24 = (f32[16,32,128]{2,1,0:T(8,128)}, f32[16,32,128]{2,1,0:T(8,128)S(1)}, f32[16,32,128]{2,1,0:T(8,128)S(1)}) fusion(f32[16,96,128]{2,1,0:T(8,128)} %all-to-all-done), kind=kLoop, calls=%fused_computation.61 | loop fusion | bytes 1572864 | tf_op jit(solution)/shard_map/slice | solution.py:135
  52.1 1.7 %copy.126 = f32[2,8,2,16,128]{4,3,2,1,0:T(8,128)} copy(f32[2,8,2,16,128]{4,3,0,1,2:T(8,128)} %bitcast.192) | data formatting | bytes 524288 | tf_op jit(solution)/shard_map/transpose | solution.py:135
  54.7 3.4 %all-to-all-start.1 = ((f32[8,2,32,128]{3,2,1,0:T(8,128)}), f32[8,2,32,128]{3,2,1,0:T(8,128)S(1)}, u32[]{:S(2)}, u32[]{:S(2)}) async-start(f32[8,2,32,128]{3,2,1,0:T(8,128)} %copy.124), calls=%async_computation.1 | async-start | bytes 524288 | tf_op jit(solution)/shard_map/all_to_all | solution.py:140
  58.1 1.5 %convolution_subtract_fusion = f32[2,256,128]{2,1,0:T(8,128)S(1)} fusion(f32[2,256,128]{2,1,0:T(8,128)} %bitcast.185, f32[2,256,128]{1,2,0:T(8,128)S(1)} %convolution_bitcast_fusion.1, f32[128,128]{1,0:T(8,128)S(1)} %fusion.26, f32[128,128]{1,0:T(8,128)S(1)} %collective-permute-done.5), kind=kOutput, calls=%fused_computation.5 | convolution fusion | flops 100745216 | bytes 917504 | tf_op jit(solution)/shard_map/abt,tu->abu/dot_general | solution.py:12
  60.8 5.8 %all-to-all-done.1 = f32[8,2,32,128]{3,2,1,0:T(8,128)S(1)} async-done(((f32[8,2,32,128]{3,2,1,0:T(8,128)}), f32[8,2,32,128]{3,2,1,0:T(8,128)S(1)}, u32[]{:S(2)}, u32[]{:S(2)}) %all-to-all-start.1) | async-done | bytes 262176 | tf_op jit(solution)/shard_map/all_to_all | solution.py:140
  66.6 1.5 %fusion.9 = f32[256,2,128]{2,0,1:T(8,128)S(1)} fusion(f32[2,256,128]{2,1,0:T(8,128)S(1)} %convolution_subtract_fusion, f32[32,8,2,128]{3,2,1,0:T(2,128)} %bitcast.182), kind=kOutput, calls=%fused_computation.19 | convolution fusion | flops 201326592 | bytes 786432 | tf_op jit(solution)/shard_map/abt,bs->ast/dot_general | solution.py:12
  68.2 5.2 %shard_map.84 = (f32[1024,256]{1,0:T(8,128)}, f32[256,128]{1,0:T(8,128)S(1)}) custom-call(s32[1]{0:T(128)} %bitcast.place_ref, f32[1024,256]{1,0:T(8,128)S(1)} %bitcast.174, f32[512,128]{1,0:T(8,128)S(1)} %bitcast.176, f32[512,128]{1,0:T(8,128)S(1)} %collective-permute-done.4.other_ref, f32[256,128]{1,0:T(8,128)S(1)} %copy-done.1), custom_call_target="tpu_custom_call" | custom-call | flops 805306368 | bytes 2097152 | tf_op jit(solution)/shard_map/pallas_call | solution.py:85
  74.3 4.2 %all-to-all-start.2 = ((f32[16,64,128]{2,1,0:T(8,128)}), f32[16,64,128]{2,1,0:T(8,128)}, u32[]{:S(2)}, u32[]{:S(2)}) async-start(f32[16,64,128]{2,1,0:T(8,128)} %pad_maximum_fusion.2), calls=%async_computation.2 | async-start | bytes 1048576 | tf_op jit(solution)/shard_map/all_to_all | solution.py:157
  78.6 1.4 %select_bitcast_fusion.1 = (f32[1,128,16,128]{3,1,2,0:T(8,128)S(1)}, f32[1,128,16,128]{3,1,2,0:T(8,128)S(1)}) fusion(f32[128,16,128]{2,0,1:T(8,128)S(1)} %copy.133, f32[128,16,128]{2,0,1:T(8,128)} %collective-permute-done.7, pred[]{:T(512)S(6)} %eq.4), kind=kLoop, calls=%fused_computation.10 | loop fusion | flops 524288 | bytes 4194305 | tf_op jit(solution)/shard_map/stack | solution.py:25
  80.0 14.4 %all-to-all-done.2 = f32[16,64,128]{2,1,0:T(8,128)} async-done(((f32[16,64,128]{2,1,0:T(8,128)}), f32[16,64,128]{2,1,0:T(8,128)}, u32[]{:S(2)}, u32[]{:S(2)}) %all-to-all-start.2) | async-done | bytes 524320 | tf_op jit(solution)/shard_map/all_to_all | solution.py:157
  95.3 1.9 %fusion.4 = f32[32,2,128]{2,0,1:T(8,128)S(1)} fusion(f32[1,128,16,128]{3,1,2,0:T(8,128)S(1)} %get-tuple-element.9, f32[1,128,16,128]{3,1,2,0:T(8,128)S(1)} %get-tuple-element.8, f32[32,16,128]{2,1,0:T(8,128)S(1)} %bitcast.186), kind=kOutput, calls=%fused_computation.7 | convolution fusion | flops 201850880 | bytes 2392064 | tf_op jit(solution)/shard_map/ast,xrst->axr/dot_general | solution.py:12
  98.9 3.4 %collective-permute-done.9 = f32[2,32,128]{2,1,0:T(8,128)S(1)} collective-permute-done((f32[2,32,128]{2,1,0:T(8,128)S(1)}, f32[2,32,128]{2,1,0:T(8,128)S(1)}, u32[]{:S(2)}, u32[]{:S(2)}) %collective-permute-start.9) | collective-permute-done | bytes 32800 | tf_op jit(solution)/shard_map/ppermute | solution.py:16
  103.1 3.5 %all-to-all-start.3 = ((f32[16,32,128]{2,1,0:T(8,128)}), f32[16,32,128]{2,1,0:T(8,128)S(1)}, u32[]{:S(2)}, u32[]{:S(2)}) async-start(f32[16,32,128]{2,1,0:T(8,128)} %bitcast.70), calls=%async_computation.3 | async-start | bytes 524288 | tf_op jit(solution)/shard_map/all_to_all | solution.py:172
  108.2 8.7 %all-to-all-done.3 = f32[16,32,128]{2,1,0:T(8,128)S(1)} async-done(((f32[16,32,128]{2,1,0:T(8,128)}), f32[16,32,128]{2,1,0:T(8,128)S(1)}, u32[]{:S(2)}, u32[]{:S(2)}) %all-to-all-start.3) | async-done | bytes 262176 | tf_op jit(solution)/shard_map/all_to_all | solution.py:172
  (77 shorter events, 17.4 us)
Async XLA Ops:
  0.6 11.1 %copy-start = (f32[32,256]{1,0:T(8,128)S(1)}, f32[32,256]{1,0:T(8,128)}, u32[]{:S(2)}) copy-start(f32[32,256]{1,0:T(8,128)} %param.8) | copy-start | bytes 98308
  0.6 5.1 %copy-start.1 = (f32[256,128]{1,0:T(8,128)S(1)}, f32[256,128]{1,0:T(8,128)}, u32[]{:S(2)}) copy-start(f32[256,128]{1,0:T(8,128)} %factor_ref.1) | copy-start | bytes 393220
  0.7 5.1 %copy-start.2 = (f32[32,32,256]{2,1,0:T(8,128)S(1)}, f32[32,32,256]{2,1,0:T(8,128)}, u32[]{:S(2)}) copy-start(f32[32,32,256]{2,1,0:T(8,128)} %param.5) | copy-start | bytes 3145732
  1.6 6.4 %collective-permute-start = (f32[32,128]{1,0:T(8,128)S(1)}, f32[32,128]{1,0:T(8,128)S(1)}, u32[]{:S(2)}, u32[]{:S(2)}) collective-permute-start(f32[32,128]{1,0:T(8,128)S(1)} %bitcast.208), channel_id=1, source_target_pairs={{0,16},{16,0},{1,17},{17,1},{2,18},{18,2},{3,19},{19,3},{4,20},{20... | collective-permute-start | bytes 49160 | tf_op jit(solution)/shard_map/ppermute | solution.py:16
  5.7 2.3 %copy-start.4 = (f32[128,32,64]{0,2,1:T(8,128)S(1)}, f32[128,32,64]{0,2,1:T(8,128)}, u32[]{:S(2)}) copy-start(f32[128,32,64]{0,2,1:T(8,128)} %param.6) | copy-start | bytes 3145732
  5.7 2.3 %collective-permute-start.1 = (f32[128,16,64]{0,2,1:T(8,128)S(1)}, f32[128,16,64]{0,2,1:T(8,128)}, u32[]{:S(2)}, u32[]{:S(2)}) collective-permute-start(f32[128,16,64]{0,2,1:T(8,128)S(1)} %dynamic-slice_bitcast_fusion), channel_id=1, source_target_pairs={{0,1},{1,0},{2,3},{3,2},{4,5},{5,4},{6,7},{7,6},{8,9},{9,8},{10,11... | collective-permute-start | bytes 1572872 | tf_op jit(solution)/shard_map/ppermute | solution.py:16
  7.5 4.6 %collective-permute-start.3 = (f32[32,16,128]{2,1,0:T(8,128)}, f32[32,16,128]{2,1,0:T(8,128)}, u32[]{:S(2)}, u32[]{:S(2)}) collective-permute-start(f32[32,16,128]{2,1,0:T(8,128)} %dynamic-slice_bitcast_fusion.1), channel_id=1, source_target_pairs={{0,1},{1,0},{2,3},{3,2},{4,5},{5,4},{6,7},{7,6},{8,9},{9,8},{10,11... | collective-permute-start | bytes 786440 | tf_op jit(solution)/shard_map/ppermute | solution.py:16
  11.4 8.6 %collective-permute-start.2 = (f32[32,16,128]{2,1,0:T(8,128)}, f32[32,16,128]{2,1,0:T(8,128)}, u32[]{:S(2)}, u32[]{:S(2)}) collective-permute-start(f32[32,16,128]{2,1,0:T(8,128)} %bitcast.172), channel_id=1, source_target_pairs={{0,16},{16,0},{1,17},{17,1},{2,18},{18,2},{3,19},{19,3},{4,20},{20... | collective-permute-start | bytes 786440 | tf_op jit(solution)/shard_map/ppermute | solution.py:16
  22.0 27.2 %all-to-all-start = ((f32[16,96,128]{2,1,0:T(8,128)}), f32[16,96,128]{2,1,0:T(8,128)}, u32[]{:S(2)}, u32[]{:S(2)}) async-start(f32[16,96,128]{2,1,0:T(8,128)} %pad_maximum_fusion.1), calls=%async_computation | async-start | bytes 1572864 | tf_op jit(solution)/shard_map/all_to_all | solution.py:132
  28.4 29.7 %collective-permute-start.5 = (f32[128,128]{1,0:T(8,128)S(1)}, f32[128,128]{1,0:T(8,128)S(1)}, u32[]{:S(2)}, u32[]{:S(2)}) collective-permute-start(f32[128,128]{1,0:T(8,128)S(1)} %fusion.26), channel_id=1, source_target_pairs={{0,1},{1,0},{2,3},{3,2},{4,5},{5,4},{6,7},{7,6},{8,9},{9,8},{10,11... | collective-permute-start | bytes 196616 | tf_op jit(solution)/shard_map/ppermute | solution.py:16
  29.2 49.4 %collective-permute-start.7 = (f32[128,16,128]{2,0,1:T(8,128)S(1)}, f32[128,16,128]{2,0,1:T(8,128)}, u32[]{:S(2)}, u32[]{:S(2)}) collective-permute-start(f32[128,16,128]{2,0,1:T(8,128)S(1)} %copy.133), channel_id=1, source_target_pairs={{0,16},{16,0},{1,17},{17,1},{2,18},{18,2},{3,19},{19,3},{4,20},{20... | collective-permute-start | bytes 3145736 | tf_op jit(solution)/shard_map/ppermute | solution.py:16
  51.3 2.6 %copy-start.3 = (f32[8,2,16,2,128]{4,3,2,1,0:T(2,128)}, f32[8,2,16,2,128]{4,3,2,1,0:T(2,128)S(1)}, u32[]{:S(2)}) copy-start(f32[8,2,16,2,128]{4,3,2,1,0:T(2,128)S(1)} %copy.121) | copy-start | bytes 786436
  54.7 11.9 %all-to-all-start.1 = ((f32[8,2,32,128]{3,2,1,0:T(8,128)}), f32[8,2,32,128]{3,2,1,0:T(8,128)S(1)}, u32[]{:S(2)}, u32[]{:S(2)}) async-start(f32[8,2,32,128]{3,2,1,0:T(8,128)} %copy.124), calls=%async_computation.1 | async-start | bytes 524288 | tf_op jit(solution)/shard_map/all_to_all | solution.py:140
  60.8 7.4 %collective-permute-start.6 = (f32[256,128]{1,0:T(8,128)}, f32[256,128]{1,0:T(8,128)S(1)}, u32[]{:S(2)}, u32[]{:S(2)}) collective-permute-start(f32[256,128]{1,0:T(8,128)} %dynamic-slice_bitcast_fusion.2), channel_id=1, source_target_pairs={{0,1},{1,0},{2,3},{3,2},{4,5},{5,4},{6,7},{7,6},{8,9},{9,8},{10,11... | collective-permute-start | bytes 393224 | tf_op jit(solution)/shard_map/ppermute | solution.py:16
  66.6 1.6 %collective-permute-start.4 = (f32[512,128]{1,0:T(8,128)S(1)}, f32[512,128]{1,0:T(8,128)S(1)}, u32[]{:S(2)}, u32[]{:S(2)}) collective-permute-start(f32[512,128]{1,0:T(8,128)S(1)} %bitcast.175), channel_id=1, source_target_pairs={{0,1},{1,0},{2,3},{3,2},{4,5},{5,4},{6,7},{7,6},{8,9},{9,8},{10,11... | collective-permute-start | bytes 786440 | tf_op jit(solution)/shard_map/ppermute | solution.py:16
  74.3 20.0 %all-to-all-start.2 = ((f32[16,64,128]{2,1,0:T(8,128)}), f32[16,64,128]{2,1,0:T(8,128)}, u32[]{:S(2)}, u32[]{:S(2)}) async-start(f32[16,64,128]{2,1,0:T(8,128)} %pad_maximum_fusion.2), calls=%async_computation.2 | async-start | bytes 1048576 | tf_op jit(solution)/shard_map/all_to_all | solution.py:157
  97.3 1.7 %collective-permute-start.8 = (f32[32,128]{1,0:T(8,128)S(1)}, f32[32,128]{1,0:T(8,128)S(1)}, u32[]{:S(2)}, u32[]{:S(2)}) collective-permute-start(f32[32,128]{1,0:T(8,128)S(1)} %dynamic-slice_bitcast_fusion.3), channel_id=1, source_target_pairs={{0,1},{1,0},{2,3},{3,2},{4,5},{5,4},{6,7},{7,6},{8,9},{9,8},{10,11... | collective-permute-start | bytes 49160 | tf_op jit(solution)/shard_map/ppermute | solution.py:16
  98.3 4.0 %collective-permute-start.9 = (f32[2,32,128]{2,1,0:T(8,128)S(1)}, f32[2,32,128]{2,1,0:T(8,128)S(1)}, u32[]{:S(2)}, u32[]{:S(2)}) collective-permute-start(f32[2,32,128]{2,1,0:T(8,128)S(1)} %bitcast_reduce_fusion), channel_id=1, source_target_pairs={{0,16},{16,0},{1,17},{17,1},{2,18},{18,2},{3,19},{19,3},{4,20},{20... | collective-permute-start | bytes 98312 | tf_op jit(solution)/shard_map/ppermute | solution.py:16
  103.1 13.8 %all-to-all-start.3 = ((f32[16,32,128]{2,1,0:T(8,128)}), f32[16,32,128]{2,1,0:T(8,128)S(1)}, u32[]{:S(2)}, u32[]{:S(2)}) async-start(f32[16,32,128]{2,1,0:T(8,128)} %bitcast.70), calls=%async_computation.3 | async-start | bytes 524288 | tf_op jit(solution)/shard_map/all_to_all | solution.py:172
  107.0 1.2 %collective-permute-start.11 = (f32[16,256]{1,0:T(8,128)S(1)}, f32[16,256]{1,0:T(8,128)S(1)}, u32[]{:S(2)}, u32[]{:S(2)}) collective-permute-start(f32[16,256]{1,0:T(8,128)S(1)} %reshape.178), channel_id=1, source_target_pairs={{0,1},{1,0},{2,3},{3,2},{4,5},{5,4},{6,7},{7,6},{8,9},{9,8},{10,11... | collective-permute-start | bytes 49160 | tf_op jit(solution)/shard_map/ppermute | solution.py:16
  116.9 1.4 %collective-permute-start.10 = (f32[16,256]{1,0:T(8,128)S(1)}, f32[16,256]{1,0:T(8,128)S(1)}, u32[]{:S(2)}, u32[]{:S(2)}) collective-permute-start(f32[16,256]{1,0:T(8,128)S(1)} %copy_bitcast_fusion.1), channel_id=1, source_target_pairs={{0,1},{1,0},{2,3},{3,2},{4,5},{5,4},{6,7},{7,6},{8,9},{9,8},{10,11... | collective-permute-start | bytes 49160 | tf_op jit(solution)/shard_map/ppermute | solution.py:16

commit v3 on v0

v3 whole, which is shorter than its diff:
```python
import jax
import jax.numpy as jnp
from jax import lax
from jax.experimental import pallas as pl
from jax.experimental.pallas import tpu as pltpu
from jax.sharding import PartitionSpec as P

highest = lax.Precision.HIGHEST
f32 = jnp.float32
vmem = pl.BlockSpec(memory_space=pltpu.VMEM)
hbm = pl.BlockSpec(memory_space=pl.ANY)
smem = pl.BlockSpec(memory_space=pltpu.SMEM)
params = pltpu.CompilerParams(vmem_limit_bytes=14 * 1024 * 1024)


def shape(*sizes):
    return jax.ShapeDtypeStruct(sizes, f32)


def dot(spec, left, right):
    return jnp.einsum(spec, left, right, precision=highest)


def product(left, right, dims):
    return lax.dot_general(left, right, (dims, ((), ())), precision=highest, preferred_element_type=f32)


def swap(x, axis):
    return lax.ppermute(x, axis, [(0, 1), (1, 0)])


def part(x, index):
    return lax.dynamic_index_in_dim(x, index, 0, keepdims=False)


def in_order(axis, mine, other):
    first = lax.axis_index(axis) == 0
    return jnp.stack([jnp.where(first, mine, other), jnp.where(first, other, mine)])


def trade(x, axis):
    if lax.axis_size(axis) != 2:
        return lax.all_to_all(x, axis, 0, 0, tiled=True)
    me = lax.axis_index(axis)
    return in_order(axis, part(x, me), swap(part(x, 1 - me), axis))


def gather(x, axis):
    if lax.axis_size(axis) != 2:
        return lax.all_gather(x, axis)
    return in_order(axis, x, swap(x, axis))


def total(x, axis):
    if lax.axis_size(axis) != 2:
        return lax.psum(x, axis)
    return x + swap(x, axis)


def mode_one(rows, core):
    a, s, t = rows.shape[0], core.shape[0], core.shape[1]
    halves = 128 // t
    q = s // halves

    def body(rows_ref, core_ref, out_ref):
        left = rows_ref[...]
        for n in range(q):
            right = jnp.concatenate([core_ref[h * q + n] for h in range(halves)], axis=0)
            out_ref[:, n, :] = product(left, right, ((1,), (1,)))

    return pl.pallas_call(
        body,
        out_shape=shape(a, q, halves * t),
        in_specs=[vmem, vmem],
        out_specs=vmem,
        compiler_params=params,
        cost_estimate=pl.CostEstimate(flops=12 * a * s * t * 128, bytes_accessed=4 * s * t * 128, transcendentals=0),
    )(rows, core)


def mode_two(place, arrived, mine, other, e, t):
    nz, ny, rows, wide = arrived.shape
    q, halves, half_j, full_s = rows // e, wide // t, mine.shape[2], mine.shape[1] * wide
    j = nz * half_j

    def body(place_ref, arrived_ref, mine_ref, other_ref, one_ref, two_ref, moved_ref):
        me = place_ref[0]
        for c in range(mine_ref.shape[1]):
            here = pl.ds(c * wide, wide)
            two_ref[:, pl.ds(me, 1), :, here] = mine_ref[:, c][:, None]
            two_ref[:, pl.ds(1 - me, 1), :, here] = other_ref[:, c][:, None]
        for n in range(e):
            for h in range(halves):
                pieces = [arrived_ref[z, :, pl.ds(n * q, q), pl.ds(h * t, t)] for z in range(nz)]
                one_ref[:, h, :, pl.ds(n * wide, wide)] = jnp.concatenate(pieces, axis=-1)
        after = product(
            two_ref[...].reshape(ny * j, full_s), one_ref[...].reshape(full_s, e * wide), ((1,), (0,))
        )
        for n in range(e):
            moved_ref[:, n] = after[:, n * wide : (n + 1) * wide].reshape(ny, j, wide)

    one, two = (ny, halves, q, e * wide), (ny, nz, half_j, full_s)
    return pl.pallas_call(
        body,
        out_shape=[shape(*one), shape(*two), shape(ny, e, j, wide)],
        in_specs=[smem, vmem, vmem, vmem],
        out_specs=[vmem] * 3,
        compiler_params=params,
    )(place, arrived, mine, other)


def back(place, moved, gram, gram_other, early, one, two):
    ny, e, j, wide = moved.shape
    _, halves, q, _ = one.shape
    _, nz, half_j, full_s = two.shape

    def body(place_ref, moved_ref, gram_ref, gram_other_ref, early_ref, one_ref, two_ref, wide_ref, keep_ref, send_ref, sum_ref):
        me = place_ref[0]
        square = gram_ref[...] + gram_other_ref[...]
        whole_two = two_ref[...].reshape(ny * j, full_s)
        for n in range(e):
            folded = product(moved_ref[:, n].reshape(ny * j, wide), square, ((1,), (0,)))
            folded = folded - early_ref[:, pl.ds(n * j, j)].reshape(ny * j, wide)
            term = product(folded, one_ref[:, :, :, pl.ds(n * wide, wide)].reshape(full_s, wide), ((1,), (1,)))
            term = term.reshape(ny, nz, half_j, full_s)
            if n == 0:
                sum_ref[...] = term
            else:
                sum_ref[...] += term
            spread = product(whole_two, folded, ((0,), (0,))).reshape(ny, halves, q, wide)
            for h in range(halves):
                wide_ref[h, :, pl.ds(n * q, q)] = spread[:, h]
        keep_ref[...] = sum_ref[:, pl.ds(me, 1)].reshape(ny, half_j, full_s)
        send_ref[...] = sum_ref[:, pl.ds(1 - me, 1)].reshape(ny, half_j, full_s)

    return pl.pallas_call(
        body,
        out_shape=[shape(halves, ny, e * q, wide), shape(ny, half_j, full_s), shape(ny, half_j, full_s)],
        in_specs=[smem] + [vmem] * 6,
        out_specs=[vmem] * 3,
        scratch_shapes=[pltpu.VMEM((ny, nz, half_j, full_s), f32)],
        compiler_params=params,
        cost_estimate=pl.CostEstimate(flops=10**9, bytes_accessed=2**21, transcendentals=0),
    )(place, moved, gram, gram_other, early, one, two)


def fit(place, tensor, mine, other, factor_three, wide_one, keep, arrived):
    rows, k = tensor.shape
    block, full_t = mine.shape
    nz, ny, edge, _ = wide_one.shape
    half_j = keep.shape[1]
    cut = k // (ny * nz)

    def body(place_ref, tensor_ref, mine_ref, other_ref, factor_ref, wide_ref, keep_ref, arrived_ref, residual_ref, late_ref, field_ref, left_ref, sems):
        me = place_ref[0]
        at = [pl.ds(pl.multiple_of(h * block, block), block) for h in (me, 1 - me)]
        fields = [pltpu.make_async_copy(tensor_ref.at[at[h]], field_ref.at[h], sems.at[h]) for h in range(2)]
        lefts = [pltpu.make_async_copy(left_ref.at[h], residual_ref.at[at[h]], sems.at[2 + h]) for h in range(2)]
        wide = pltpu.make_async_copy(wide_ref, late_ref.at[:, :, pl.ds(0, edge)], sems.at[4])
        for copy in fields:
            copy.start()
        wide.start()
        both = keep_ref[...] + arrived_ref[...]
        for z in range(nz):
            late_ref[z, :, pl.ds(edge, half_j)] = both[:, :, z * full_t : (z + 1) * full_t]
        term = jnp.zeros((full_t, k), f32)
        factor = factor_ref[...].T
        for h, ref in enumerate((mine_ref, other_ref)):
            after = ref[...]
            left = product(after, factor, ((1,), (0,)))
            fields[h].wait()
            left = left - field_ref[h]
            left_ref[h] = left
            lefts[h].start()
            term = term + product(after, left, ((0,), (0,)))
        pieces = term.T.reshape(ny, nz, cut, full_t)
        for z in range(nz):
            late_ref[z, :, pl.ds(edge + half_j, cut)] = pieces[:, z]
        wide.wait()
        for copy in lefts:
            copy.wait()

    return pl.pallas_call(
        body,
        out_shape=[shape(rows, k), shape(nz, ny, edge + half_j + cut, full_t)],
        in_specs=[smem, hbm, vmem, vmem, vmem, hbm, vmem, vmem],
        out_specs=[hbm, vmem],
        scratch_shapes=[pltpu.VMEM((2, block, k), f32), pltpu.VMEM((2, block, k), f32), pltpu.SemaphoreType.DMA((5,))],
        compiler_params=params,
        cost_estimate=pl.CostEstimate(flops=24 * rows * k * full_t, bytes_accessed=8 * rows * k, transcendentals=0),
    )(place, tensor, mine, other, factor_three, wide_one, keep, arrived)


def mode_one_term(place, late, own_mine, own_other, near_mine, near_other, e):
    n, _, wide = late.shape
    q, t, r = own_mine.shape
    i = n * e
    group = min(q, 256 // t)

    def body(place_ref, late_ref, own_mine_ref, own_other_ref, near_mine_ref, near_other_ref, keep_ref, send_ref, rows_ref):
        rows_ref[...] = late_ref[:, pl.ds(0, e * q)].reshape(i * q, wide)
        first = place_ref[0] == 0
        sum_here = jnp.zeros((i, 2 * r), f32)
        for p in range(0, q, group):
            parts = [rows_ref[pl.ds(p + m, i, stride=q), :] for m in range(group)]
            low = jnp.concatenate([x[:, :t] for x in parts], axis=1)
            high = jnp.concatenate([x[:, t:] for x in parts], axis=1)
            for left, pair in (
                (jnp.where(first, low, high), (own_mine_ref, near_mine_ref)),
                (jnp.where(first, high, low), (own_other_ref, near_other_ref)),
            ):
                right = jnp.concatenate([ref[pl.ds(p, group)].reshape(group * t, r) for ref in pair], axis=1)
                sum_here = sum_here + product(left, right, ((1,), (0,)))
        same = place_ref[0] == place_ref[1]
        keep_ref[...] = jnp.where(same, sum_here[:, :r], sum_here[:, r:])
        send_ref[...] = jnp.where(same, sum_here[:, r:], sum_here[:, :r])

    return pl.pallas_call(
        body,
        out_shape=[shape(i, r), shape(i, r)],
        in_specs=[smem] + [vmem] * 5,
        out_specs=[vmem] * 2,
        scratch_shapes=[pltpu.VMEM((i * q, wide), f32)],
        compiler_params=params,
    )(place, late, own_mine, own_other, near_mine, near_other)


def local(tensor, core, factor_one, factor_two, factor_three):
    nx, ny, nz = lax.axis_size("gx"), lax.axis_size("gy"), lax.axis_size("gz")
    i, j, k = tensor.shape
    r, s, t = core.shape
    e, q, full_t, full_s, full_r = i // (ny * nz), s // nz, t * nz, s * ny, r * nx
    half_j, half_r, rows = j // nz, full_r // nz, i * j
    gx, gz = lax.axis_index("gx"), lax.axis_index("gz")
    place = jnp.stack([gz, gx]).astype(jnp.int32)
    flat = core.transpose(1, 2, 0)

    if nx == 2:
        other_one = swap(lax.dynamic_slice_in_dim(factor_one, (1 - gx) * r, r, axis=1), "gx")

    halves = tensor.reshape(nz, rows // nz, k)
    folded = swap(dot("ac,ct->at", part(halves, 1 - gz), factor_three), "gz")
    folded = folded + dot("ac,ct->at", part(halves, gz), factor_three)
    mine_two = part(factor_two.reshape(nz, half_j, full_s), gz)
    mine_two = jnp.concatenate([mine_two[:, c * full_t : (c + 1) * full_t] for c in range(full_s // full_t)], axis=0)
    early = jnp.concatenate(
        [folded.reshape(ny, e * j, full_t), jnp.broadcast_to(mine_two[None], (ny,) + mine_two.shape)], axis=1
    )
    if nx == 2:
        mine_one = lax.dynamic_slice_in_dim(factor_one, gx * r, r, axis=1)
        early, other_one = lax.optimization_barrier((early, other_one))
        sent = swap(mode_one(other_one, flat), "gx")
        after_one = mode_one(mine_one, flat) + sent
    else:
        every_one = trade(factor_one.reshape(i, nx, r).transpose(1, 0, 2), "gx")
        after_one = dot("xar,hqtr->xaqht", every_one, flat.reshape(nz, q, t, r)).reshape(nx, i, q, full_t)
        after_one = lax.psum_scatter(after_one, "gx", scatter_dimension=0)

    early = lax.all_to_all(early, "gy", 0, 0, tiled=True)
    early, after_one = lax.optimization_barrier((early, after_one))
    mine_two = early[:, e * j :].reshape(ny, full_s // full_t, half_j, full_t)
    other_two = swap(mine_two, "gz")
    gram = dot("ct,cu->tu", factor_three, factor_three)
    gram_other = swap(gram, "gz")

    flat = flat.reshape(nz, q, t, r)
    if nx == 2:
        own_mine, own_other = part(flat, gz), swap(part(flat, 1 - gz), "gz")
        near_mine = swap(own_mine, "gx")
    after_one = lax.all_to_all(after_one.reshape(nz * ny, e * q, full_t), ("gz", "gy"), 0, 0, tiled=True)
    after_one = after_one.reshape(nz, ny, e * q, full_t)
    one, two, moved = mode_two(place, after_one, mine_two, other_two, e, t)
    home = lax.all_to_all(moved, "gy", 0, 0, tiled=True).reshape(rows // nz, full_t)
    wide_one, keep, send = back(place, moved, gram, gram_other, early, one, two)
    arrived = swap(send, "gz")

    home, arrived = lax.optimization_barrier((home, arrived))

    residual, late = fit(place, tensor.reshape(rows, k), home, swap(home, "gz"), factor_three, wide_one, keep, arrived)
    if nx == 2:
        late, near_mine = lax.optimization_barrier((late, near_mine))
    late = lax.all_to_all(late.reshape((nz * ny,) + late.shape[2:]), ("gz", "gy"), 0, 0, tiled=True)
    sums = total(late[:, e * q :].reshape(nz, ny, -1, full_t).sum(axis=1), "gx")
    share_two, share_three = sums[:, :half_j], sums[:, half_j:]
    if nx == 2:
        keep_one, send_one = mode_one_term(place, late, own_mine, own_other, near_mine, swap(own_other, "gx"), e)
        term_one = keep_one + swap(send_one, "gz")
    else:
        share_one = late[:, : e * q].reshape(i, q, full_t)
        every_core = gather(trade(flat, "gz"), "gx")
        term_one = dot("aqht,xhqtr->axr", share_one.reshape(i, q, nz, t), every_core)
        term_one = lax.psum_scatter(term_one.reshape(i, nz, half_r).transpose(1, 0, 2), "gz", scatter_dimension=0)

    last = jnp.concatenate([term_one.reshape(nz, -1, full_t), share_three], axis=1)
    last = jnp.broadcast_to(last[:, None], (nz, ny) + last.shape[1:])
    last = lax.all_to_all(last.reshape((nz * ny,) + last.shape[2:]), ("gz", "gy"), 0, 0, tiled=True)
    last = last.reshape((nz, ny) + last.shape[1:])
    cut = (i // nz) * half_r // full_t
    grad_one = last[:, :, :cut].sum(axis=1).reshape(nz, i // nz, half_r)
    grad_one = gather(grad_one.transpose(1, 0, 2).reshape(i // nz, full_r), "gz").reshape(i, full_r)
    grad_three = last[:, :, cut:].transpose(1, 0, 2, 3).reshape(k, full_t)
    share_two = gather(share_two.reshape(j, full_s // nz), "gz")
    grad_two = jnp.concatenate([share_two[z] for z in range(nz)], axis=1)

    grad_one = grad_one / jnp.sqrt(f32(j * ny * k * nz))
    grad_two = grad_two / jnp.sqrt(f32(i * nx * k * nz))
    grad_three = grad_three / jnp.sqrt(f32(i * nx * j * ny))
    return (residual.reshape(i, j, k), grad_one, grad_two, grad_three)


def solution(mesh):
    placed = (P("gx", "gy", "gz"), P("gx", "gy", "gz"), P("gx", None), P("gy", None), P("gz", None))
    return jax.shard_map(
        local,
        mesh=mesh,
        in_specs=placed,
        out_specs=(P("gx", "gy", "gz"), P("gx", None), P("gy", None), P("gz", None)),
        check_vma=False,
    )
```

time: 582 us -> 107 us (0.18)
  waiting for transfers between devices: 426 us -> 44.3 us
  blocking collectives: 78.9 us -> 0 us
  matrix products: 38.3 us -> 3.65 us
  starting transfers between devices: 0.51 us -> 35 us
  local copies, waits for them, and re-layouts: 20.4 us -> 5.56 us
  Pallas kernels: 0 us -> 13.8 us
  between operations: 14.3 us -> 0.91 us
    all_gather x3 -> x0, waiting for transfers between devices: 172 us -> none  [the longest x1 73.5 us: local(): lax.all_gather(after_one, 'gy', axis=1, tiled=True)]
    reduce_scatter x3 -> x0, waiting for transfers between devices: 136 us -> none  [the longest x1 75.7 us: local(): lax.psum_scatter(wide_one, 'gy', scatter_dimension=1, tiled=True)]
    psum x1 -> x0, waiting for transfers between devices: 110 us -> none  [local(): grad_three = lax.psum(term_three, ('gx', 'gy'))]
    psum x2 -> x0, blocking collectives: 75.6 us -> none  [the longest x1 63.8 us: local(): grad_one = lax.psum(term_one, ('gy', 'gz'))]
    dot_general x9 -> x3, matrix products: 38.3 us -> 3.65 us  [dot(): return jnp.einsum(spec, left, right, precision=highest)]
    all_to_all x0 -> x5, waiting for transfers between devices: none -> 32.2 us  [the longest x1 12.4 us: local(): lax.all_to_all(late.reshape((nz * ny,) + late.shape[2:]), ('gz', 'gy'), 0...]
    all_to_all x0 -> x5, starting transfers between devices: none -> 24.5 us  [the longest x1 5.84 us: local(): early = lax.all_to_all(early, 'gy', 0, 0, tiled=True)]
    pallas_call x0 -> x6, Pallas kernels: none -> 13.8 us  [the longest x1 4.17 us: fit(): pl.pallas_call(body, out_shape=[shape(rows, k), shape(nz, ny, edge + half...]
  transfers between devices with their start and end apart: 8 -> 19, of which waited for: 8 -> 12; matrix products, arithmetic and copies ran while one was open for 4% -> 5% of each run, Pallas kernels for 0% -> 11%
where the time goes in v3:
time: 107 us; the launch traced here: 106 us
  waiting for transfers between devices  44.3 us (41%)
  starting transfers between devices  35 us (33%)
  Pallas kernels  13.8 us (13%)
  local copies, waits for them, and re-layouts  5.56 us (5%)
  matrix products  3.65 us (3%)
  other arithmetic  2.88 us (3%)
    all_to_all x1, waiting for transfers between devices, local(): lax.all_to_all(late.reshape((nz * ny,) + late.shape[2:]), ('gz', 'gy'), 0...  12.4 us
    ppermute x14, waiting for transfers between devices, swap(): return lax.ppermute(x, axis, [(0, 1), (1, 0)])  12.1 us
    ppermute x14, starting transfers between devices, swap(): return lax.ppermute(x, axis, [(0, 1), (1, 0)])  10.5 us
    all_to_all x1, waiting for transfers between devices, local(): lax.all_to_all(last.reshape((nz * ny,) + last.shape[2:]), ('gz', 'gy'), 0...  9.11 us
    all_to_all x1, waiting for transfers between devices, local(): lax.all_to_all(after_one.reshape(nz * ny, e * q, full_t), ('gz', 'gy'), 0...  8.89 us
    all_to_all x1, starting transfers between devices, local(): early = lax.all_to_all(early, 'gy', 0, 0, tiled=True)  5.84 us
    all_to_all x1, starting transfers between devices, local(): lax.all_to_all(late.reshape((nz * ny,) + late.shape[2:]), ('gz', 'gy'), 0...  5.71 us
    all_to_all x1, starting transfers between devices, local(): lax.all_to_all(last.reshape((nz * ny,) + last.shape[2:]), ('gz', 'gy'), 0...  5.05 us
  transfers between devices with their start and end apart: 19, of which 12 were waited for; matrix products, arithmetic and copies ran while one was open for 5% of the time, Pallas kernels for 11%

profile of v3, /device:TPU:0, one launch (start us, length us, event | category | flops | bytes accessed | tf_op | source)
XLA Modules:
  0.0 106.1 jit_solution(12237757820456436057)
XLA Ops:
  0.7 1.6 %fusion.1 = f32[512,128]{1,0:T(8,128)S(1)} fusion(f32[256,128]{1,0:T(8,128)} %factor_ref.1, f32[2,512,256]{2,1,0:T(8,128)} %bitcast.64, s32[]{:T(128)S(6)} %select_n.42), kind=kOutput, calls=%fused_computation.2 | convolution fusion | flops 201326592 | bytes 917508 | tf_op jit(solution)/shard_map/ac,ct->at/dot_general | solution.py:21
  2.9 2.6 %collective-permute-start.1 = (f32[32,128]{1,0:T(8,128)S(1)}, f32[32,128]{1,0:T(8,128)S(1)}, u32[]{:S(2)}, u32[]{:S(2)}) collective-permute-start(f32[32,128]{1,0:T(8,128)S(1)} %get-tuple-element.51), channel_id=1, source_target_pairs={{0,16},{16,0},{1,17},{17,1},{2,18},{18,2},{3,19},{19,3},{4,20},{20... | collective-permute-start | bytes 49160 | tf_op jit(solution)/shard_map/ppermute | solution.py:29
  5.5 1.6 %convolution_add_fusion = f32[512,128]{1,0:T(8,128)S(1)} fusion(f32[512,128]{1,0:T(8,128)S(1)} %collective-permute-done, f32[256,128]{1,0:T(8,128)S(1)} %copy-done.2, f32[2,512,256]{2,1,0:T(8,128)} %bitcast.65, s32[]{:T(128)S(6)} %select_n.43), kind=kOutput, calls=%fused_computation | convolution fusion | flops 201392128 | bytes 1179652 | tf_op jit(solution)/shard_map/ac,ct->at/dot_general | solution.py:21
  7.9 5.8 %all-to-all-start = ((f32[8,96,128]{2,1,0:T(8,128)}), f32[8,96,128]{2,1,0:T(8,128)S(1)}, u32[]{:S(2)}, u32[]{:S(2)}) async-start(f32[8,96,128]{2,1,0:T(8,128)} %pad_maximum_fusion), calls=%async_computation | async-start | bytes 786432 | tf_op jit(solution)/shard_map/all_to_all | solution.py:259
  13.8 1.8 %shard_map.85 = f32[32,16,128]{2,1,0:T(8,128)S(1)} custom-call(f32[32,128]{1,0:T(8,128)S(1)} %collective-permute-done.1.rows_ref, f32[32,64,128]{2,1,0:T(8,128)S(1)} %bitcast.60), custom_call_target="tpu_custom_call" | custom-call | flops 100663296 | bytes 1048576 | tf_op jit(solution)/shard_map/pallas_call | solution.py:71
  15.5 1.4 %collective-permute-start.2 = (f32[32,16,128]{2,1,0:T(8,128)S(1)}, f32[32,16,128]{2,1,0:T(8,128)S(1)}, u32[]{:S(2)}, u32[]{:S(2)}) collective-permute-start(f32[32,16,128]{2,1,0:T(8,128)S(1)} %shard_map.85), channel_id=1, source_target_pairs={{0,16},{16,0},{1,17},{17,1},{2,18},{18,2},{3,19},{19,3},{4,20},{20... | collective-permute-start | bytes 786440 | tf_op jit(solution)/shard_map/ppermute | solution.py:29
  17.0 1.8 %shard_map.84 = f32[32,16,128]{2,1,0:T(8,128)S(1)} custom-call(f32[32,128]{1,0:T(8,128)S(1)} %get-tuple-element.50.rows_ref, f32[32,64,128]{2,1,0:T(8,128)S(1)} %bitcast.61), custom_call_target="tpu_custom_call" | custom-call | flops 100663296 | bytes 1048576 | tf_op jit(solution)/shard_map/pallas_call | solution.py:71
  18.7 4.9 %collective-permute-done.2 = f32[32,16,128]{2,1,0:T(8,128)S(1)} collective-permute-done((f32[32,16,128]{2,1,0:T(8,128)S(1)}, f32[32,16,128]{2,1,0:T(8,128)S(1)}, u32[]{:S(2)}, u32[]{:S(2)}) %collective-permute-start.2) | collective-permute-done | bytes 262176 | tf_op jit(solution)/shard_map/ppermute | solution.py:29
  25.7 4.5 %all-to-all-start.1 = ((f32[16,32,128]{2,1,0:T(8,128)}), f32[16,32,128]{2,1,0:T(8,128)S(1)}, u32[]{:S(2)}, u32[]{:S(2)}) async-start(f32[16,32,128]{2,1,0:T(8,128)} %bitcast.10), calls=%async_computation.1 | async-start | bytes 524288 | tf_op jit(solution)/shard_map/all_to_all | solution.py:270
  31.7 8.9 %all-to-all-done.1 = f32[16,32,128]{2,1,0:T(8,128)S(1)} async-done(((f32[16,32,128]{2,1,0:T(8,128)}), f32[16,32,128]{2,1,0:T(8,128)S(1)}, u32[]{:S(2)}, u32[]{:S(2)}) %all-to-all-start.1) | async-done | bytes 262176 | tf_op jit(solution)/shard_map/all_to_all | solution.py:270
  40.6 1.7 %shard_map.86 = (f32[8,2,16,256]{3,2,1,0:T(8,128)S(1)}, f32[8,2,16,256]{3,2,1,0:T(8,128)S(1)}, f32[8,2,32,128]{3,2,1,0:T(8,128)}) custom-call(s32[2]{0:T(128)S(1)} %pad_add_fusion.place_ref, f32[2,8,32,128]{3,2,1,0:T(8,128)S(1)} %bitcast.63, f32[8,2,16,128]{3,2,1,0:T(8,128)S(1)} %bitcast.68, f32[8,2,16,128]{3,2,1,0:T(8,128)S(1)} %collective-permute-done.3.other_ref), custom_call_target="tpu_custom_call" | custom-call | tf_op jit(solution)/shard_map/pallas_call | solution.py:103
  42.3 3.4 %all-to-all-start.2 = ((f32[8,2,32,128]{3,2,1,0:T(8,128)}), f32[8,2,32,128]{3,2,1,0:T(8,128)S(1)}, u32[]{:S(2)}, u32[]{:S(2)}) async-start(f32[8,2,32,128]{3,2,1,0:T(8,128)} %get-tuple-element.26.moved_ref), calls=%async_computation.2 | async-start | bytes 524288 | tf_op jit(solution)/shard_map/all_to_all | solution.py:273
  47.1 1.4 %collective-permute-start.7 = (f32[16,64,128]{2,1,0:T(8,128)S(1)}, f32[16,64,128]{2,1,0:T(8,128)S(1)}, u32[]{:S(2)}, u32[]{:S(2)}) collective-permute-start(f32[16,64,128]{2,1,0:T(8,128)S(1)} %get-tuple-element.41.own_mine_ref), channel_id=1, source_target_pairs={{0,16},{16,0},{1,17},{17,1},{2,18},{18,2},{3,19},{19,3},{4,20},{20... | collective-permute-start | bytes 1572872 | tf_op jit(solution)/shard_map/ppermute | solution.py:29
  48.5 2.6 %shard_map.87 = (f32[2,8,32,128]{3,2,1,0:T(8,128)S(1)}, f32[8,16,256]{2,1,0:T(8,128)S(1)}, f32[8,16,256]{2,1,0:T(8,128)S(1)}) custom-call(s32[2]{0:T(128)S(1)} %pad_add_fusion.place_ref, f32[8,2,32,128]{3,2,1,0:T(8,128)} %get-tuple-element.26.moved_ref, f32[128,128]{1,0:T(8,128)S(1)} %fusion.10.gram_ref, ...), custom_call_target="tpu_custom_call" | custom-call | flops 1000000000 | bytes 2097152 | tf_op jit(solution)/shard_map/pallas_call | solution.py:136
  54.3 1.5 %collective-permute-done.6.other_ref = f32[512,128]{1,0:T(8,128)S(1)} collective-permute-done((f32[512,128]{1,0:T(8,128)S(1)}, f32[512,128]{1,0:T(8,128)S(1)}, u32[]{:S(2)}, u32[]{:S(2)}) %collective-permute-start.6) | collective-permute-done | bytes 262176 | tf_op jit(solution)/shard_map/ppermute | solution.py:29
  57.7 4.2 %shard_map.88 = (f32[1024,256]{1,0:T(8,128)}, f32[2,8,64,128]{3,2,1,0:T(8,128)}) custom-call(s32[2]{0:T(128)S(1)} %pad_add_fusion.place_ref, f32[1024,256]{1,0:T(8,128)S(1)} %bitcast.66, f32[512,128]{1,0:T(8,128)S(1)} %bitcast.70, f32[512,128]{1,0:T(8,128)S(1)} %collective-permute-done.6.other_ref, f32[256,128]{1,0:T(8,128)S(1)} %copy-done.2, ...), custom_call_target="tpu_custom_call" | custom-call | flops 805306368 | bytes 2097152 | tf_op jit(solution)/shard_map/pallas_call | solution.py:183
  61.9 5.7 %all-to-all-start.3 = ((f32[16,64,128]{2,1,0:T(8,128)}), f32[16,64,128]{2,1,0:T(8,128)S(1)}, u32[]{:S(2)}, u32[]{:S(2)}) async-start(f32[16,64,128]{2,1,0:T(8,128)} %bitcast.17), calls=%async_computation.3 | async-start | bytes 1048576 | tf_op jit(solution)/shard_map/all_to_all | solution.py:282
  68.1 1.5 %collective-permute-done.8.own_other_ref = f32[16,64,128]{2,1,0:T(8,128)S(1)} collective-permute-done((f32[16,64,128]{2,1,0:T(8,128)S(1)}, f32[16,64,128]{2,1,0:T(8,128)S(1)}, u32[]{:S(2)}, u32[]{:S(2)}) %collective-permute-start.8) | collective-permute-done | bytes 524320 | tf_op jit(solution)/shard_map/ppermute | solution.py:29
  69.6 1.4 %collective-permute-start.9 = (f32[16,64,128]{2,1,0:T(8,128)S(1)}, f32[16,64,128]{2,1,0:T(8,128)S(1)}, u32[]{:S(2)}, u32[]{:S(2)}) collective-permute-start(f32[16,64,128]{2,1,0:T(8,128)S(1)} %collective-permute-done.8.own_other_ref), channel_id=1, source_target_pairs={{0,16},{16,0},{1,17},{17,1},{2,18},{18,2},{3,19},{19,3},{4,20},{20... | collective-permute-start | bytes 1572872 | tf_op jit(solution)/shard_map/ppermute | solution.py:29
  71.0 12.4 %all-to-all-done.3.late_ref = f32[16,64,128]{2,1,0:T(8,128)S(1)} async-done(((f32[16,64,128]{2,1,0:T(8,128)}), f32[16,64,128]{2,1,0:T(8,128)S(1)}, u32[]{:S(2)}, u32[]{:S(2)}) %all-to-all-start.3) | async-done | bytes 524320 | tf_op jit(solution)/shard_map/all_to_all | solution.py:282
  83.4 1.4 %collective-permute-start.11 = (f32[2,32,128]{2,1,0:T(8,128)S(1)}, f32[2,32,128]{2,1,0:T(8,128)S(1)}, u32[]{:S(2)}, u32[]{:S(2)}) collective-permute-start(f32[2,32,128]{2,1,0:T(8,128)S(1)} %bitcast_reduce_fusion), channel_id=1, source_target_pairs={{0,16},{16,0},{1,17},{17,1},{2,18},{18,2},{3,19},{19,3},{4,20},{20... | collective-permute-start | bytes 98312 | tf_op jit(solution)/shard_map/ppermute | solution.py:29
  84.9 1.8 %shard_map.89 = (f32[32,128]{1,0:T(8,128)S(1)}, f32[32,128]{1,0:T(8,128)S(1)}) custom-call(s32[2]{0:T(128)S(1)} %pad_add_fusion.place_ref, f32[16,64,128]{2,1,0:T(8,128)S(1)} %all-to-all-done.3.late_ref, f32[16,64,128]{2,1,0:T(8,128)S(1)} %get-tuple-element.41.own_mine_ref, f32[16,64,128]{2,1,0:T(8,128)S(1)} %collective-permute-done.8.own_other_ref, ...), custom_call_target="tpu_custom_call" | custom-call | tf_op jit(solution)/shard_map/pallas_call | solution.py:218
  88.7 5.0 %all-to-all-start.4 = ((f32[16,32,128]{2,1,0:T(8,128)}), f32[16,32,128]{2,1,0:T(8,128)S(1)}, u32[]{:S(2)}, u32[]{:S(2)}) async-start(f32[16,32,128]{2,1,0:T(8,128)} %bitcast.22), calls=%async_computation.4 | async-start | bytes 524288 | tf_op jit(solution)/shard_map/all_to_all | solution.py:296
  95.0 9.1 %all-to-all-done.4 = f32[16,32,128]{2,1,0:T(8,128)S(1)} async-done(((f32[16,32,128]{2,1,0:T(8,128)}), f32[16,32,128]{2,1,0:T(8,128)S(1)}, u32[]{:S(2)}, u32[]{:S(2)}) %all-to-all-start.4) | async-done | bytes 262176 | tf_op jit(solution)/shard_map/all_to_all | solution.py:296
  (66 shorter events, 17.0 us)
Async XLA Ops:
  0.6 4.8 %copy-start = (f32[32,256]{1,0:T(8,128)S(1)}, f32[32,256]{1,0:T(8,128)}, u32[]{:S(2)}) copy-start(f32[32,256]{1,0:T(8,128)} %param.8) | copy-start | bytes 98308
  2.3 3.2 %copy-start.2 = (f32[256,128]{1,0:T(8,128)S(1)}, f32[256,128]{1,0:T(8,128)}, u32[]{:S(2)}) copy-start(f32[256,128]{1,0:T(8,128)} %factor_ref.1) | copy-start | bytes 393220
  2.3 3.1 %collective-permute-start = (f32[512,128]{1,0:T(8,128)S(1)}, f32[512,128]{1,0:T(8,128)S(1)}, u32[]{:S(2)}, u32[]{:S(2)}) collective-permute-start(f32[512,128]{1,0:T(8,128)S(1)} %fusion.1), channel_id=1, source_target_pairs={{0,1},{1,0},{2,3},{3,2},{4,5},{5,4},{6,7},{7,6},{8,9},{9,8},{10,11... | collective-permute-start | bytes 786440 | tf_op jit(solution)/shard_map/ppermute | solution.py:29
  2.9 5.1 %collective-permute-start.1 = (f32[32,128]{1,0:T(8,128)S(1)}, f32[32,128]{1,0:T(8,128)S(1)}, u32[]{:S(2)}, u32[]{:S(2)}) collective-permute-start(f32[32,128]{1,0:T(8,128)S(1)} %get-tuple-element.51), channel_id=1, source_target_pairs={{0,16},{16,0},{1,17},{17,1},{2,18},{18,2},{3,19},{19,3},{4,20},{20... | collective-permute-start | bytes 49160 | tf_op jit(solution)/shard_map/ppermute | solution.py:29
  7.1 6.6 %copy-start.1 = (f32[128,32,64]{0,2,1:T(8,128)S(1)}, f32[128,32,64]{0,2,1:T(8,128)}, u32[]{:S(2)}) copy-start(f32[128,32,64]{0,2,1:T(8,128)} %param.6) | copy-start | bytes 3145732
  7.9 17.8 %all-to-all-start = ((f32[8,96,128]{2,1,0:T(8,128)}), f32[8,96,128]{2,1,0:T(8,128)S(1)}, u32[]{:S(2)}, u32[]{:S(2)}) async-start(f32[8,96,128]{2,1,0:T(8,128)} %pad_maximum_fusion), calls=%async_computation | async-start | bytes 786432 | tf_op jit(solution)/shard_map/all_to_all | solution.py:259
  15.5 8.1 %collective-permute-start.2 = (f32[32,16,128]{2,1,0:T(8,128)S(1)}, f32[32,16,128]{2,1,0:T(8,128)S(1)}, u32[]{:S(2)}, u32[]{:S(2)}) collective-permute-start(f32[32,16,128]{2,1,0:T(8,128)S(1)} %shard_map.85), channel_id=1, source_target_pairs={{0,16},{16,0},{1,17},{17,1},{2,18},{18,2},{3,19},{19,3},{4,20},{20... | collective-permute-start | bytes 786440 | tf_op jit(solution)/shard_map/ppermute | solution.py:29
  25.7 14.9 %all-to-all-start.1 = ((f32[16,32,128]{2,1,0:T(8,128)}), f32[16,32,128]{2,1,0:T(8,128)S(1)}, u32[]{:S(2)}, u32[]{:S(2)}) async-start(f32[16,32,128]{2,1,0:T(8,128)} %bitcast.10), calls=%async_computation.1 | async-start | bytes 524288 | tf_op jit(solution)/shard_map/all_to_all | solution.py:270
  30.2 1.5 %collective-permute-start.3 = (f32[8,2,16,128]{3,2,1,0:T(8,128)S(1)}, f32[8,2,16,128]{3,2,1,0:T(8,128)S(1)}, u32[]{:S(2)}, u32[]{:S(2)}) collective-permute-start(f32[8,2,16,128]{3,2,1,0:T(8,128)S(1)} %bitcast.67), channel_id=1, source_target_pairs={{0,1},{1,0},{2,3},{3,2},{4,5},{5,4},{6,7},{7,6},{8,9},{9,8},{10,11... | collective-permute-start | bytes 393224 | tf_op jit(solution)/shard_map/ppermute | solution.py:29
  42.3 12.0 %all-to-all-start.2 = ((f32[8,2,32,128]{3,2,1,0:T(8,128)}), f32[8,2,32,128]{3,2,1,0:T(8,128)S(1)}, u32[]{:S(2)}, u32[]{:S(2)}) async-start(f32[8,2,32,128]{3,2,1,0:T(8,128)} %get-tuple-element.26.moved_ref), calls=%async_computation.2 | async-start | bytes 524288 | tf_op jit(solution)/shard_map/all_to_all | solution.py:273
  46.1 2.3 %collective-permute-start.4 = (f32[128,128]{1,0:T(8,128)S(1)}, f32[128,128]{1,0:T(8,128)S(1)}, u32[]{:S(2)}, u32[]{:S(2)}) collective-permute-start(f32[128,128]{1,0:T(8,128)S(1)} %fusion.10.gram_ref), channel_id=1, source_target_pairs={{0,1},{1,0},{2,3},{3,2},{4,5},{5,4},{6,7},{7,6},{8,9},{9,8},{10,11... | collective-permute-start | bytes 196616 | tf_op jit(solution)/shard_map/ppermute | solution.py:29
  47.1 14.8 %collective-permute-start.7 = (f32[16,64,128]{2,1,0:T(8,128)S(1)}, f32[16,64,128]{2,1,0:T(8,128)S(1)}, u32[]{:S(2)}, u32[]{:S(2)}) collective-permute-start(f32[16,64,128]{2,1,0:T(8,128)S(1)} %get-tuple-element.41.own_mine_ref), channel_id=1, source_target_pairs={{0,16},{16,0},{1,17},{17,1},{2,18},{18,2},{3,19},{19,3},{4,20},{20... | collective-permute-start | bytes 1572872 | tf_op jit(solution)/shard_map/ppermute | solution.py:29
  48.5 7.3 %copy-start.3 = (f32[32,32,256]{2,1,0:T(8,128)S(1)}, f32[32,32,256]{2,1,0:T(8,128)}, u32[]{:S(2)}) copy-start(f32[32,32,256]{2,1,0:T(8,128)} %param.5) | copy-start | bytes 3145732
  52.5 1.3 %collective-permute-start.5 = (f32[8,16,256]{2,1,0:T(8,128)S(1)}, f32[8,16,256]{2,1,0:T(8,128)S(1)}, u32[]{:S(2)}, u32[]{:S(2)}) collective-permute-start(f32[8,16,256]{2,1,0:T(8,128)S(1)} %get-tuple-element.29), channel_id=1, source_target_pairs={{0,1},{1,0},{2,3},{3,2},{4,5},{5,4},{6,7},{7,6},{8,9},{9,8},{10,11... | collective-permute-start | bytes 393224 | tf_op jit(solution)/shard_map/ppermute | solution.py:29
  54.3 1.5 %collective-permute-start.6 = (f32[512,128]{1,0:T(8,128)S(1)}, f32[512,128]{1,0:T(8,128)S(1)}, u32[]{:S(2)}, u32[]{:S(2)}) collective-permute-start(f32[512,128]{1,0:T(8,128)S(1)} %bitcast.69), channel_id=1, source_target_pairs={{0,1},{1,0},{2,3},{3,2},{4,5},{5,4},{6,7},{7,6},{8,9},{9,8},{10,11... | collective-permute-start | bytes 786440 | tf_op jit(solution)/shard_map/ppermute | solution.py:29
  61.9 5.7 %copy-start.8 = (f32[16,64,128]{2,1,0:T(8,128)S(1)}, f32[16,64,128]{2,1,0:T(8,128)}, u32[]{:S(2)}) copy-start(f32[16,64,128]{2,1,0:T(8,128)} %get-tuple-element.40) | copy-start | bytes 1572868
  61.9 21.5 %all-to-all-start.3 = ((f32[16,64,128]{2,1,0:T(8,128)}), f32[16,64,128]{2,1,0:T(8,128)S(1)}, u32[]{:S(2)}, u32[]{:S(2)}) async-start(f32[16,64,128]{2,1,0:T(8,128)} %bitcast.17), calls=%async_computation.3 | async-start | bytes 1048576 | tf_op jit(solution)/shard_map/all_to_all | solution.py:282
  67.6 2.0 %collective-permute-start.8 = (f32[16,64,128]{2,1,0:T(8,128)S(1)}, f32[16,64,128]{2,1,0:T(8,128)S(1)}, u32[]{:S(2)}, u32[]{:S(2)}) collective-permute-start(f32[16,64,128]{2,1,0:T(8,128)S(1)} %copy-done.8), channel_id=1, source_target_pairs={{0,1},{1,0},{2,3},{3,2},{4,5},{5,4},{6,7},{7,6},{8,9},{9,8},{10,11... | collective-permute-start | bytes 1572872 | tf_op jit(solution)/shard_map/ppermute | solution.py:29
  69.6 15.2 %collective-permute-start.9 = (f32[16,64,128]{2,1,0:T(8,128)S(1)}, f32[16,64,128]{2,1,0:T(8,128)S(1)}, u32[]{:S(2)}, u32[]{:S(2)}) collective-permute-start(f32[16,64,128]{2,1,0:T(8,128)S(1)} %collective-permute-done.8.own_other_ref), channel_id=1, source_target_pairs={{0,16},{16,0},{1,17},{17,1},{2,18},{18,2},{3,19},{19,3},{4,20},{20... | collective-permute-start | bytes 1572872 | tf_op jit(solution)/shard_map/ppermute | solution.py:29
  83.4 4.5 %collective-permute-start.11 = (f32[2,32,128]{2,1,0:T(8,128)S(1)}, f32[2,32,128]{2,1,0:T(8,128)S(1)}, u32[]{:S(2)}, u32[]{:S(2)}) collective-permute-start(f32[2,32,128]{2,1,0:T(8,128)S(1)} %bitcast_reduce_fusion), channel_id=1, source_target_pairs={{0,16},{16,0},{1,17},{17,1},{2,18},{18,2},{3,19},{19,3},{4,20},{20... | collective-permute-start | bytes 98312 | tf_op jit(solution)/shard_map/ppermute | solution.py:29
  86.7 1.2 %collective-permute-start.10 = (f32[32,128]{1,0:T(8,128)S(1)}, f32[32,128]{1,0:T(8,128)S(1)}, u32[]{:S(2)}, u32[]{:S(2)}) collective-permute-start(f32[32,128]{1,0:T(8,128)S(1)} %get-tuple-element.39), channel_id=1, source_target_pairs={{0,1},{1,0},{2,3},{3,2},{4,5},{5,4},{6,7},{7,6},{8,9},{9,8},{10,11... | collective-permute-start | bytes 49160 | tf_op jit(solution)/shard_map/ppermute | solution.py:29
  88.7 15.4 %all-to-all-start.4 = ((f32[16,32,128]{2,1,0:T(8,128)}), f32[16,32,128]{2,1,0:T(8,128)S(1)}, u32[]{:S(2)}, u32[]{:S(2)}) async-start(f32[16,32,128]{2,1,0:T(8,128)} %bitcast.22), calls=%async_computation.4 | async-start | bytes 524288 | tf_op jit(solution)/shard_map/all_to_all | solution.py:296
  93.7 1.3 %collective-permute-start.13 = (f32[32,128]{1,0:T(8,128)S(1)}, f32[32,128]{1,0:T(8,128)S(1)}, u32[]{:S(2)}, u32[]{:S(2)}) collective-permute-start(f32[32,128]{1,0:T(8,128)S(1)} %bitcast.75), channel_id=1, source_target_pairs={{0,1},{1,0},{2,3},{3,2},{4,5},{5,4},{6,7},{7,6},{8,9},{9,8},{10,11... | collective-permute-start | bytes 49160 | tf_op jit(solution)/shard_map/ppermute | solution.py:29
  104.1 1.4 %collective-permute-start.12 = (f32[16,256]{1,0:T(8,128)S(1)}, f32[16,256]{1,0:T(8,128)S(1)}, u32[]{:S(2)}, u32[]{:S(2)}) collective-permute-start(f32[16,256]{1,0:T(8,128)S(1)} %copy_bitcast_fusion), channel_id=1, source_target_pairs={{0,1},{1,0},{2,3},{3,2},{4,5},{5,4},{6,7},{7,6},{8,9},{9,8},{10,11... | collective-permute-start | bytes 49160 | tf_op jit(solution)/shard_map/ppermute | solution.py:29
  (5 other events, 5.4 us)

commit v4 on v3

--- a/solution.py
+++ b/solution.py
@@ -55,6 +55,75 @@
     if lax.axis_size(axis) != 2:
         return lax.psum(x, axis)
     return x + swap(x, axis)
+
+
+def fold_tensor(half, tensor, factor_three):
+    rows, k = tensor.shape
+    block, full_t = rows // 2, factor_three.shape[1]
+    pieces = 2
+    cut = block // pieces
+
+    def body(half_ref, tensor_ref, factor_in, keep_ref, send_ref, copy_ref, field_ref, whole_ref, factor_ref, loads_sem, stores_sem, sem):
+        me = half_ref[0]
+        weight = pltpu.make_async_copy(factor_in, factor_ref, sem)
+        weight.start()
+        ats = [pl.ds(n * cut, cut) for n in range(2 * pieces)]
+        loads = [pltpu.make_async_copy(tensor_ref.at[at], field_ref.at[at], loads_sem.at[n]) for n, at in enumerate(ats)]
+        stores = [pltpu.make_async_copy(field_ref.at[at], copy_ref.at[at], stores_sem.at[n]) for n, at in enumerate(ats)]
+        for copy in loads:
+            copy.start()
+        for n in range(2 * pieces):
+            loads[n].wait()
+            stores[n].start()
+        weight.wait()
+        whole_ref[...] = product(field_ref[...], factor_ref[...], ((1,), (0,)))
+        keep_ref[...] = whole_ref[pl.ds(pl.multiple_of(me * block, block), block), :]
+        send_ref[...] = whole_ref[pl.ds(pl.multiple_of((1 - me) * block, block), block), :]
+        for copy in stores:
+            copy.wait()
+
+    dma = pltpu.SemaphoreType.DMA
+    return pl.pallas_call(
+        body,
+        out_shape=[shape(block, full_t), shape(block, full_t), shape(rows, k)],
+        in_specs=[smem, hbm, hbm],
+        out_specs=[vmem, vmem, hbm],
+        scratch_shapes=[
+            pltpu.VMEM((rows, k), f32),
+            pltpu.VMEM((rows, full_t), f32),
+            pltpu.VMEM(factor_three.shape, f32),
+            dma((2 * pieces,)),
+            dma((2 * pieces,)),
+            dma,
+        ],
+        compiler_params=pltpu.CompilerParams(vmem_limit_bytes=63 * 1024 * 1024),
+    )(half, tensor, factor_three)
+
+
+def pack_early(half, keep, arrived, factor_two, ny, nz):
+    j, full_s = factor_two.shape
+    wide = keep.shape[1]
+    edge, half_j = keep.shape[0] // ny, j // nz
+    parts = full_s // wide
+
+    def body(half_ref, keep_ref, arrived_ref, factor_ref, out_ref, rows_ref, sem):
+        at = pl.ds(pl.multiple_of(half_ref[0] * half_j, half_j), half_j)
+        copy = pltpu.make_async_copy(factor_ref.at[at], rows_ref, sem)
+        copy.start()
+        out_ref[:, pl.ds(0, edge)] = (keep_ref[...] + arrived_ref[...]).reshape(ny, edge, wide)
+        copy.wait()
+        for c in range(parts):
+            piece = rows_ref[:, c * wide : (c + 1) * wide]
+            out_ref[:, pl.ds(edge + c * half_j, half_j)] = jnp.broadcast_to(piece[None], (ny, half_j, wide))
+
+    return pl.pallas_call(
+        body,
+        out_shape=shape(ny, edge + parts * half_j, wide),
+        in_specs=[smem, vmem, vmem, hbm],
+        out_specs=vmem,
+        scratch_shapes=[pltpu.VMEM((half_j, full_s), f32), pltpu.SemaphoreType.DMA],
+        compiler_params=params,
+    )(half, keep, arrived, factor_two)
 
 
 def mode_one(rows, core):
@@ -109,12 +178,12 @@
     )(place, arrived, mine, other)
 
 
-def back(place, moved, gram, gram_other, early, one, two):
+def back(place, moved, gram, gram_other, early, one, two, length):
     ny, e, j, wide = moved.shape
     _, halves, q, _ = one.shape
     _, nz, half_j, full_s = two.shape
 
-    def body(place_ref, moved_ref, gram_ref, gram_other_ref, early_ref, one_ref, two_ref, wide_ref, keep_ref, send_ref, sum_ref):
+    def body(place_ref, moved_ref, gram_ref, gram_other_ref, early_ref, one_ref, two_ref, late_ref, keep_ref, send_ref, sum_ref, wide_ref, sem):
         me = place_ref[0]
         square = gram_ref[...] + gram_other_ref[...]
         whole_two = two_ref[...].reshape(ny * j, full_s)
@@ -130,65 +199,108 @@
             spread = product(whole_two, folded, ((0,), (0,))).reshape(ny, halves, q, wide)
             for h in range(halves):
                 wide_ref[h, :, pl.ds(n * q, q)] = spread[:, h]
+        copy = pltpu.make_async_copy(wide_ref, late_ref.at[:, :, pl.ds(0, e * q)], sem)
+        copy.start()
         keep_ref[...] = sum_ref[:, pl.ds(me, 1)].reshape(ny, half_j, full_s)
         send_ref[...] = sum_ref[:, pl.ds(1 - me, 1)].reshape(ny, half_j, full_s)
-
-    return pl.pallas_call(
-        body,
-        out_shape=[shape(halves, ny, e * q, wide), shape(ny, half_j, full_s), shape(ny, half_j, full_s)],
+        copy.wait()
+
+    return pl.pallas_call(
+        body,
+        out_shape=[shape(halves, ny, length, wide), shape(ny, half_j, full_s), shape(ny, half_j, full_s)],
         in_specs=[smem] + [vmem] * 6,
-        out_specs=[vmem] * 3,
-        scratch_shapes=[pltpu.VMEM((ny, nz, half_j, full_s), f32)],
+        out_specs=[hbm, vmem, vmem],
+        scratch_shapes=[
+            pltpu.VMEM((ny, nz, half_j, full_s), f32),
+            pltpu.VMEM((halves, ny, e * q, wide), f32),
+            pltpu.SemaphoreType.DMA,
+        ],
         compiler_params=params,
         cost_estimate=pl.CostEstimate(flops=10**9, bytes_accessed=2**21, transcendentals=0),
     )(place, moved, gram, gram_other, early, one, two)
 
 
-def fit(place, tensor, mine, other, factor_three, wide_one, keep, arrived):
-    rows, k = tensor.shape
-    block, full_t = mine.shape
-    nz, ny, edge, _ = wide_one.shape
+def put_two(late, keep, arrived, edge):
+    nz, ny, _, wide = late.shape
     half_j = keep.shape[1]
-    cut = k // (ny * nz)
-
-    def body(place_ref, tensor_ref, mine_ref, other_ref, factor_ref, wide_ref, keep_ref, arrived_ref, residual_ref, late_ref, field_ref, left_ref, sems):
-        me = place_ref[0]
-        at = [pl.ds(pl.multiple_of(h * block, block), block) for h in (me, 1 - me)]
-        fields = [pltpu.make_async_copy(tensor_ref.at[at[h]], field_ref.at[h], sems.at[h]) for h in range(2)]
-        lefts = [pltpu.make_async_copy(left_ref.at[h], residual_ref.at[at[h]], sems.at[2 + h]) for h in range(2)]
-        wide = pltpu.make_async_copy(wide_ref, late_ref.at[:, :, pl.ds(0, edge)], sems.at[4])
-        for copy in fields:
-            copy.start()
-        wide.start()
+
+    def body(_, keep_ref, arrived_ref, late_ref, both_ref, sem):
         both = keep_ref[...] + arrived_ref[...]
         for z in range(nz):
-            late_ref[z, :, pl.ds(edge, half_j)] = both[:, :, z * full_t : (z + 1) * full_t]
-        term = jnp.zeros((full_t, k), f32)
-        factor = factor_ref[...].T
-        for h, ref in enumerate((mine_ref, other_ref)):
-            after = ref[...]
-            left = product(after, factor, ((1,), (0,)))
-            fields[h].wait()
-            left = left - field_ref[h]
-            left_ref[h] = left
-            lefts[h].start()
-            term = term + product(after, left, ((0,), (0,)))
-        pieces = term.T.reshape(ny, nz, cut, full_t)
+            both_ref[z] = both[:, :, z * wide : (z + 1) * wide]
+        copy = pltpu.make_async_copy(both_ref, late_ref.at[:, :, pl.ds(edge, half_j)], sem)
+        copy.start()
+        copy.wait()
+
+    return pl.pallas_call(
+        body,
+        out_shape=shape(*late.shape),
+        in_specs=[hbm, vmem, vmem],
+        out_specs=hbm,
+        scratch_shapes=[pltpu.VMEM((nz, ny, half_j, wide), f32), pltpu.SemaphoreType.DMA],
+        input_output_aliases={0: 0},
+        compiler_params=params,
+    )(late, keep, arrived)
+
+
+def fit(half, field, after, factor_three, before=None):
+    rows, k = field.shape
+    block, full_t = after.shape
+
+    def compute(half_ref, after_ref, factor_ref, residual_ref, field_ref, left_ref, sems):
+        at = pl.ds(pl.multiple_of(half_ref[0] * block, block), block)
+        field = pltpu.make_async_copy(residual_ref.at[at], field_ref, sems.at[0])
+        field.start()
+        after = after_ref[...]
+        left = product(after, factor_ref[...].T, ((1,), (0,)))
+        field.wait()
+        left = left - field_ref[...]
+        left_ref[...] = left
+        out = pltpu.make_async_copy(left_ref, residual_ref.at[at], sems.at[1])
+        out.start()
+        return product(after, left, ((0,), (0,))), out
+
+    scratch = [pltpu.VMEM((block, k), f32), pltpu.VMEM((block, k), f32), pltpu.SemaphoreType.DMA((3,))]
+    if before is None:
+
+        def body(half_ref, _, after_ref, factor_ref, residual_ref, term_ref, field_ref, left_ref, sems):
+            term, out = compute(half_ref, after_ref, factor_ref, residual_ref, field_ref, left_ref, sems)
+            term_ref[...] = term
+            out.wait()
+
+        return pl.pallas_call(
+            body,
+            out_shape=[shape(rows, k), shape(full_t, k)],
+            in_specs=[smem, hbm, vmem, vmem],
+            out_specs=[hbm, vmem],
+            scratch_shapes=scratch,
+            input_output_aliases={1: 0},
+            compiler_params=params,
+        )(half, field, after, factor_three)
+
+    term, late = before
+    nz, ny, length, _ = late.shape
+    cut = k // (ny * nz)
+
+    def body(half_ref, _, after_ref, factor_ref, term_ref, __, residual_ref, late_ref, field_ref, left_ref, sems, pieces_ref):
+        term, out = compute(half_ref, after_ref, factor_ref, residual_ref, field_ref, left_ref, sems)
+        pieces = (term + term_ref[...]).T.reshape(ny, nz, cut, full_t)
         for z in range(nz):
-            late_ref[z, :, pl.ds(edge + half_j, cut)] = pieces[:, z]
-        wide.wait()
-        for copy in lefts:
-            copy.wait()
-
-    return pl.pallas_call(
-        body,
-        out_shape=[shape(rows, k), shape(nz, ny, edge + half_j + cut, full_t)],
-        in_specs=[smem, hbm, vmem, vmem, vmem, hbm, vmem, vmem],
-        out_specs=[hbm, vmem],
-        scratch_shapes=[pltpu.VMEM((2, block, k), f32), pltpu.VMEM((2, block, k), f32), pltpu.SemaphoreType.DMA((5,))],
-        compiler_params=params,
-        cost_estimate=pl.CostEstimate(flops=24 * rows * k * full_t, bytes_accessed=8 * rows * k, transcendentals=0),
-    )(place, tensor, mine, other, factor_three, wide_one, keep, arrived)
+            pieces_ref[z] = pieces[:, z]
+        copy = pltpu.make_async_copy(pieces_ref, late_ref.at[:, :, pl.ds(length - cut, cut)], sems.at[2])
+        copy.start()
+        copy.wait()
+        out.wait()
+
+    return pl.pallas_call(
+        body,
+        out_shape=[shape(rows, k), shape(*late.shape)],
+        in_specs=[smem, hbm, vmem, vmem, vmem, hbm],
+        out_specs=[hbm, hbm],
+        scratch_shapes=scratch + [pltpu.VMEM((nz, ny, cut, full_t), f32)],
+        input_output_aliases={1: 0, 5: 1},
+        compiler_params=params,
+    )(half, field, after, factor_three, term, late)
 
 
 def mode_one_term(place, late, own_mine, own_other, near_mine, near_other, e):
@@ -238,14 +350,9 @@
     if nx == 2:
         other_one = swap(lax.dynamic_slice_in_dim(factor_one, (1 - gx) * r, r, axis=1), "gx")
 
-    halves = tensor.reshape(nz, rows // nz, k)
-    folded = swap(dot("ac,ct->at", part(halves, 1 - gz), factor_three), "gz")
-    folded = folded + dot("ac,ct->at", part(halves, gz), factor_three)
-    mine_two = part(factor_two.reshape(nz, half_j, full_s), gz)
-    mine_two = jnp.concatenate([mine_two[:, c * full_t : (c + 1) * full_t] for c in range(full_s // full_t)], axis=0)
-    early = jnp.concatenate(
-        [folded.reshape(ny, e * j, full_t), jnp.broadcast_to(mine_two[None], (ny,) + mine_two.shape)], axis=1
-    )
+    half = place[:1]
+    keep, send, field = fold_tensor(half, tensor.reshape(rows, k), factor_three)
+    early = pack_early(half, keep, swap(send, "gz"), factor_two, ny, nz)
     if nx == 2:
         mine_one = lax.dynamic_slice_in_dim(factor_one, gx * r, r, axis=1)
         early, other_one = lax.optimization_barrier((early, other_one))
@@ -271,14 +378,14 @@
     after_one = after_one.reshape(nz, ny, e * q, full_t)
     one, two, moved = mode_two(place, after_one, mine_two, other_two, e, t)
     home = lax.all_to_all(moved, "gy", 0, 0, tiled=True).reshape(rows // nz, full_t)
-    wide_one, keep, send = back(place, moved, gram, gram_other, early, one, two)
-    arrived = swap(send, "gz")
-
-    home, arrived = lax.optimization_barrier((home, arrived))
-
-    residual, late = fit(place, tensor.reshape(rows, k), home, swap(home, "gz"), factor_three, wide_one, keep, arrived)
+    late, keep, send = back(place, moved, gram, gram_other, early, one, two, e * q + half_j + k // (ny * nz))
+    late = put_two(late, keep, swap(send, "gz"), e * q)
+
     if nx == 2:
-        late, near_mine = lax.optimization_barrier((late, near_mine))
+        home, late, near_mine = lax.optimization_barrier((home, late, near_mine))
+
+    field, term_three = fit(half, field, home, factor_three)
+    residual, late = fit(1 - half, field, swap(home, "gz"), factor_three, (term_three, late))
     late = lax.all_to_all(late.reshape((nz * ny,) + late.shape[2:]), ("gz", "gy"), 0, 0, tiled=True)
     sums = total(late[:, e * q :].reshape(nz, ny, -1, full_t).sum(axis=1), "gx")
     share_two, share_three = sums[:, :half_j], sums[:, half_j:]

time: 107 us -> 104 us (0.972)
  Pallas kernels: 13.8 us -> 19.4 us
  matrix products: 3.65 us -> 0.39 us
  local copies, waits for them, and re-layouts: 5.56 us -> 3.27 us
  waiting for transfers between devices: 44.3 us -> 42.1 us
    pallas_call x2 -> x6, Pallas kernels: 6.79 us -> 12.4 us  [the longest x1 3.25 us: back(): pl.pallas_call(body, out_shape=[shape(halves, ny, length, wide), shape(ny...]
    dot_general x3 -> x1, matrix products: 3.65 us -> 0.39 us  [dot(): return jnp.einsum(spec, left, right, precision=highest)]
    unnamed x20 -> x12, local copies, waits for them, and re-layouts: 3.24 us -> 0.97 us
    ppermute x14, waiting for transfers between devices: 12.1 us -> 10.5 us  [swap(): return lax.ppermute(x, axis, [(0, 1), (1, 0)])]
    all_to_all x1, waiting for transfers between devices: 8.89 us -> 7.41 us  [local(): lax.all_to_all(after_one.reshape(nz * ny, e * q, full_t), ('gz', 'gy'), 0...]
  transfers between devices with their start and end apart: 19 -> 19, of which waited for: 12 -> 11; matrix products, arithmetic and copies ran while one was open for 5% -> 3% of each run, Pallas kernels for 11% -> 13%
where the time goes in v4:
time: 104 us; the launch traced here: 103 us
  waiting for transfers between devices  42.1 us (40%)
  starting transfers between devices  35.2 us (34%)
  Pallas kernels  19.4 us (19%)
  local copies, waits for them, and re-layouts  3.27 us (3%)
  other arithmetic  2.1 us (2%)
    all_to_all x1, waiting for transfers between devices, local(): lax.all_to_all(late.reshape((nz * ny,) + late.shape[2:]), ('gz', 'gy'), 0...  12.3 us
    ppermute x14, starting transfers between devices, swap(): return lax.ppermute(x, axis, [(0, 1), (1, 0)])  11 us
    ppermute x14, waiting for transfers between devices, swap(): return lax.ppermute(x, axis, [(0, 1), (1, 0)])  10.5 us
    all_to_all x1, waiting for transfers between devices, local(): lax.all_to_all(last.reshape((nz * ny,) + last.shape[2:]), ('gz', 'gy'), 0...  9.11 us
    all_to_all x1, waiting for transfers between devices, local(): lax.all_to_all(after_one.reshape(nz * ny, e * q, full_t), ('gz', 'gy'), 0...  7.41 us
    all_to_all x1, starting transfers between devices, local(): early = lax.all_to_all(early, 'gy', 0, 0, tiled=True)  6.31 us
    all_to_all x1, starting transfers between devices, local(): lax.all_to_all(late.reshape((nz * ny,) + late.shape[2:]), ('gz', 'gy'), 0...  4.97 us
    all_to_all x1, starting transfers between devices, local(): lax.all_to_all(last.reshape((nz * ny,) + last.shape[2:]), ('gz', 'gy'), 0...  4.92 us
  transfers between devices with their start and end apart: 19, of which 11 were waited for; matrix products, arithmetic and copies ran while one was open for 3% of the time, Pallas kernels for 13%

profile of v4, /device:TPU:0, one launch (start us, length us, event | category | flops | bytes accessed | tf_op | source)
XLA Modules:
  0.0 103.4 jit_solution(6049556953919659154)
XLA Ops:
  0.7 3.1 %shard_map.84 = (f32[512,128]{1,0:T(8,128)}, f32[512,128]{1,0:T(8,128)}, f32[1024,256]{1,0:T(8,128)}) custom-call(s32[1]{0:T(128)} %bitcast.half_ref, f32[1024,256]{1,0:T(8,128)} %bitcast.55, f32[256,128]{1,0:T(8,128)} %factor_ref.5), custom_call_target="tpu_custom_call" | custom-call | tf_op jit(solution)/shard_map/pallas_call | solution.py:86
  4.3 2.6 %collective-permute-start.1 = (f32[32,128]{1,0:T(8,128)S(1)}, f32[32,128]{1,0:T(8,128)S(1)}, u32[]{:S(2)}, u32[]{:S(2)}) collective-permute-start(f32[32,128]{1,0:T(8,128)S(1)} %get-tuple-element.59), channel_id=1, source_target_pairs={{0,16},{16,0},{1,17},{17,1},{2,18},{18,2},{3,19},{19,3},{4,20},{20... | collective-permute-start | bytes 49160 | tf_op jit(solution)/shard_map/ppermute | solution.py:29
  8.7 6.3 %all-to-all-start = ((f32[8,96,128]{2,1,0:T(8,128)}), f32[8,96,128]{2,1,0:T(8,128)S(1)}, u32[]{:S(2)}, u32[]{:S(2)}) async-start(f32[8,96,128]{2,1,0:T(8,128)} %shard_map.85), calls=%async_computation | async-start | bytes 786432 | tf_op jit(solution)/shard_map/all_to_all | solution.py:366
  15.0 1.8 %shard_map.87 = f32[32,16,128]{2,1,0:T(8,128)S(1)} custom-call(f32[32,128]{1,0:T(8,128)S(1)} %collective-permute-done.1.rows_ref, f32[32,64,128]{2,1,0:T(8,128)S(1)} %bitcast.46), custom_call_target="tpu_custom_call" | custom-call | flops 100663296 | bytes 1048576 | tf_op jit(solution)/shard_map/pallas_call | solution.py:140
  16.8 1.6 %collective-permute-start.2 = (f32[32,16,128]{2,1,0:T(8,128)S(1)}, f32[32,16,128]{2,1,0:T(8,128)S(1)}, u32[]{:S(2)}, u32[]{:S(2)}) collective-permute-start(f32[32,16,128]{2,1,0:T(8,128)S(1)} %shard_map.87), channel_id=1, source_target_pairs={{0,16},{16,0},{1,17},{17,1},{2,18},{18,2},{3,19},{19,3},{4,20},{20... | collective-permute-start | bytes 786440 | tf_op jit(solution)/shard_map/ppermute | solution.py:29
  18.4 1.8 %shard_map.86 = f32[32,16,128]{2,1,0:T(8,128)S(1)} custom-call(f32[32,128]{1,0:T(8,128)S(1)} %get-tuple-element.58.rows_ref, f32[32,64,128]{2,1,0:T(8,128)S(1)} %bitcast.47), custom_call_target="tpu_custom_call" | custom-call | flops 100663296 | bytes 1048576 | tf_op jit(solution)/shard_map/pallas_call | solution.py:140
  20.1 4.5 %collective-permute-done.2 = f32[32,16,128]{2,1,0:T(8,128)S(1)} collective-permute-done((f32[32,16,128]{2,1,0:T(8,128)S(1)}, f32[32,16,128]{2,1,0:T(8,128)S(1)}, u32[]{:S(2)}, u32[]{:S(2)}) %collective-permute-start.2) | collective-permute-done | bytes 262176 | tf_op jit(solution)/shard_map/ppermute | solution.py:29
  26.7 4.5 %all-to-all-start.1 = ((f32[16,32,128]{2,1,0:T(8,128)}), f32[16,32,128]{2,1,0:T(8,128)S(1)}, u32[]{:S(2)}, u32[]{:S(2)}) async-start(f32[16,32,128]{2,1,0:T(8,128)} %bitcast.4), calls=%async_computation.1 | async-start | bytes 524288 | tf_op jit(solution)/shard_map/all_to_all | solution.py:377
  32.5 1.5 %collective-permute-start.6 = (f32[16,64,128]{2,1,0:T(8,128)S(1)}, f32[16,64,128]{2,1,0:T(8,128)S(1)}, u32[]{:S(2)}, u32[]{:S(2)}) collective-permute-start(f32[16,64,128]{2,1,0:T(8,128)S(1)} %get-tuple-element.49.own_mine_ref), channel_id=1, source_target_pairs={{0,16},{16,0},{1,17},{17,1},{2,18},{18,2},{3,19},{19,3},{4,20},{20... | collective-permute-start | bytes 1572872 | tf_op jit(solution)/shard_map/ppermute | solution.py:29
  34.1 7.4 %all-to-all-done.1 = f32[16,32,128]{2,1,0:T(8,128)S(1)} async-done(((f32[16,32,128]{2,1,0:T(8,128)}), f32[16,32,128]{2,1,0:T(8,128)S(1)}, u32[]{:S(2)}, u32[]{:S(2)}) %all-to-all-start.1) | async-done | bytes 262176 | tf_op jit(solution)/shard_map/all_to_all | solution.py:377
  41.5 1.7 %shard_map.88 = (f32[8,2,16,256]{3,2,1,0:T(8,128)S(1)}, f32[8,2,16,256]{3,2,1,0:T(8,128)S(1)}, f32[8,2,32,128]{3,2,1,0:T(8,128)}) custom-call(s32[2]{0:T(128)S(1)} %pad_add_fusion.place_ref, f32[2,8,32,128]{3,2,1,0:T(8,128)S(1)} %bitcast.49, f32[8,2,16,128]{3,2,1,0:T(8,128)S(1)} %bitcast.53, f32[8,2,16,128]{3,2,1,0:T(8,128)S(1)} %collective-permute-done.3.other_ref), custom_call_target="tpu_custom_call" | custom-call | tf_op jit(solution)/shard_map/pallas_call | solution.py:172
  43.2 3.5 %all-to-all-start.2 = ((f32[8,2,32,128]{3,2,1,0:T(8,128)}), f32[8,2,32,128]{3,2,1,0:T(8,128)S(1)}, u32[]{:S(2)}, u32[]{:S(2)}) async-start(f32[8,2,32,128]{3,2,1,0:T(8,128)} %get-tuple-element.33.moved_ref), calls=%async_computation.2 | async-start | bytes 524288 | tf_op jit(solution)/shard_map/all_to_all | solution.py:380
  48.5 3.3 %shard_map.89 = (f32[2,8,64,128]{3,2,1,0:T(8,128)}, f32[8,16,256]{2,1,0:T(8,128)S(1)}, f32[8,16,256]{2,1,0:T(8,128)S(1)}) custom-call(s32[2]{0:T(128)S(1)} %pad_add_fusion.place_ref, f32[8,2,32,128]{3,2,1,0:T(8,128)} %get-tuple-element.33.moved_ref, f32[128,128]{1,0:T(8,128)S(1)} %fusion.2.gram_ref, f32[128,128]{1,0:T(8,128)S(1)} %collective-permute-done.4.gram_other_ref, ...), custom_call_target="tpu_custom_call" | custom-call | flops 1000000000 | bytes 2097152 | tf_op jit(solution)/shard_map/pallas_call | solution.py:208
  53.9 1.4 %all-to-all-done.2 = f32[8,2,32,128]{3,2,1,0:T(8,128)S(1)} async-done(((f32[8,2,32,128]{3,2,1,0:T(8,128)}), f32[8,2,32,128]{3,2,1,0:T(8,128)S(1)}, u32[]{:S(2)}, u32[]{:S(2)}) %all-to-all-start.2) | async-done | bytes 262176 | tf_op jit(solution)/shard_map/all_to_all | solution.py:380
  55.3 2.1 %shard_map.91 = (f32[1024,256]{1,0:T(8,128)}, f32[128,256]{1,0:T(8,128)S(1)}) custom-call(s32[1]{0:T(128)} %bitcast.half_ref, f32[1024,256]{1,0:T(8,128)} %get-tuple-element.26._, f32[512,128]{1,0:T(8,128)S(1)} %bitcast.51, f32[256,128]{1,0:T(8,128)S(1)} %copy-done.1), custom_call_target="tpu_custom_call", output_to_operand_aliasing={{0}: (1, {})} | custom-call | tf_op jit(solution)/shard_map/pallas_call | solution.py:271
  57.4 2.4 %shard_map.92 = (f32[1024,256]{1,0:T(8,128)}, f32[2,8,64,128]{3,2,1,0:T(8,128)}) custom-call(s32[1]{0:T(128)S(6)} %sub.9.half_ref, f32[1024,256]{1,0:T(8,128)} %get-tuple-element.40._, f32[512,128]{1,0:T(8,128)S(1)} %collective-permute-done.7.after_ref, f32[256,128]{1,0:T(8,128)S(1)} %copy-done.1, ...), custom_call_target="tpu_custom_call", output_to_operand_aliasing={{0}: (1, {}), {1}: (5, {})} | custom-call | tf_op jit(solution)/shard_map/pallas_call | solution.py:295
  59.9 5.0 %all-to-all-start.3 = ((f32[16,64,128]{2,1,0:T(8,128)}), f32[16,64,128]{2,1,0:T(8,128)S(1)}, u32[]{:S(2)}, u32[]{:S(2)}) async-start(f32[16,64,128]{2,1,0:T(8,128)} %bitcast.11), calls=%async_computation.3 | async-start | bytes 1048576 | tf_op jit(solution)/shard_map/all_to_all | solution.py:389
  65.4 1.5 %collective-permute-done.8.own_other_ref = f32[16,64,128]{2,1,0:T(8,128)S(1)} collective-permute-done((f32[16,64,128]{2,1,0:T(8,128)S(1)}, f32[16,64,128]{2,1,0:T(8,128)S(1)}, u32[]{:S(2)}, u32[]{:S(2)}) %collective-permute-start.8) | collective-permute-done | bytes 524320 | tf_op jit(solution)/shard_map/ppermute | solution.py:29
  66.9 1.5 %collective-permute-start.9 = (f32[16,64,128]{2,1,0:T(8,128)S(1)}, f32[16,64,128]{2,1,0:T(8,128)S(1)}, u32[]{:S(2)}, u32[]{:S(2)}) collective-permute-start(f32[16,64,128]{2,1,0:T(8,128)S(1)} %collective-permute-done.8.own_other_ref), channel_id=1, source_target_pairs={{0,16},{16,0},{1,17},{17,1},{2,18},{18,2},{3,19},{19,3},{4,20},{20... | collective-permute-start | bytes 1572872 | tf_op jit(solution)/shard_map/ppermute | solution.py:29
  68.4 12.3 %all-to-all-done.3.late_ref = f32[16,64,128]{2,1,0:T(8,128)S(1)} async-done(((f32[16,64,128]{2,1,0:T(8,128)}), f32[16,64,128]{2,1,0:T(8,128)S(1)}, u32[]{:S(2)}, u32[]{:S(2)}) %all-to-all-start.3) | async-done | bytes 524320 | tf_op jit(solution)/shard_map/all_to_all | solution.py:389
  80.7 1.6 %collective-permute-start.11 = (f32[2,32,128]{2,1,0:T(8,128)S(1)}, f32[2,32,128]{2,1,0:T(8,128)S(1)}, u32[]{:S(2)}, u32[]{:S(2)}) collective-permute-start(f32[2,32,128]{2,1,0:T(8,128)S(1)} %bitcast_reduce_fusion), channel_id=1, source_target_pairs={{0,16},{16,0},{1,17},{17,1},{2,18},{18,2},{3,19},{19,3},{4,20},{20... | collective-permute-start | bytes 98312 | tf_op jit(solution)/shard_map/ppermute | solution.py:29
  82.3 1.8 %shard_map.93 = (f32[32,128]{1,0:T(8,128)S(1)}, f32[32,128]{1,0:T(8,128)S(1)}) custom-call(s32[2]{0:T(128)S(1)} %pad_add_fusion.place_ref, f32[16,64,128]{2,1,0:T(8,128)S(1)} %all-to-all-done.3.late_ref, f32[16,64,128]{2,1,0:T(8,128)S(1)} %get-tuple-element.49.own_mine_ref, f32[16,64,128]{2,1,0:T(8,128)S(1)} %collective-permute-done.8.own_other_ref, ...), custom_call_target="tpu_custom_call" | custom-call | tf_op jit(solution)/shard_map/pallas_call | solution.py:330
  86.1 4.9 %all-to-all-start.4 = ((f32[16,32,128]{2,1,0:T(8,128)}), f32[16,32,128]{2,1,0:T(8,128)S(1)}, u32[]{:S(2)}, u32[]{:S(2)}) async-start(f32[16,32,128]{2,1,0:T(8,128)} %bitcast.16), calls=%async_computation.4 | async-start | bytes 524288 | tf_op jit(solution)/shard_map/all_to_all | solution.py:403
  92.3 9.1 %all-to-all-done.4 = f32[16,32,128]{2,1,0:T(8,128)S(1)} async-done(((f32[16,32,128]{2,1,0:T(8,128)}), f32[16,32,128]{2,1,0:T(8,128)S(1)}, u32[]{:S(2)}, u32[]{:S(2)}) %all-to-all-start.4) | async-done | bytes 262176 | tf_op jit(solution)/shard_map/all_to_all | solution.py:403
  (55 shorter events, 15.4 us)
Async XLA Ops:
  0.6 3.7 %copy-start.5 = (f32[32,256]{1,0:T(8,128)S(1)}, f32[32,256]{1,0:T(8,128)}, u32[]{:S(2)}) copy-start(f32[32,256]{1,0:T(8,128)} %param.7) | copy-start | bytes 98308
  0.6 6.3 %copy-start.3 = (f32[32,256]{1,0:T(8,128)S(1)}, f32[32,256]{1,0:T(8,128)}, u32[]{:S(2)}) copy-start(f32[32,256]{1,0:T(8,128)} %factor_ref.3) | copy-start | bytes 98308
  3.8 11.2 %copy-start = (f32[128,32,64]{0,2,1:T(8,128)S(1)}, f32[128,32,64]{0,2,1:T(8,128)}, u32[]{:S(2)}) copy-start(f32[128,32,64]{0,2,1:T(8,128)} %param.6) | copy-start | bytes 3145732
  3.8 3.1 %collective-permute-start = (f32[512,128]{1,0:T(8,128)}, f32[512,128]{1,0:T(8,128)S(1)}, u32[]{:S(2)}, u32[]{:S(2)}) collective-permute-start(f32[512,128]{1,0:T(8,128)} %get-tuple-element.28), channel_id=1, source_target_pairs={{0,1},{1,0},{2,3},{3,2},{4,5},{5,4},{6,7},{7,6},{8,9},{9,8},{10,11... | collective-permute-start | bytes 786440 | tf_op jit(solution)/shard_map/ppermute | solution.py:29
  4.3 4.4 %collective-permute-start.1 = (f32[32,128]{1,0:T(8,128)S(1)}, f32[32,128]{1,0:T(8,128)S(1)}, u32[]{:S(2)}, u32[]{:S(2)}) collective-permute-start(f32[32,128]{1,0:T(8,128)S(1)} %get-tuple-element.59), channel_id=1, source_target_pairs={{0,16},{16,0},{1,17},{17,1},{2,18},{18,2},{3,19},{19,3},{4,20},{20... | collective-permute-start | bytes 49160 | tf_op jit(solution)/shard_map/ppermute | solution.py:29
  8.7 18.0 %all-to-all-start = ((f32[8,96,128]{2,1,0:T(8,128)}), f32[8,96,128]{2,1,0:T(8,128)S(1)}, u32[]{:S(2)}, u32[]{:S(2)}) async-start(f32[8,96,128]{2,1,0:T(8,128)} %shard_map.85), calls=%async_computation | async-start | bytes 786432 | tf_op jit(solution)/shard_map/all_to_all | solution.py:366
  16.8 7.8 %collective-permute-start.2 = (f32[32,16,128]{2,1,0:T(8,128)S(1)}, f32[32,16,128]{2,1,0:T(8,128)S(1)}, u32[]{:S(2)}, u32[]{:S(2)}) collective-permute-start(f32[32,16,128]{2,1,0:T(8,128)S(1)} %shard_map.87), channel_id=1, source_target_pairs={{0,16},{16,0},{1,17},{17,1},{2,18},{18,2},{3,19},{19,3},{4,20},{20... | collective-permute-start | bytes 786440 | tf_op jit(solution)/shard_map/ppermute | solution.py:29
  26.7 14.8 %all-to-all-start.1 = ((f32[16,32,128]{2,1,0:T(8,128)}), f32[16,32,128]{2,1,0:T(8,128)S(1)}, u32[]{:S(2)}, u32[]{:S(2)}) async-start(f32[16,32,128]{2,1,0:T(8,128)} %bitcast.4), calls=%async_computation.1 | async-start | bytes 524288 | tf_op jit(solution)/shard_map/all_to_all | solution.py:377
  31.2 2.9 %collective-permute-start.3 = (f32[8,2,16,128]{3,2,1,0:T(8,128)S(1)}, f32[8,2,16,128]{3,2,1,0:T(8,128)S(1)}, u32[]{:S(2)}, u32[]{:S(2)}) collective-permute-start(f32[8,2,16,128]{3,2,1,0:T(8,128)S(1)} %bitcast.52), channel_id=1, source_target_pairs={{0,1},{1,0},{2,3},{3,2},{4,5},{5,4},{6,7},{7,6},{8,9},{9,8},{10,11... | collective-permute-start | bytes 393224 | tf_op jit(solution)/shard_map/ppermute | solution.py:29
  32.5 21.4 %collective-permute-start.6 = (f32[16,64,128]{2,1,0:T(8,128)S(1)}, f32[16,64,128]{2,1,0:T(8,128)S(1)}, u32[]{:S(2)}, u32[]{:S(2)}) collective-permute-start(f32[16,64,128]{2,1,0:T(8,128)S(1)} %get-tuple-element.49.own_mine_ref), channel_id=1, source_target_pairs={{0,16},{16,0},{1,17},{17,1},{2,18},{18,2},{3,19},{19,3},{4,20},{20... | collective-permute-start | bytes 1572872 | tf_op jit(solution)/shard_map/ppermute | solution.py:29
  43.2 3.6 %copy-start.1 = (f32[256,128]{1,0:T(8,128)S(1)}, f32[256,128]{1,0:T(8,128)}, u32[]{:S(2)}) copy-start(f32[256,128]{1,0:T(8,128)} %factor_ref.5) | copy-start | bytes 393220
  43.2 12.1 %all-to-all-start.2 = ((f32[8,2,32,128]{3,2,1,0:T(8,128)}), f32[8,2,32,128]{3,2,1,0:T(8,128)S(1)}, u32[]{:S(2)}, u32[]{:S(2)}) async-start(f32[8,2,32,128]{3,2,1,0:T(8,128)} %get-tuple-element.33.moved_ref), calls=%async_computation.2 | async-start | bytes 524288 | tf_op jit(solution)/shard_map/all_to_all | solution.py:380
  47.2 1.3 %collective-permute-start.4 = (f32[128,128]{1,0:T(8,128)S(1)}, f32[128,128]{1,0:T(8,128)S(1)}, u32[]{:S(2)}, u32[]{:S(2)}) collective-permute-start(f32[128,128]{1,0:T(8,128)S(1)} %fusion.2.gram_ref), channel_id=1, source_target_pairs={{0,1},{1,0},{2,3},{3,2},{4,5},{5,4},{6,7},{7,6},{8,9},{9,8},{10,11... | collective-permute-start | bytes 196616 | tf_op jit(solution)/shard_map/ppermute | solution.py:29
  51.8 1.4 %collective-permute-start.5 = (f32[8,16,256]{2,1,0:T(8,128)S(1)}, f32[8,16,256]{2,1,0:T(8,128)S(1)}, u32[]{:S(2)}, u32[]{:S(2)}) collective-permute-start(f32[8,16,256]{2,1,0:T(8,128)S(1)} %get-tuple-element.38), channel_id=1, source_target_pairs={{0,1},{1,0},{2,3},{3,2},{4,5},{5,4},{6,7},{7,6},{8,9},{9,8},{10,11... | collective-permute-start | bytes 393224 | tf_op jit(solution)/shard_map/ppermute | solution.py:29
  55.3 2.1 %collective-permute-start.7 = (f32[512,128]{1,0:T(8,128)S(1)}, f32[512,128]{1,0:T(8,128)S(1)}, u32[]{:S(2)}, u32[]{:S(2)}) collective-permute-start(f32[512,128]{1,0:T(8,128)S(1)} %bitcast.50), channel_id=1, source_target_pairs={{0,1},{1,0},{2,3},{3,2},{4,5},{5,4},{6,7},{7,6},{8,9},{9,8},{10,11... | collective-permute-start | bytes 786440 | tf_op jit(solution)/shard_map/ppermute | solution.py:29
  59.9 5.0 %copy-start.4 = (f32[16,64,128]{2,1,0:T(8,128)S(1)}, f32[16,64,128]{2,1,0:T(8,128)}, u32[]{:S(2)}) copy-start(f32[16,64,128]{2,1,0:T(8,128)} %get-tuple-element.48) | copy-start | bytes 1572868
  59.9 20.8 %all-to-all-start.3 = ((f32[16,64,128]{2,1,0:T(8,128)}), f32[16,64,128]{2,1,0:T(8,128)S(1)}, u32[]{:S(2)}, u32[]{:S(2)}) async-start(f32[16,64,128]{2,1,0:T(8,128)} %bitcast.11), calls=%async_computation.3 | async-start | bytes 1048576 | tf_op jit(solution)/shard_map/all_to_all | solution.py:389
  64.9 2.0 %collective-permute-start.8 = (f32[16,64,128]{2,1,0:T(8,128)S(1)}, f32[16,64,128]{2,1,0:T(8,128)S(1)}, u32[]{:S(2)}, u32[]{:S(2)}) collective-permute-start(f32[16,64,128]{2,1,0:T(8,128)S(1)} %copy-done.4), channel_id=1, source_target_pairs={{0,1},{1,0},{2,3},{3,2},{4,5},{5,4},{6,7},{7,6},{8,9},{9,8},{10,11... | collective-permute-start | bytes 1572872 | tf_op jit(solution)/shard_map/ppermute | solution.py:29
  66.9 15.4 %collective-permute-start.9 = (f32[16,64,128]{2,1,0:T(8,128)S(1)}, f32[16,64,128]{2,1,0:T(8,128)S(1)}, u32[]{:S(2)}, u32[]{:S(2)}) collective-permute-start(f32[16,64,128]{2,1,0:T(8,128)S(1)} %collective-permute-done.8.own_other_ref), channel_id=1, source_target_pairs={{0,16},{16,0},{1,17},{17,1},{2,18},{18,2},{3,19},{19,3},{4,20},{20... | collective-permute-start | bytes 1572872 | tf_op jit(solution)/shard_map/ppermute | solution.py:29
  80.7 4.6 %collective-permute-start.11 = (f32[2,32,128]{2,1,0:T(8,128)S(1)}, f32[2,32,128]{2,1,0:T(8,128)S(1)}, u32[]{:S(2)}, u32[]{:S(2)}) collective-permute-start(f32[2,32,128]{2,1,0:T(8,128)S(1)} %bitcast_reduce_fusion), channel_id=1, source_target_pairs={{0,16},{16,0},{1,17},{17,1},{2,18},{18,2},{3,19},{19,3},{4,20},{20... | collective-permute-start | bytes 98312 | tf_op jit(solution)/shard_map/ppermute | solution.py:29
  84.1 1.2 %collective-permute-start.10 = (f32[32,128]{1,0:T(8,128)S(1)}, f32[32,128]{1,0:T(8,128)S(1)}, u32[]{:S(2)}, u32[]{:S(2)}) collective-permute-start(f32[32,128]{1,0:T(8,128)S(1)} %get-tuple-element.47), channel_id=1, source_target_pairs={{0,1},{1,0},{2,3},{3,2},{4,5},{5,4},{6,7},{7,6},{8,9},{9,8},{10,11... | collective-permute-start | bytes 49160 | tf_op jit(solution)/shard_map/ppermute | solution.py:29
  86.1 15.3 %all-to-all-start.4 = ((f32[16,32,128]{2,1,0:T(8,128)}), f32[16,32,128]{2,1,0:T(8,128)S(1)}, u32[]{:S(2)}, u32[]{:S(2)}) async-start(f32[16,32,128]{2,1,0:T(8,128)} %bitcast.16), calls=%async_computation.4 | async-start | bytes 524288 | tf_op jit(solution)/shard_map/all_to_all | solution.py:403
  91.0 1.3 %collective-permute-start.13 = (f32[32,128]{1,0:T(8,128)S(1)}, f32[32,128]{1,0:T(8,128)S(1)}, u32[]{:S(2)}, u32[]{:S(2)}) collective-permute-start(f32[32,128]{1,0:T(8,128)S(1)} %bitcast.59), channel_id=1, source_target_pairs={{0,1},{1,0},{2,3},{3,2},{4,5},{5,4},{6,7},{7,6},{8,9},{9,8},{10,11... | collective-permute-start | bytes 49160 | tf_op jit(solution)/shard_map/ppermute | solution.py:29
  101.4 1.4 %collective-permute-start.12 = (f32[16,256]{1,0:T(8,128)S(1)}, f32[16,256]{1,0:T(8,128)S(1)}, u32[]{:S(2)}, u32[]{:S(2)}) collective-permute-start(f32[16,256]{1,0:T(8,128)S(1)} %copy_bitcast_fusion), channel_id=1, source_target_pairs={{0,1},{1,0},{2,3},{3,2},{4,5},{5,4},{6,7},{7,6},{8,9},{9,8},{10,11... | collective-permute-start | bytes 49160 | tf_op jit(solution)/shard_map/ppermute | solution.py:29
  (1 other events, 1.0 us)

commit v5 on v4

--- a/solution.py
+++ b/solution.py
@@ -57,85 +57,16 @@
     return x + swap(x, axis)
 
 
-def fold_tensor(half, tensor, factor_three):
-    rows, k = tensor.shape
-    block, full_t = rows // 2, factor_three.shape[1]
-    pieces = 2
-    cut = block // pieces
-
-    def body(half_ref, tensor_ref, factor_in, keep_ref, send_ref, copy_ref, field_ref, whole_ref, factor_ref, loads_sem, stores_sem, sem):
-        me = half_ref[0]
-        weight = pltpu.make_async_copy(factor_in, factor_ref, sem)
-        weight.start()
-        ats = [pl.ds(n * cut, cut) for n in range(2 * pieces)]
-        loads = [pltpu.make_async_copy(tensor_ref.at[at], field_ref.at[at], loads_sem.at[n]) for n, at in enumerate(ats)]
-        stores = [pltpu.make_async_copy(field_ref.at[at], copy_ref.at[at], stores_sem.at[n]) for n, at in enumerate(ats)]
-        for copy in loads:
-            copy.start()
-        for n in range(2 * pieces):
-            loads[n].wait()
-            stores[n].start()
-        weight.wait()
-        whole_ref[...] = product(field_ref[...], factor_ref[...], ((1,), (0,)))
-        keep_ref[...] = whole_ref[pl.ds(pl.multiple_of(me * block, block), block), :]
-        send_ref[...] = whole_ref[pl.ds(pl.multiple_of((1 - me) * block, block), block), :]
-        for copy in stores:
-            copy.wait()
-
-    dma = pltpu.SemaphoreType.DMA
-    return pl.pallas_call(
-        body,
-        out_shape=[shape(block, full_t), shape(block, full_t), shape(rows, k)],
-        in_specs=[smem, hbm, hbm],
-        out_specs=[vmem, vmem, hbm],
-        scratch_shapes=[
-            pltpu.VMEM((rows, k), f32),
-            pltpu.VMEM((rows, full_t), f32),
-            pltpu.VMEM(factor_three.shape, f32),
-            dma((2 * pieces,)),
-            dma((2 * pieces,)),
-            dma,
-        ],
-        compiler_params=pltpu.CompilerParams(vmem_limit_bytes=63 * 1024 * 1024),
-    )(half, tensor, factor_three)
-
-
-def pack_early(half, keep, arrived, factor_two, ny, nz):
-    j, full_s = factor_two.shape
-    wide = keep.shape[1]
-    edge, half_j = keep.shape[0] // ny, j // nz
-    parts = full_s // wide
-
-    def body(half_ref, keep_ref, arrived_ref, factor_ref, out_ref, rows_ref, sem):
-        at = pl.ds(pl.multiple_of(half_ref[0] * half_j, half_j), half_j)
-        copy = pltpu.make_async_copy(factor_ref.at[at], rows_ref, sem)
-        copy.start()
-        out_ref[:, pl.ds(0, edge)] = (keep_ref[...] + arrived_ref[...]).reshape(ny, edge, wide)
-        copy.wait()
-        for c in range(parts):
-            piece = rows_ref[:, c * wide : (c + 1) * wide]
-            out_ref[:, pl.ds(edge + c * half_j, half_j)] = jnp.broadcast_to(piece[None], (ny, half_j, wide))
-
-    return pl.pallas_call(
-        body,
-        out_shape=shape(ny, edge + parts * half_j, wide),
-        in_specs=[smem, vmem, vmem, hbm],
-        out_specs=vmem,
-        scratch_shapes=[pltpu.VMEM((half_j, full_s), f32), pltpu.SemaphoreType.DMA],
-        compiler_params=params,
-    )(half, keep, arrived, factor_two)
-
-
 def mode_one(rows, core):
     a, s, t = rows.shape[0], core.shape[0], core.shape[1]
     halves = 128 // t
     q = s // halves
 
     def body(rows_ref, core_ref, out_ref):
-        left = rows_ref[...]
+        right = jnp.concatenate([core_ref[h * q + n] for n in range(q) for h in range(halves)], axis=0)
+        both = product(rows_ref[...], right, ((1,), (1,)))
         for n in range(q):
-            right = jnp.concatenate([core_ref[h * q + n] for h in range(halves)], axis=0)
-            out_ref[:, n, :] = product(left, right, ((1,), (1,)))
+            out_ref[:, n, :] = both[:, n * halves * t : (n + 1) * halves * t]
 
     return pl.pallas_call(
         body,
@@ -246,27 +177,34 @@
 def fit(half, field, after, factor_three, before=None):
     rows, k = field.shape
     block, full_t = after.shape
+    pieces = 1
 
     def compute(half_ref, after_ref, factor_ref, residual_ref, field_ref, left_ref, sems):
-        at = pl.ds(pl.multiple_of(half_ref[0] * block, block), block)
-        field = pltpu.make_async_copy(residual_ref.at[at], field_ref, sems.at[0])
-        field.start()
+        cut = block // pieces
+        ats = [pl.ds(pl.multiple_of(half_ref[0] * block + n * cut, cut), cut) for n in range(pieces)]
+        here = [pl.ds(n * cut, cut) for n in range(pieces)]
+        loads = [pltpu.make_async_copy(residual_ref.at[ats[n]], field_ref.at[here[n]], sems.at[n]) for n in range(pieces)]
+        outs = [pltpu.make_async_copy(left_ref.at[here[n]], residual_ref.at[ats[n]], sems.at[pieces + n]) for n in range(pieces)]
+        for copy in loads:
+            copy.start()
         after = after_ref[...]
         left = product(after, factor_ref[...].T, ((1,), (0,)))
-        field.wait()
+        for copy in loads:
+            copy.wait()
         left = left - field_ref[...]
         left_ref[...] = left
-        out = pltpu.make_async_copy(left_ref, residual_ref.at[at], sems.at[1])
-        out.start()
-        return product(after, left, ((0,), (0,))), out
-
-    scratch = [pltpu.VMEM((block, k), f32), pltpu.VMEM((block, k), f32), pltpu.SemaphoreType.DMA((3,))]
+        for copy in outs:
+            copy.start()
+        return product(after, left, ((0,), (0,))), outs
+
+    scratch = [pltpu.VMEM((block, k), f32), pltpu.VMEM((block, k), f32), pltpu.SemaphoreType.DMA((2 * pieces + 1,))]
     if before is None:
 
         def body(half_ref, _, after_ref, factor_ref, residual_ref, term_ref, field_ref, left_ref, sems):
-            term, out = compute(half_ref, after_ref, factor_ref, residual_ref, field_ref, left_ref, sems)
+            term, outs = compute(half_ref, after_ref, factor_ref, residual_ref, field_ref, left_ref, sems)
             term_ref[...] = term
-            out.wait()
+            for copy in outs:
+                copy.wait()
 
         return pl.pallas_call(
             body,
@@ -282,15 +220,16 @@
     nz, ny, length, _ = late.shape
     cut = k // (ny * nz)
 
-    def body(half_ref, _, after_ref, factor_ref, term_ref, __, residual_ref, late_ref, field_ref, left_ref, sems, pieces_ref):
-        term, out = compute(half_ref, after_ref, factor_ref, residual_ref, field_ref, left_ref, sems)
-        pieces = (term + term_ref[...]).T.reshape(ny, nz, cut, full_t)
+    def body(half_ref, _, after_ref, factor_ref, term_ref, __, residual_ref, late_ref, field_ref, left_ref, sems, parted_ref):
+        term, outs = compute(half_ref, after_ref, factor_ref, residual_ref, field_ref, left_ref, sems)
+        parted = (term + term_ref[...]).T.reshape(ny, nz, cut, full_t)
         for z in range(nz):
-            pieces_ref[z] = pieces[:, z]
-        copy = pltpu.make_async_copy(pieces_ref, late_ref.at[:, :, pl.ds(length - cut, cut)], sems.at[2])
-        copy.start()
-        copy.wait()
-        out.wait()
+            parted_ref[z] = parted[:, z]
+        message = pltpu.make_async_copy(parted_ref, late_ref.at[:, :, pl.ds(length - cut, cut)], sems.at[2 * pieces])
+        message.start()
+        for copy in outs:
+            copy.wait()
+        message.wait()
 
     return pl.pallas_call(
         body,
@@ -351,8 +290,15 @@
         other_one = swap(lax.dynamic_slice_in_dim(factor_one, (1 - gx) * r, r, axis=1), "gx")
 
     half = place[:1]
-    keep, send, field = fold_tensor(half, tensor.reshape(rows, k), factor_three)
-    early = pack_early(half, keep, swap(send, "gz"), factor_two, ny, nz)
+    field = tensor.reshape(rows, k)
+    halves = tensor.reshape(nz, rows // nz, k)
+    folded = swap(dot("ac,ct->at", part(halves, 1 - gz), factor_three), "gz")
+    folded = folded + dot("ac,ct->at", part(halves, gz), factor_three)
+    mine_two = part(factor_two.reshape(nz, half_j, full_s), gz)
+    mine_two = jnp.concatenate([mine_two[:, c * full_t : (c + 1) * full_t] for c in range(full_s // full_t)], axis=0)
+    early = jnp.concatenate(
+        [folded.reshape(ny, e * j, full_t), jnp.broadcast_to(mine_two[None], (ny,) + mine_two.shape)], axis=1
+    )
     if nx == 2:
         mine_one = lax.dynamic_slice_in_dim(factor_one, gx * r, r, axis=1)
         early, other_one = lax.optimization_barrier((early, other_one))

time: 104 us -> 102 us (0.981)
  Pallas kernels: 19.4 us -> 14.3 us
  matrix products: 0.39 us -> 1.55 us
  waiting for transfers between devices: 42.1 us -> 43.2 us
    pallas_call x2 -> x0, Pallas kernels: 3.94 us -> none  [the longest x1 3.15 us: fold_tensor(): pl.pallas_call(body, out_shape=[shape(block, full_t), shape(block, full_t...]
    pallas_call x2, Pallas kernels: 3.51 us -> 2.3 us  [mode_one(): pl.pallas_call(body, out_shape=shape(a, q, halves * t), in_specs=[vmem, v...]
    dot_general x1 -> x3, matrix products: 0.39 us -> 1.55 us  [dot(): return jnp.einsum(spec, left, right, precision=highest)]
  transfers between devices with their start and end apart: 19 -> 19, of which waited for: 11 -> 12; matrix products, arithmetic and copies ran while one was open for 3% -> 5% of each run, Pallas kernels for 13% -> 12%
where the time goes in v5:
time: 102 us; the launch traced here: 101 us
  waiting for transfers between devices  43.2 us (42%)
  starting transfers between devices  34.4 us (34%)
  Pallas kernels  14.3 us (14%)
  local copies, waits for them, and re-layouts  3.61 us (4%)
  other arithmetic  2.88 us (3%)
  matrix products  1.55 us (2%)
    all_to_all x1, waiting for transfers between devices, local(): lax.all_to_all(late.reshape((nz * ny,) + late.shape[2:]), ('gz', 'gy'), 0...  12.3 us
    ppermute x14, waiting for transfers between devices, swap(): return lax.ppermute(x, axis, [(0, 1), (1, 0)])  10.9 us
    ppermute x14, starting transfers between devices, swap(): return lax.ppermute(x, axis, [(0, 1), (1, 0)])  10.9 us
    all_to_all x1, waiting for transfers between devices, local(): lax.all_to_all(last.reshape((nz * ny,) + last.shape[2:]), ('gz', 'gy'), 0...  9.11 us
    all_to_all x1, waiting for transfers between devices, local(): lax.all_to_all(after_one.reshape(nz * ny, e * q, full_t), ('gz', 'gy'), 0...  7.46 us
    all_to_all x1, starting transfers between devices, local(): early = lax.all_to_all(early, 'gy', 0, 0, tiled=True)  6.37 us
    all_to_all x1, starting transfers between devices, local(): lax.all_to_all(last.reshape((nz * ny,) + last.shape[2:]), ('gz', 'gy'), 0...  4.97 us
    all_to_all x1, starting transfers between devices, local(): lax.all_to_all(late.reshape((nz * ny,) + late.shape[2:]), ('gz', 'gy'), 0...  4.97 us
  transfers between devices with their start and end apart: 19, of which 12 were waited for; matrix products, arithmetic and copies ran while one was open for 5% of the time, Pallas kernels for 12%

profile of v5, /device:TPU:0, one launch (start us, length us, event | category | flops | bytes accessed | tf_op | source)
XLA Modules:
  0.0 100.9 jit_solution(10346114522867173911)
XLA Ops:
  0.7 1.3 %copy.28 = f32[32,32,256]{2,1,0:T(8,128)S(1)} copy(f32[32,32,256]{2,1,0:T(8,128)} %param.5) | data formatting | bytes 2097152
  3.0 2.6 %collective-permute-start.1 = (f32[32,128]{1,0:T(8,128)S(1)}, f32[32,128]{1,0:T(8,128)S(1)}, u32[]{:S(2)}, u32[]{:S(2)}) collective-permute-start(f32[32,128]{1,0:T(8,128)S(1)} %get-tuple-element.53), channel_id=1, source_target_pairs={{0,16},{16,0},{1,17},{17,1},{2,18},{18,2},{3,19},{19,3},{4,20},{20... | collective-permute-start | bytes 49160 | tf_op jit(solution)/shard_map/ppermute | solution.py:29
  7.3 6.4 %all-to-all-start = ((f32[8,96,128]{2,1,0:T(8,128)}), f32[8,96,128]{2,1,0:T(8,128)S(1)}, u32[]{:S(2)}, u32[]{:S(2)}) async-start(f32[8,96,128]{2,1,0:T(8,128)} %pad_maximum_fusion), calls=%async_computation | async-start | bytes 786432 | tf_op jit(solution)/shard_map/all_to_all | solution.py:312
  14.9 1.6 %collective-permute-start.2 = (f32[32,16,128]{2,1,0:T(8,128)S(1)}, f32[32,16,128]{2,1,0:T(8,128)S(1)}, u32[]{:S(2)}, u32[]{:S(2)}) collective-permute-start(f32[32,16,128]{2,1,0:T(8,128)S(1)} %shard_map.85), channel_id=1, source_target_pairs={{0,16},{16,0},{1,17},{17,1},{2,18},{18,2},{3,19},{19,3},{4,20},{20... | collective-permute-start | bytes 786440 | tf_op jit(solution)/shard_map/ppermute | solution.py:29
  17.6 4.6 %collective-permute-done.2 = f32[32,16,128]{2,1,0:T(8,128)S(1)} collective-permute-done((f32[32,16,128]{2,1,0:T(8,128)S(1)}, f32[32,16,128]{2,1,0:T(8,128)S(1)}, u32[]{:S(2)}, u32[]{:S(2)}) %collective-permute-start.2) | collective-permute-done | bytes 262176 | tf_op jit(solution)/shard_map/ppermute | solution.py:29
  22.9 2.0 %all-to-all-done.early_ref = f32[8,96,128]{2,1,0:T(8,128)S(1)} async-done(((f32[8,96,128]{2,1,0:T(8,128)}), f32[8,96,128]{2,1,0:T(8,128)S(1)}, u32[]{:S(2)}, u32[]{:S(2)}) %all-to-all-start) | async-done | bytes 393248 | tf_op jit(solution)/shard_map/all_to_all | solution.py:312
  24.9 3.8 %all-to-all-start.1 = ((f32[16,32,128]{2,1,0:T(8,128)}), f32[16,32,128]{2,1,0:T(8,128)S(1)}, u32[]{:S(2)}, u32[]{:S(2)}) async-start(f32[16,32,128]{2,1,0:T(8,128)} %bitcast.10), calls=%async_computation.1 | async-start | bytes 524288 | tf_op jit(solution)/shard_map/all_to_all | solution.py:323
  30.1 1.4 %collective-permute-start.6 = (f32[16,64,128]{2,1,0:T(8,128)S(1)}, f32[16,64,128]{2,1,0:T(8,128)S(1)}, u32[]{:S(2)}, u32[]{:S(2)}) collective-permute-start(f32[16,64,128]{2,1,0:T(8,128)S(1)} %get-tuple-element.43.own_mine_ref), channel_id=1, source_target_pairs={{0,16},{16,0},{1,17},{17,1},{2,18},{18,2},{3,19},{19,3},{4,20},{20... | collective-permute-start | bytes 1572872 | tf_op jit(solution)/shard_map/ppermute | solution.py:29
  31.7 7.5 %all-to-all-done.1 = f32[16,32,128]{2,1,0:T(8,128)S(1)} async-done(((f32[16,32,128]{2,1,0:T(8,128)}), f32[16,32,128]{2,1,0:T(8,128)S(1)}, u32[]{:S(2)}, u32[]{:S(2)}) %all-to-all-start.1) | async-done | bytes 262176 | tf_op jit(solution)/shard_map/all_to_all | solution.py:323
  39.1 1.7 %shard_map.86 = (f32[8,2,16,256]{3,2,1,0:T(8,128)S(1)}, f32[8,2,16,256]{3,2,1,0:T(8,128)S(1)}, f32[8,2,32,128]{3,2,1,0:T(8,128)}) custom-call(s32[2]{0:T(128)S(1)} %pad_add_fusion.place_ref, f32[2,8,32,128]{3,2,1,0:T(8,128)S(1)} %bitcast.63, f32[8,2,16,128]{3,2,1,0:T(8,128)S(1)} %bitcast.67, f32[8,2,16,128]{3,2,1,0:T(8,128)S(1)} %collective-permute-done.3.other_ref), custom_call_target="tpu_custom_call" | custom-call | tf_op jit(solution)/shard_map/pallas_call | solution.py:103
  40.8 3.4 %all-to-all-start.2 = ((f32[8,2,32,128]{3,2,1,0:T(8,128)}), f32[8,2,32,128]{3,2,1,0:T(8,128)S(1)}, u32[]{:S(2)}, u32[]{:S(2)}) async-start(f32[8,2,32,128]{3,2,1,0:T(8,128)} %get-tuple-element.27.moved_ref), calls=%async_computation.2 | async-start | bytes 524288 | tf_op jit(solution)/shard_map/all_to_all | solution.py:326
  44.7 1.2 %collective-permute-done.4.gram_other_ref = f32[128,128]{1,0:T(8,128)S(1)} collective-permute-done((f32[128,128]{1,0:T(8,128)S(1)}, f32[128,128]{1,0:T(8,128)S(1)}, u32[]{:S(2)}, u32[]{:S(2)}) %collective-permute-start.4) | collective-permute-done | bytes 65568 | tf_op jit(solution)/shard_map/ppermute | solution.py:29
  46.0 3.3 %shard_map.87 = (f32[2,8,64,128]{3,2,1,0:T(8,128)}, f32[8,16,256]{2,1,0:T(8,128)S(1)}, f32[8,16,256]{2,1,0:T(8,128)S(1)}) custom-call(s32[2]{0:T(128)S(1)} %pad_add_fusion.place_ref, f32[8,2,32,128]{3,2,1,0:T(8,128)} %get-tuple-element.27.moved_ref, f32[128,128]{1,0:T(8,128)S(1)} %fusion.10.gram_ref, f32[128,128]{1,0:T(8,128)S(1)} %collective-permute-done.4.gram_other_ref, ...), custom_call_target="tpu_custom_call" | custom-call | flops 1000000000 | bytes 2097152 | tf_op jit(solution)/shard_map/pallas_call | solution.py:139
  51.4 1.4 %all-to-all-done.2 = f32[8,2,32,128]{3,2,1,0:T(8,128)S(1)} async-done(((f32[8,2,32,128]{3,2,1,0:T(8,128)}), f32[8,2,32,128]{3,2,1,0:T(8,128)S(1)}, u32[]{:S(2)}, u32[]{:S(2)}) %all-to-all-start.2) | async-done | bytes 262176 | tf_op jit(solution)/shard_map/all_to_all | solution.py:326
  52.8 2.1 %shard_map.89 = (f32[1024,256]{1,0:T(8,128)}, f32[128,256]{1,0:T(8,128)S(1)}) custom-call(s32[1]{0:T(128)} %bitcast.half_ref, f32[1024,256]{1,0:T(8,128)} %bitcast.70, f32[512,128]{1,0:T(8,128)S(1)} %bitcast.65, f32[256,128]{1,0:T(8,128)S(1)} %copy-done.2), custom_call_target="tpu_custom_call", output_to_operand_aliasing={{0}: (1, {})} | custom-call | tf_op jit(solution)/shard_map/pallas_call | solution.py:209
  54.9 2.4 %shard_map.90 = (f32[1024,256]{1,0:T(8,128)}, f32[2,8,64,128]{3,2,1,0:T(8,128)}) custom-call(s32[1]{0:T(128)S(6)} %sub.10.half_ref, f32[1024,256]{1,0:T(8,128)} %get-tuple-element.34._, f32[512,128]{1,0:T(8,128)S(1)} %collective-permute-done.7.after_ref, f32[256,128]{1,0:T(8,128)S(1)} %copy-done.2, ...), custom_call_target="tpu_custom_call", output_to_operand_aliasing={{0}: (1, {}), {1}: (5, {})} | custom-call | tf_op jit(solution)/shard_map/pallas_call | solution.py:234
  57.4 5.0 %all-to-all-start.3 = ((f32[16,64,128]{2,1,0:T(8,128)}), f32[16,64,128]{2,1,0:T(8,128)S(1)}, u32[]{:S(2)}, u32[]{:S(2)}) async-start(f32[16,64,128]{2,1,0:T(8,128)} %bitcast.17), calls=%async_computation.3 | async-start | bytes 1048576 | tf_op jit(solution)/shard_map/all_to_all | solution.py:335
  62.8 1.5 %collective-permute-done.8.own_other_ref = f32[16,64,128]{2,1,0:T(8,128)S(1)} collective-permute-done((f32[16,64,128]{2,1,0:T(8,128)S(1)}, f32[16,64,128]{2,1,0:T(8,128)S(1)}, u32[]{:S(2)}, u32[]{:S(2)}) %collective-permute-start.8) | collective-permute-done | bytes 524320 | tf_op jit(solution)/shard_map/ppermute | solution.py:29
  64.4 1.5 %collective-permute-start.9 = (f32[16,64,128]{2,1,0:T(8,128)S(1)}, f32[16,64,128]{2,1,0:T(8,128)S(1)}, u32[]{:S(2)}, u32[]{:S(2)}) collective-permute-start(f32[16,64,128]{2,1,0:T(8,128)S(1)} %collective-permute-done.8.own_other_ref), channel_id=1, source_target_pairs={{0,16},{16,0},{1,17},{17,1},{2,18},{18,2},{3,19},{19,3},{4,20},{20... | collective-permute-start | bytes 1572872 | tf_op jit(solution)/shard_map/ppermute | solution.py:29
  65.8 12.3 %all-to-all-done.3.late_ref = f32[16,64,128]{2,1,0:T(8,128)S(1)} async-done(((f32[16,64,128]{2,1,0:T(8,128)}), f32[16,64,128]{2,1,0:T(8,128)S(1)}, u32[]{:S(2)}, u32[]{:S(2)}) %all-to-all-start.3) | async-done | bytes 524320 | tf_op jit(solution)/shard_map/all_to_all | solution.py:335
  78.2 1.5 %collective-permute-start.11 = (f32[2,32,128]{2,1,0:T(8,128)S(1)}, f32[2,32,128]{2,1,0:T(8,128)S(1)}, u32[]{:S(2)}, u32[]{:S(2)}) collective-permute-start(f32[2,32,128]{2,1,0:T(8,128)S(1)} %bitcast_reduce_fusion), channel_id=1, source_target_pairs={{0,16},{16,0},{1,17},{17,1},{2,18},{18,2},{3,19},{19,3},{4,20},{20... | collective-permute-start | bytes 98312 | tf_op jit(solution)/shard_map/ppermute | solution.py:29
  79.7 1.8 %shard_map.91 = (f32[32,128]{1,0:T(8,128)S(1)}, f32[32,128]{1,0:T(8,128)S(1)}) custom-call(s32[2]{0:T(128)S(1)} %pad_add_fusion.place_ref, f32[16,64,128]{2,1,0:T(8,128)S(1)} %all-to-all-done.3.late_ref, f32[16,64,128]{2,1,0:T(8,128)S(1)} %get-tuple-element.43.own_mine_ref, f32[16,64,128]{2,1,0:T(8,128)S(1)} %collective-permute-done.8.own_other_ref, ...), custom_call_target="tpu_custom_call" | custom-call | tf_op jit(solution)/shard_map/pallas_call | solution.py:269
  83.5 5.0 %all-to-all-start.4 = ((f32[16,32,128]{2,1,0:T(8,128)}), f32[16,32,128]{2,1,0:T(8,128)S(1)}, u32[]{:S(2)}, u32[]{:S(2)}) async-start(f32[16,32,128]{2,1,0:T(8,128)} %bitcast.22), calls=%async_computation.4 | async-start | bytes 524288 | tf_op jit(solution)/shard_map/all_to_all | solution.py:349
  89.8 9.1 %all-to-all-done.4 = f32[16,32,128]{2,1,0:T(8,128)S(1)} async-done(((f32[16,32,128]{2,1,0:T(8,128)}), f32[16,32,128]{2,1,0:T(8,128)S(1)}, u32[]{:S(2)}, u32[]{:S(2)}) %all-to-all-start.4) | async-done | bytes 262176 | tf_op jit(solution)/shard_map/all_to_all | solution.py:349
  (61 shorter events, 15.6 us)
Async XLA Ops:
  0.6 5.0 %copy-start = (f32[32,256]{1,0:T(8,128)S(1)}, f32[32,256]{1,0:T(8,128)}, u32[]{:S(2)}) copy-start(f32[32,256]{1,0:T(8,128)} %param.8) | copy-start | bytes 98308
  0.6 1.3 %copy-start.2 = (f32[256,128]{1,0:T(8,128)S(1)}, f32[256,128]{1,0:T(8,128)}, u32[]{:S(2)}) copy-start(f32[256,128]{1,0:T(8,128)} %factor_ref.3) | copy-start | bytes 393220
  1.9 3.7 %copy-start.3 = (f32[32,32,256]{2,1,0:T(8,128)}, f32[32,32,256]{2,1,0:T(8,128)S(1)}, u32[]{:S(2)}) copy-start(f32[32,32,256]{2,1,0:T(8,128)S(1)} %copy.28) | copy-start | bytes 3145732
  2.5 3.1 %collective-permute-start = (f32[512,128]{1,0:T(8,128)S(1)}, f32[512,128]{1,0:T(8,128)S(1)}, u32[]{:S(2)}, u32[]{:S(2)}) collective-permute-start(f32[512,128]{1,0:T(8,128)S(1)} %fusion.1), channel_id=1, source_target_pairs={{0,1},{1,0},{2,3},{3,2},{4,5},{5,4},{6,7},{7,6},{8,9},{9,8},{10,11... | collective-permute-start | bytes 786440 | tf_op jit(solution)/shard_map/ppermute | solution.py:29
  3.0 4.3 %collective-permute-start.1 = (f32[32,128]{1,0:T(8,128)S(1)}, f32[32,128]{1,0:T(8,128)S(1)}, u32[]{:S(2)}, u32[]{:S(2)}) collective-permute-start(f32[32,128]{1,0:T(8,128)S(1)} %get-tuple-element.53), channel_id=1, source_target_pairs={{0,16},{16,0},{1,17},{17,1},{2,18},{18,2},{3,19},{19,3},{4,20},{20... | collective-permute-start | bytes 49160 | tf_op jit(solution)/shard_map/ppermute | solution.py:29
  6.3 7.5 %copy-start.1 = (f32[128,32,64]{0,2,1:T(8,128)S(1)}, f32[128,32,64]{0,2,1:T(8,128)}, u32[]{:S(2)}) copy-start(f32[128,32,64]{0,2,1:T(8,128)} %param.6) | copy-start | bytes 3145732
  7.3 17.6 %all-to-all-start = ((f32[8,96,128]{2,1,0:T(8,128)}), f32[8,96,128]{2,1,0:T(8,128)S(1)}, u32[]{:S(2)}, u32[]{:S(2)}) async-start(f32[8,96,128]{2,1,0:T(8,128)} %pad_maximum_fusion), calls=%async_computation | async-start | bytes 786432 | tf_op jit(solution)/shard_map/all_to_all | solution.py:312
  14.9 7.3 %collective-permute-start.2 = (f32[32,16,128]{2,1,0:T(8,128)S(1)}, f32[32,16,128]{2,1,0:T(8,128)S(1)}, u32[]{:S(2)}, u32[]{:S(2)}) collective-permute-start(f32[32,16,128]{2,1,0:T(8,128)S(1)} %shard_map.85), channel_id=1, source_target_pairs={{0,16},{16,0},{1,17},{17,1},{2,18},{18,2},{3,19},{19,3},{4,20},{20... | collective-permute-start | bytes 786440 | tf_op jit(solution)/shard_map/ppermute | solution.py:29
  24.9 14.2 %all-to-all-start.1 = ((f32[16,32,128]{2,1,0:T(8,128)}), f32[16,32,128]{2,1,0:T(8,128)S(1)}, u32[]{:S(2)}, u32[]{:S(2)}) async-start(f32[16,32,128]{2,1,0:T(8,128)} %bitcast.10), calls=%async_computation.1 | async-start | bytes 524288 | tf_op jit(solution)/shard_map/all_to_all | solution.py:323
  28.8 2.9 %collective-permute-start.3 = (f32[8,2,16,128]{3,2,1,0:T(8,128)S(1)}, f32[8,2,16,128]{3,2,1,0:T(8,128)S(1)}, u32[]{:S(2)}, u32[]{:S(2)}) collective-permute-start(f32[8,2,16,128]{3,2,1,0:T(8,128)S(1)} %bitcast.66), channel_id=1, source_target_pairs={{0,1},{1,0},{2,3},{3,2},{4,5},{5,4},{6,7},{7,6},{8,9},{9,8},{10,11... | collective-permute-start | bytes 393224 | tf_op jit(solution)/shard_map/ppermute | solution.py:29
  30.1 21.2 %collective-permute-start.6 = (f32[16,64,128]{2,1,0:T(8,128)S(1)}, f32[16,64,128]{2,1,0:T(8,128)S(1)}, u32[]{:S(2)}, u32[]{:S(2)}) collective-permute-start(f32[16,64,128]{2,1,0:T(8,128)S(1)} %get-tuple-element.43.own_mine_ref), channel_id=1, source_target_pairs={{0,16},{16,0},{1,17},{17,1},{2,18},{18,2},{3,19},{19,3},{4,20},{20... | collective-permute-start | bytes 1572872 | tf_op jit(solution)/shard_map/ppermute | solution.py:29
  40.8 12.0 %all-to-all-start.2 = ((f32[8,2,32,128]{3,2,1,0:T(8,128)}), f32[8,2,32,128]{3,2,1,0:T(8,128)S(1)}, u32[]{:S(2)}, u32[]{:S(2)}) async-start(f32[8,2,32,128]{3,2,1,0:T(8,128)} %get-tuple-element.27.moved_ref), calls=%async_computation.2 | async-start | bytes 524288 | tf_op jit(solution)/shard_map/all_to_all | solution.py:326
  44.7 1.3 %collective-permute-start.4 = (f32[128,128]{1,0:T(8,128)S(1)}, f32[128,128]{1,0:T(8,128)S(1)}, u32[]{:S(2)}, u32[]{:S(2)}) collective-permute-start(f32[128,128]{1,0:T(8,128)S(1)} %fusion.10.gram_ref), channel_id=1, source_target_pairs={{0,1},{1,0},{2,3},{3,2},{4,5},{5,4},{6,7},{7,6},{8,9},{9,8},{10,11... | collective-permute-start | bytes 196616 | tf_op jit(solution)/shard_map/ppermute | solution.py:29
  49.2 1.4 %collective-permute-start.5 = (f32[8,16,256]{2,1,0:T(8,128)S(1)}, f32[8,16,256]{2,1,0:T(8,128)S(1)}, u32[]{:S(2)}, u32[]{:S(2)}) collective-permute-start(f32[8,16,256]{2,1,0:T(8,128)S(1)} %get-tuple-element.32), channel_id=1, source_target_pairs={{0,1},{1,0},{2,3},{3,2},{4,5},{5,4},{6,7},{7,6},{8,9},{9,8},{10,11... | collective-permute-start | bytes 393224 | tf_op jit(solution)/shard_map/ppermute | solution.py:29
  52.8 2.1 %collective-permute-start.7 = (f32[512,128]{1,0:T(8,128)S(1)}, f32[512,128]{1,0:T(8,128)S(1)}, u32[]{:S(2)}, u32[]{:S(2)}) collective-permute-start(f32[512,128]{1,0:T(8,128)S(1)} %bitcast.64), channel_id=1, source_target_pairs={{0,1},{1,0},{2,3},{3,2},{4,5},{5,4},{6,7},{7,6},{8,9},{9,8},{10,11... | collective-permute-start | bytes 786440 | tf_op jit(solution)/shard_map/ppermute | solution.py:29
  57.4 5.0 %copy-start.4 = (f32[16,64,128]{2,1,0:T(8,128)S(1)}, f32[16,64,128]{2,1,0:T(8,128)}, u32[]{:S(2)}) copy-start(f32[16,64,128]{2,1,0:T(8,128)} %get-tuple-element.42) | copy-start | bytes 1572868
  57.4 20.8 %all-to-all-start.3 = ((f32[16,64,128]{2,1,0:T(8,128)}), f32[16,64,128]{2,1,0:T(8,128)S(1)}, u32[]{:S(2)}, u32[]{:S(2)}) async-start(f32[16,64,128]{2,1,0:T(8,128)} %bitcast.17), calls=%async_computation.3 | async-start | bytes 1048576 | tf_op jit(solution)/shard_map/all_to_all | solution.py:335
  62.4 2.0 %collective-permute-start.8 = (f32[16,64,128]{2,1,0:T(8,128)S(1)}, f32[16,64,128]{2,1,0:T(8,128)S(1)}, u32[]{:S(2)}, u32[]{:S(2)}) collective-permute-start(f32[16,64,128]{2,1,0:T(8,128)S(1)} %copy-done.4), channel_id=1, source_target_pairs={{0,1},{1,0},{2,3},{3,2},{4,5},{5,4},{6,7},{7,6},{8,9},{9,8},{10,11... | collective-permute-start | bytes 1572872 | tf_op jit(solution)/shard_map/ppermute | solution.py:29
  64.4 15.3 %collective-permute-start.9 = (f32[16,64,128]{2,1,0:T(8,128)S(1)}, f32[16,64,128]{2,1,0:T(8,128)S(1)}, u32[]{:S(2)}, u32[]{:S(2)}) collective-permute-start(f32[16,64,128]{2,1,0:T(8,128)S(1)} %collective-permute-done.8.own_other_ref), channel_id=1, source_target_pairs={{0,16},{16,0},{1,17},{17,1},{2,18},{18,2},{3,19},{19,3},{4,20},{20... | collective-permute-start | bytes 1572872 | tf_op jit(solution)/shard_map/ppermute | solution.py:29
  78.2 4.6 %collective-permute-start.11 = (f32[2,32,128]{2,1,0:T(8,128)S(1)}, f32[2,32,128]{2,1,0:T(8,128)S(1)}, u32[]{:S(2)}, u32[]{:S(2)}) collective-permute-start(f32[2,32,128]{2,1,0:T(8,128)S(1)} %bitcast_reduce_fusion), channel_id=1, source_target_pairs={{0,16},{16,0},{1,17},{17,1},{2,18},{18,2},{3,19},{19,3},{4,20},{20... | collective-permute-start | bytes 98312 | tf_op jit(solution)/shard_map/ppermute | solution.py:29
  81.5 1.2 %collective-permute-start.10 = (f32[32,128]{1,0:T(8,128)S(1)}, f32[32,128]{1,0:T(8,128)S(1)}, u32[]{:S(2)}, u32[]{:S(2)}) collective-permute-start(f32[32,128]{1,0:T(8,128)S(1)} %get-tuple-element.41), channel_id=1, source_target_pairs={{0,1},{1,0},{2,3},{3,2},{4,5},{5,4},{6,7},{7,6},{8,9},{9,8},{10,11... | collective-permute-start | bytes 49160 | tf_op jit(solution)/shard_map/ppermute | solution.py:29
  83.5 15.3 %all-to-all-start.4 = ((f32[16,32,128]{2,1,0:T(8,128)}), f32[16,32,128]{2,1,0:T(8,128)S(1)}, u32[]{:S(2)}, u32[]{:S(2)}) async-start(f32[16,32,128]{2,1,0:T(8,128)} %bitcast.22), calls=%async_computation.4 | async-start | bytes 524288 | tf_op jit(solution)/shard_map/all_to_all | solution.py:349
  88.5 1.3 %collective-permute-start.13 = (f32[32,128]{1,0:T(8,128)S(1)}, f32[32,128]{1,0:T(8,128)S(1)}, u32[]{:S(2)}, u32[]{:S(2)}) collective-permute-start(f32[32,128]{1,0:T(8,128)S(1)} %bitcast.76), channel_id=1, source_target_pairs={{0,1},{1,0},{2,3},{3,2},{4,5},{5,4},{6,7},{7,6},{8,9},{9,8},{10,11... | collective-permute-start | bytes 49160 | tf_op jit(solution)/shard_map/ppermute | solution.py:29
  98.9 1.4 %collective-permute-start.12 = (f32[16,256]{1,0:T(8,128)S(1)}, f32[16,256]{1,0:T(8,128)S(1)}, u32[]{:S(2)}, u32[]{:S(2)}) collective-permute-start(f32[16,256]{1,0:T(8,128)S(1)} %copy_bitcast_fusion), channel_id=1, source_target_pairs={{0,1},{1,0},{2,3},{3,2},{4,5},{5,4},{6,7},{7,6},{8,9},{9,8},{10,11... | collective-permute-start | bytes 49160 | tf_op jit(solution)/shard_map/ppermute | solution.py:29
  (1 other events, 1.1 us)

commit v6 on v5

--- a/solution.py
+++ b/solution.py
@@ -344,20 +344,17 @@
         term_one = dot("aqht,xhqtr->axr", share_one.reshape(i, q, nz, t), every_core)
         term_one = lax.psum_scatter(term_one.reshape(i, nz, half_r).transpose(1, 0, 2), "gz", scatter_dimension=0)
 
-    last = jnp.concatenate([term_one.reshape(nz, -1, full_t), share_three], axis=1)
-    last = jnp.broadcast_to(last[:, None], (nz, ny) + last.shape[1:])
-    last = lax.all_to_all(last.reshape((nz * ny,) + last.shape[2:]), ("gz", "gy"), 0, 0, tiled=True)
-    last = last.reshape((nz, ny) + last.shape[1:])
-    cut = (i // nz) * half_r // full_t
-    grad_one = last[:, :, :cut].sum(axis=1).reshape(nz, i // nz, half_r)
-    grad_one = gather(grad_one.transpose(1, 0, 2).reshape(i // nz, full_r), "gz").reshape(i, full_r)
-    grad_three = last[:, :, cut:].transpose(1, 0, 2, 3).reshape(k, full_t)
+    last = jnp.concatenate([term_one.reshape(-1, full_t), share_three.reshape(-1, full_t)], axis=0)
+    last = lax.all_to_all(jnp.broadcast_to(last[None], (ny,) + last.shape), "gy", 0, 0, tiled=True)
     share_two = gather(share_two.reshape(j, full_s // nz), "gz")
-    grad_two = jnp.concatenate([share_two[z] for z in range(nz)], axis=1)
-
-    grad_one = grad_one / jnp.sqrt(f32(j * ny * k * nz))
-    grad_two = grad_two / jnp.sqrt(f32(i * nx * k * nz))
-    grad_three = grad_three / jnp.sqrt(f32(i * nx * j * ny))
+    grad_two = jnp.concatenate([share_two[z] for z in range(nz)], axis=1) / jnp.sqrt(f32(i * nx * k * nz))
+    last, grad_two = lax.optimization_barrier((last, grad_two))
+
+    cut = i * half_r // full_t
+    grad_one = gather(last[:, :cut].sum(axis=0).reshape(i, half_r), "gz")
+    grad_one = jnp.concatenate([grad_one[z] for z in range(nz)], axis=1) / jnp.sqrt(f32(j * ny * k * nz))
+    last = last[:, cut:].reshape(ny, nz, -1, full_t).transpose(1, 0, 2, 3)
+    grad_three = trade(last, "gz").transpose(1, 0, 2, 3).reshape(k, full_t) / jnp.sqrt(f32(i * nx * j * ny))
     return (residual.reshape(i, j, k), grad_one, grad_two, grad_three)
 
 

time: 102 us -> 101 us (level)
    all_to_all x1, waiting for transfers between devices: 9.11 us -> 7.43 us  [local(): lax.all_to_all(jnp.broadcast_to(last[None], (ny,) + last.shape), 'gy', 0,...]
    ppermute x14 -> x15, waiting for transfers between devices: 10.9 us -> 11.9 us  [swap(): return lax.ppermute(x, axis, [(0, 1), (1, 0)])]
    ppermute x14 -> x15, starting transfers between devices: 10.9 us -> 10.9 us  [swap(): return lax.ppermute(x, axis, [(0, 1), (1, 0)])]
  transfers between devices with their start and end apart: 19 -> 20, of which waited for: 12 -> 13; matrix products, arithmetic and copies ran while one was open for 5% -> 5% of each run, Pallas kernels for 12% -> 12%
where the time goes in v6:
time: 101 us; the launch traced here: 100 us
  waiting for transfers between devices  42.6 us (42%)
  starting transfers between devices  34.4 us (34%)
  Pallas kernels  14.3 us (14%)
  other arithmetic  3.6 us (4%)
  local copies, waits for them, and re-layouts  2.95 us (3%)
  matrix products  1.55 us (2%)
    all_to_all x1, waiting for transfers between devices, local(): lax.all_to_all(late.reshape((nz * ny,) + late.shape[2:]), ('gz', 'gy'), 0...  12.3 us
    ppermute x15, waiting for transfers between devices, swap(): return lax.ppermute(x, axis, [(0, 1), (1, 0)])  11.9 us
    ppermute x15, starting transfers between devices, swap(): return lax.ppermute(x, axis, [(0, 1), (1, 0)])  10.9 us
    all_to_all x1, waiting for transfers between devices, local(): lax.all_to_all(after_one.reshape(nz * ny, e * q, full_t), ('gz', 'gy'), 0...  7.48 us
    all_to_all x1, waiting for transfers between devices, local(): lax.all_to_all(jnp.broadcast_to(last[None], (ny,) + last.shape), 'gy', 0,...  7.43 us
    all_to_all x1, starting transfers between devices, local(): early = lax.all_to_all(early, 'gy', 0, 0, tiled=True)  6.37 us
    all_to_all x1, starting transfers between devices, local(): lax.all_to_all(late.reshape((nz * ny,) + late.shape[2:]), ('gz', 'gy'), 0...  4.97 us
    all_to_all x1, starting transfers between devices, local(): lax.all_to_all(jnp.broadcast_to(last[None], (ny,) + last.shape), 'gy', 0,...  4.89 us
  transfers between devices with their start and end apart: 20, of which 13 were waited for; matrix products, arithmetic and copies ran while one was open for 5% of the time, Pallas kernels for 12%

profile of v6, /device:TPU:0, one launch (start us, length us, event | category | flops | bytes accessed | tf_op | source)
XLA Modules:
  0.0 100.2 jit_solution(3979954156644495977)
XLA Ops:
  0.7 1.3 %copy.20 = f32[32,32,256]{2,1,0:T(8,128)S(1)} copy(f32[32,32,256]{2,1,0:T(8,128)} %param.5) | data formatting | bytes 2097152
  3.0 2.6 %collective-permute-start.1 = (f32[32,128]{1,0:T(8,128)S(1)}, f32[32,128]{1,0:T(8,128)S(1)}, u32[]{:S(2)}, u32[]{:S(2)}) collective-permute-start(f32[32,128]{1,0:T(8,128)S(1)} %get-tuple-element.59), channel_id=1, source_target_pairs={{0,16},{16,0},{1,17},{17,1},{2,18},{18,2},{3,19},{19,3},{4,20},{20... | collective-permute-start | bytes 49160 | tf_op jit(solution)/shard_map/ppermute | solution.py:29
  7.3 6.4 %all-to-all-start = ((f32[8,96,128]{2,1,0:T(8,128)}), f32[8,96,128]{2,1,0:T(8,128)S(1)}, u32[]{:S(2)}, u32[]{:S(2)}) async-start(f32[8,96,128]{2,1,0:T(8,128)} %pad_maximum_fusion), calls=%async_computation | async-start | bytes 786432 | tf_op jit(solution)/shard_map/all_to_all | solution.py:312
  14.9 1.6 %collective-permute-start.2 = (f32[32,16,128]{2,1,0:T(8,128)S(1)}, f32[32,16,128]{2,1,0:T(8,128)S(1)}, u32[]{:S(2)}, u32[]{:S(2)}) collective-permute-start(f32[32,16,128]{2,1,0:T(8,128)S(1)} %shard_map.85), channel_id=1, source_target_pairs={{0,16},{16,0},{1,17},{17,1},{2,18},{18,2},{3,19},{19,3},{4,20},{20... | collective-permute-start | bytes 786440 | tf_op jit(solution)/shard_map/ppermute | solution.py:29
  17.6 4.6 %collective-permute-done.2 = f32[32,16,128]{2,1,0:T(8,128)S(1)} collective-permute-done((f32[32,16,128]{2,1,0:T(8,128)S(1)}, f32[32,16,128]{2,1,0:T(8,128)S(1)}, u32[]{:S(2)}, u32[]{:S(2)}) %collective-permute-start.2) | collective-permute-done | bytes 262176 | tf_op jit(solution)/shard_map/ppermute | solution.py:29
  23.0 2.0 %all-to-all-done.early_ref = f32[8,96,128]{2,1,0:T(8,128)S(1)} async-done(((f32[8,96,128]{2,1,0:T(8,128)}), f32[8,96,128]{2,1,0:T(8,128)S(1)}, u32[]{:S(2)}, u32[]{:S(2)}) %all-to-all-start) | async-done | bytes 393248 | tf_op jit(solution)/shard_map/all_to_all | solution.py:312
  24.9 3.8 %all-to-all-start.1 = ((f32[16,32,128]{2,1,0:T(8,128)}), f32[16,32,128]{2,1,0:T(8,128)S(1)}, u32[]{:S(2)}, u32[]{:S(2)}) async-start(f32[16,32,128]{2,1,0:T(8,128)} %bitcast.10), calls=%async_computation.1 | async-start | bytes 524288 | tf_op jit(solution)/shard_map/all_to_all | solution.py:323
  30.2 1.4 %collective-permute-start.6 = (f32[16,64,128]{2,1,0:T(8,128)S(1)}, f32[16,64,128]{2,1,0:T(8,128)S(1)}, u32[]{:S(2)}, u32[]{:S(2)}) collective-permute-start(f32[16,64,128]{2,1,0:T(8,128)S(1)} %get-tuple-element.47.own_mine_ref), channel_id=1, source_target_pairs={{0,16},{16,0},{1,17},{17,1},{2,18},{18,2},{3,19},{19,3},{4,20},{20... | collective-permute-start | bytes 1572872 | tf_op jit(solution)/shard_map/ppermute | solution.py:29
  31.7 7.5 %all-to-all-done.1 = f32[16,32,128]{2,1,0:T(8,128)S(1)} async-done(((f32[16,32,128]{2,1,0:T(8,128)}), f32[16,32,128]{2,1,0:T(8,128)S(1)}, u32[]{:S(2)}, u32[]{:S(2)}) %all-to-all-start.1) | async-done | bytes 262176 | tf_op jit(solution)/shard_map/all_to_all | solution.py:323
  39.2 1.7 %shard_map.86 = (f32[8,2,16,256]{3,2,1,0:T(8,128)S(1)}, f32[8,2,16,256]{3,2,1,0:T(8,128)S(1)}, f32[8,2,32,128]{3,2,1,0:T(8,128)}) custom-call(s32[2]{0:T(128)S(1)} %pad_add_fusion.place_ref, f32[2,8,32,128]{3,2,1,0:T(8,128)S(1)} %bitcast.60, f32[8,2,16,128]{3,2,1,0:T(8,128)S(1)} %bitcast.64, f32[8,2,16,128]{3,2,1,0:T(8,128)S(1)} %collective-permute-done.3.other_ref), custom_call_target="tpu_custom_call" | custom-call | tf_op jit(solution)/shard_map/pallas_call | solution.py:103
  40.9 3.4 %all-to-all-start.2 = ((f32[8,2,32,128]{3,2,1,0:T(8,128)}), f32[8,2,32,128]{3,2,1,0:T(8,128)S(1)}, u32[]{:S(2)}, u32[]{:S(2)}) async-start(f32[8,2,32,128]{3,2,1,0:T(8,128)} %get-tuple-element.29.moved_ref), calls=%async_computation.2 | async-start | bytes 524288 | tf_op jit(solution)/shard_map/all_to_all | solution.py:326
  44.8 1.2 %collective-permute-done.4.gram_other_ref = f32[128,128]{1,0:T(8,128)S(1)} collective-permute-done((f32[128,128]{1,0:T(8,128)S(1)}, f32[128,128]{1,0:T(8,128)S(1)}, u32[]{:S(2)}, u32[]{:S(2)}) %collective-permute-start.4) | collective-permute-done | bytes 65568 | tf_op jit(solution)/shard_map/ppermute | solution.py:29
  46.0 3.2 %shard_map.87 = (f32[2,8,64,128]{3,2,1,0:T(8,128)}, f32[8,16,256]{2,1,0:T(8,128)S(1)}, f32[8,16,256]{2,1,0:T(8,128)S(1)}) custom-call(s32[2]{0:T(128)S(1)} %pad_add_fusion.place_ref, f32[8,2,32,128]{3,2,1,0:T(8,128)} %get-tuple-element.29.moved_ref, f32[128,128]{1,0:T(8,128)S(1)} %fusion.12.gram_ref, f32[128,128]{1,0:T(8,128)S(1)} %collective-permute-done.4.gram_other_ref, ...), custom_call_target="tpu_custom_call" | custom-call | flops 1000000000 | bytes 2097152 | tf_op jit(solution)/shard_map/pallas_call | solution.py:139
  51.4 1.4 %all-to-all-done.2 = f32[8,2,32,128]{3,2,1,0:T(8,128)S(1)} async-done(((f32[8,2,32,128]{3,2,1,0:T(8,128)}), f32[8,2,32,128]{3,2,1,0:T(8,128)S(1)}, u32[]{:S(2)}, u32[]{:S(2)}) %all-to-all-start.2) | async-done | bytes 262176 | tf_op jit(solution)/shard_map/all_to_all | solution.py:326
  52.8 2.1 %shard_map.89 = (f32[1024,256]{1,0:T(8,128)}, f32[128,256]{1,0:T(8,128)S(1)}) custom-call(s32[1]{0:T(128)} %bitcast.half_ref, f32[1024,256]{1,0:T(8,128)} %bitcast.67, f32[512,128]{1,0:T(8,128)S(1)} %bitcast.62, f32[256,128]{1,0:T(8,128)S(1)} %copy-done.2), custom_call_target="tpu_custom_call", output_to_operand_aliasing={{0}: (1, {})} | custom-call | tf_op jit(solution)/shard_map/pallas_call | solution.py:209
  54.9 2.4 %shard_map.90 = (f32[1024,256]{1,0:T(8,128)}, f32[2,8,64,128]{3,2,1,0:T(8,128)}) custom-call(s32[1]{0:T(128)S(6)} %sub.11.half_ref, f32[1024,256]{1,0:T(8,128)} %get-tuple-element.36._, f32[512,128]{1,0:T(8,128)S(1)} %collective-permute-done.7.after_ref, f32[256,128]{1,0:T(8,128)S(1)} %copy-done.2, ...), custom_call_target="tpu_custom_call", output_to_operand_aliasing={{0}: (1, {}), {1}: (5, {})} | custom-call | tf_op jit(solution)/shard_map/pallas_call | solution.py:234
  57.4 5.0 %all-to-all-start.3 = ((f32[16,64,128]{2,1,0:T(8,128)}), f32[16,64,128]{2,1,0:T(8,128)S(1)}, u32[]{:S(2)}, u32[]{:S(2)}) async-start(f32[16,64,128]{2,1,0:T(8,128)} %bitcast.17), calls=%async_computation.3 | async-start | bytes 1048576 | tf_op jit(solution)/shard_map/all_to_all | solution.py:335
  62.8 1.5 %collective-permute-done.8.own_other_ref = f32[16,64,128]{2,1,0:T(8,128)S(1)} collective-permute-done((f32[16,64,128]{2,1,0:T(8,128)S(1)}, f32[16,64,128]{2,1,0:T(8,128)S(1)}, u32[]{:S(2)}, u32[]{:S(2)}) %collective-permute-start.8) | collective-permute-done | bytes 524320 | tf_op jit(solution)/shard_map/ppermute | solution.py:29
  64.4 1.4 %collective-permute-start.9 = (f32[16,64,128]{2,1,0:T(8,128)S(1)}, f32[16,64,128]{2,1,0:T(8,128)S(1)}, u32[]{:S(2)}, u32[]{:S(2)}) collective-permute-start(f32[16,64,128]{2,1,0:T(8,128)S(1)} %collective-permute-done.8.own_other_ref), channel_id=1, source_target_pairs={{0,16},{16,0},{1,17},{17,1},{2,18},{18,2},{3,19},{19,3},{4,20},{20... | collective-permute-start | bytes 1572872 | tf_op jit(solution)/shard_map/ppermute | solution.py:29
  65.8 12.3 %all-to-all-done.3.late_ref = f32[16,64,128]{2,1,0:T(8,128)S(1)} async-done(((f32[16,64,128]{2,1,0:T(8,128)}), f32[16,64,128]{2,1,0:T(8,128)S(1)}, u32[]{:S(2)}, u32[]{:S(2)}) %all-to-all-start.3) | async-done | bytes 524320 | tf_op jit(solution)/shard_map/all_to_all | solution.py:335
  78.2 1.5 %collective-permute-start.11 = (f32[2,32,128]{2,1,0:T(8,128)S(1)}, f32[2,32,128]{2,1,0:T(8,128)S(1)}, u32[]{:S(2)}, u32[]{:S(2)}) collective-permute-start(f32[2,32,128]{2,1,0:T(8,128)S(1)} %bitcast_reduce_fusion), channel_id=1, source_target_pairs={{0,16},{16,0},{1,17},{17,1},{2,18},{18,2},{3,19},{19,3},{4,20},{20... | collective-permute-start | bytes 98312 | tf_op jit(solution)/shard_map/ppermute | solution.py:29
  79.7 1.8 %shard_map.91 = (f32[32,128]{1,0:T(8,128)S(1)}, f32[32,128]{1,0:T(8,128)S(1)}) custom-call(s32[2]{0:T(128)S(1)} %pad_add_fusion.place_ref, f32[16,64,128]{2,1,0:T(8,128)S(1)} %all-to-all-done.3.late_ref, f32[16,64,128]{2,1,0:T(8,128)S(1)} %get-tuple-element.47.own_mine_ref, f32[16,64,128]{2,1,0:T(8,128)S(1)} %collective-permute-done.8.own_other_ref, ...), custom_call_target="tpu_custom_call" | custom-call | tf_op jit(solution)/shard_map/pallas_call | solution.py:269
  83.5 4.9 %all-to-all-start.4 = ((f32[8,64,128]{2,1,0:T(8,128)}), f32[8,64,128]{2,1,0:T(8,128)S(1)}, u32[]{:S(2)}, u32[]{:S(2)}) async-start(f32[8,64,128]{2,1,0:T(8,128)} %broadcast_in_dim.5), calls=%async_computation.4 | async-start | bytes 524288 | tf_op jit(solution)/shard_map/all_to_all | solution.py:348
  90.2 7.4 %all-to-all-done.4 = f32[8,64,128]{2,1,0:T(8,128)S(1)} async-done(((f32[8,64,128]{2,1,0:T(8,128)}), f32[8,64,128]{2,1,0:T(8,128)S(1)}, u32[]{:S(2)}, u32[]{:S(2)}) %all-to-all-start.4) | async-done | bytes 262176 | tf_op jit(solution)/shard_map/all_to_all | solution.py:348
  (64 shorter events, 16.7 us)
Async XLA Ops:
  0.6 5.0 %copy-start = (f32[32,256]{1,0:T(8,128)S(1)}, f32[32,256]{1,0:T(8,128)}, u32[]{:S(2)}) copy-start(f32[32,256]{1,0:T(8,128)} %param.8) | copy-start | bytes 98308
  1.9 3.7 %copy-start.3 = (f32[32,32,256]{2,1,0:T(8,128)}, f32[32,32,256]{2,1,0:T(8,128)S(1)}, u32[]{:S(2)}) copy-start(f32[32,32,256]{2,1,0:T(8,128)S(1)} %copy.20) | copy-start | bytes 3145732
  2.5 3.1 %collective-permute-start = (f32[512,128]{1,0:T(8,128)S(1)}, f32[512,128]{1,0:T(8,128)S(1)}, u32[]{:S(2)}, u32[]{:S(2)}) collective-permute-start(f32[512,128]{1,0:T(8,128)S(1)} %fusion.1), channel_id=1, source_target_pairs={{0,1},{1,0},{2,3},{3,2},{4,5},{5,4},{6,7},{7,6},{8,9},{9,8},{10,11... | collective-permute-start | bytes 786440 | tf_op jit(solution)/shard_map/ppermute | solution.py:29
  3.0 4.3 %collective-permute-start.1 = (f32[32,128]{1,0:T(8,128)S(1)}, f32[32,128]{1,0:T(8,128)S(1)}, u32[]{:S(2)}, u32[]{:S(2)}) collective-permute-start(f32[32,128]{1,0:T(8,128)S(1)} %get-tuple-element.59), channel_id=1, source_target_pairs={{0,16},{16,0},{1,17},{17,1},{2,18},{18,2},{3,19},{19,3},{4,20},{20... | collective-permute-start | bytes 49160 | tf_op jit(solution)/shard_map/ppermute | solution.py:29
  6.3 7.5 %copy-start.1 = (f32[128,32,64]{0,2,1:T(8,128)S(1)}, f32[128,32,64]{0,2,1:T(8,128)}, u32[]{:S(2)}) copy-start(f32[128,32,64]{0,2,1:T(8,128)} %param.6) | copy-start | bytes 3145732
  7.3 17.6 %all-to-all-start = ((f32[8,96,128]{2,1,0:T(8,128)}), f32[8,96,128]{2,1,0:T(8,128)S(1)}, u32[]{:S(2)}, u32[]{:S(2)}) async-start(f32[8,96,128]{2,1,0:T(8,128)} %pad_maximum_fusion), calls=%async_computation | async-start | bytes 786432 | tf_op jit(solution)/shard_map/all_to_all | solution.py:312
  14.9 7.3 %collective-permute-start.2 = (f32[32,16,128]{2,1,0:T(8,128)S(1)}, f32[32,16,128]{2,1,0:T(8,128)S(1)}, u32[]{:S(2)}, u32[]{:S(2)}) collective-permute-start(f32[32,16,128]{2,1,0:T(8,128)S(1)} %shard_map.85), channel_id=1, source_target_pairs={{0,16},{16,0},{1,17},{17,1},{2,18},{18,2},{3,19},{19,3},{4,20},{20... | collective-permute-start | bytes 786440 | tf_op jit(solution)/shard_map/ppermute | solution.py:29
  24.9 14.2 %all-to-all-start.1 = ((f32[16,32,128]{2,1,0:T(8,128)}), f32[16,32,128]{2,1,0:T(8,128)S(1)}, u32[]{:S(2)}, u32[]{:S(2)}) async-start(f32[16,32,128]{2,1,0:T(8,128)} %bitcast.10), calls=%async_computation.1 | async-start | bytes 524288 | tf_op jit(solution)/shard_map/all_to_all | solution.py:323
  28.8 2.9 %collective-permute-start.3 = (f32[8,2,16,128]{3,2,1,0:T(8,128)S(1)}, f32[8,2,16,128]{3,2,1,0:T(8,128)S(1)}, u32[]{:S(2)}, u32[]{:S(2)}) collective-permute-start(f32[8,2,16,128]{3,2,1,0:T(8,128)S(1)} %bitcast.63), channel_id=1, source_target_pairs={{0,1},{1,0},{2,3},{3,2},{4,5},{5,4},{6,7},{7,6},{8,9},{9,8},{10,11... | collective-permute-start | bytes 393224 | tf_op jit(solution)/shard_map/ppermute | solution.py:29
  30.2 21.2 %collective-permute-start.6 = (f32[16,64,128]{2,1,0:T(8,128)S(1)}, f32[16,64,128]{2,1,0:T(8,128)S(1)}, u32[]{:S(2)}, u32[]{:S(2)}) collective-permute-start(f32[16,64,128]{2,1,0:T(8,128)S(1)} %get-tuple-element.47.own_mine_ref), channel_id=1, source_target_pairs={{0,16},{16,0},{1,17},{17,1},{2,18},{18,2},{3,19},{19,3},{4,20},{20... | collective-permute-start | bytes 1572872 | tf_op jit(solution)/shard_map/ppermute | solution.py:29
  40.9 12.0 %all-to-all-start.2 = ((f32[8,2,32,128]{3,2,1,0:T(8,128)}), f32[8,2,32,128]{3,2,1,0:T(8,128)S(1)}, u32[]{:S(2)}, u32[]{:S(2)}) async-start(f32[8,2,32,128]{3,2,1,0:T(8,128)} %get-tuple-element.29.moved_ref), calls=%async_computation.2 | async-start | bytes 524288 | tf_op jit(solution)/shard_map/all_to_all | solution.py:326
  44.7 1.3 %collective-permute-start.4 = (f32[128,128]{1,0:T(8,128)S(1)}, f32[128,128]{1,0:T(8,128)S(1)}, u32[]{:S(2)}, u32[]{:S(2)}) collective-permute-start(f32[128,128]{1,0:T(8,128)S(1)} %fusion.12.gram_ref), channel_id=1, source_target_pairs={{0,1},{1,0},{2,3},{3,2},{4,5},{5,4},{6,7},{7,6},{8,9},{9,8},{10,11... | collective-permute-start | bytes 196616 | tf_op jit(solution)/shard_map/ppermute | solution.py:29
  49.2 1.4 %collective-permute-start.5 = (f32[8,16,256]{2,1,0:T(8,128)S(1)}, f32[8,16,256]{2,1,0:T(8,128)S(1)}, u32[]{:S(2)}, u32[]{:S(2)}) collective-permute-start(f32[8,16,256]{2,1,0:T(8,128)S(1)} %get-tuple-element.34), channel_id=1, source_target_pairs={{0,1},{1,0},{2,3},{3,2},{4,5},{5,4},{6,7},{7,6},{8,9},{9,8},{10,11... | collective-permute-start | bytes 393224 | tf_op jit(solution)/shard_map/ppermute | solution.py:29
  52.8 2.1 %collective-permute-start.7 = (f32[512,128]{1,0:T(8,128)S(1)}, f32[512,128]{1,0:T(8,128)S(1)}, u32[]{:S(2)}, u32[]{:S(2)}) collective-permute-start(f32[512,128]{1,0:T(8,128)S(1)} %bitcast.61), channel_id=1, source_target_pairs={{0,1},{1,0},{2,3},{3,2},{4,5},{5,4},{6,7},{7,6},{8,9},{9,8},{10,11... | collective-permute-start | bytes 786440 | tf_op jit(solution)/shard_map/ppermute | solution.py:29
  57.4 5.0 %copy-start.4 = (f32[16,64,128]{2,1,0:T(8,128)S(1)}, f32[16,64,128]{2,1,0:T(8,128)}, u32[]{:S(2)}) copy-start(f32[16,64,128]{2,1,0:T(8,128)} %get-tuple-element.46) | copy-start | bytes 1572868
  57.4 20.8 %all-to-all-start.3 = ((f32[16,64,128]{2,1,0:T(8,128)}), f32[16,64,128]{2,1,0:T(8,128)S(1)}, u32[]{:S(2)}, u32[]{:S(2)}) async-start(f32[16,64,128]{2,1,0:T(8,128)} %bitcast.17), calls=%async_computation.3 | async-start | bytes 1048576 | tf_op jit(solution)/shard_map/all_to_all | solution.py:335
  62.4 2.0 %collective-permute-start.8 = (f32[16,64,128]{2,1,0:T(8,128)S(1)}, f32[16,64,128]{2,1,0:T(8,128)S(1)}, u32[]{:S(2)}, u32[]{:S(2)}) collective-permute-start(f32[16,64,128]{2,1,0:T(8,128)S(1)} %copy-done.4), channel_id=1, source_target_pairs={{0,1},{1,0},{2,3},{3,2},{4,5},{5,4},{6,7},{7,6},{8,9},{9,8},{10,11... | collective-permute-start | bytes 1572872 | tf_op jit(solution)/shard_map/ppermute | solution.py:29
  64.4 15.3 %collective-permute-start.9 = (f32[16,64,128]{2,1,0:T(8,128)S(1)}, f32[16,64,128]{2,1,0:T(8,128)S(1)}, u32[]{:S(2)}, u32[]{:S(2)}) collective-permute-start(f32[16,64,128]{2,1,0:T(8,128)S(1)} %collective-permute-done.8.own_other_ref), channel_id=1, source_target_pairs={{0,16},{16,0},{1,17},{17,1},{2,18},{18,2},{3,19},{19,3},{4,20},{20... | collective-permute-start | bytes 1572872 | tf_op jit(solution)/shard_map/ppermute | solution.py:29
  78.2 4.5 %collective-permute-start.11 = (f32[2,32,128]{2,1,0:T(8,128)S(1)}, f32[2,32,128]{2,1,0:T(8,128)S(1)}, u32[]{:S(2)}, u32[]{:S(2)}) collective-permute-start(f32[2,32,128]{2,1,0:T(8,128)S(1)} %bitcast_reduce_fusion), channel_id=1, source_target_pairs={{0,16},{16,0},{1,17},{17,1},{2,18},{18,2},{3,19},{19,3},{4,20},{20... | collective-permute-start | bytes 98312 | tf_op jit(solution)/shard_map/ppermute | solution.py:29
  81.5 1.2 %collective-permute-start.10 = (f32[32,128]{1,0:T(8,128)S(1)}, f32[32,128]{1,0:T(8,128)S(1)}, u32[]{:S(2)}, u32[]{:S(2)}) collective-permute-start(f32[32,128]{1,0:T(8,128)S(1)} %get-tuple-element.43), channel_id=1, source_target_pairs={{0,1},{1,0},{2,3},{3,2},{4,5},{5,4},{6,7},{7,6},{8,9},{9,8},{10,11... | collective-permute-start | bytes 49160 | tf_op jit(solution)/shard_map/ppermute | solution.py:29
  83.5 14.1 %all-to-all-start.4 = ((f32[8,64,128]{2,1,0:T(8,128)}), f32[8,64,128]{2,1,0:T(8,128)S(1)}, u32[]{:S(2)}, u32[]{:S(2)}) async-start(f32[8,64,128]{2,1,0:T(8,128)} %broadcast_in_dim.5), calls=%async_computation.4 | async-start | bytes 524288 | tf_op jit(solution)/shard_map/all_to_all | solution.py:348
  88.4 1.2 %collective-permute-start.12 = (f32[32,128]{1,0:T(8,128)S(1)}, f32[32,128]{1,0:T(8,128)S(1)}, u32[]{:S(2)}, u32[]{:S(2)}) collective-permute-start(f32[32,128]{1,0:T(8,128)S(1)} %bitcast.73), channel_id=1, source_target_pairs={{0,1},{1,0},{2,3},{3,2},{4,5},{5,4},{6,7},{7,6},{8,9},{9,8},{10,11... | collective-permute-start | bytes 49160 | tf_op jit(solution)/shard_map/ppermute | solution.py:29
  97.7 1.2 %collective-permute-start.13 = (f32[32,128]{1,0:T(8,128)S(1)}, f32[32,128]{1,0:T(8,128)S(1)}, u32[]{:S(2)}, u32[]{:S(2)}) collective-permute-start(f32[32,128]{1,0:T(8,128)S(1)} %get-tuple-element.49), channel_id=1, source_target_pairs={{0,1},{1,0},{2,3},{3,2},{4,5},{5,4},{6,7},{7,6},{8,9},{9,8},{10,11... | collective-permute-start | bytes 49160 | tf_op jit(solution)/shard_map/ppermute | solution.py:29
  97.8 1.8 %collective-permute-start.14 = (f32[8,16,128]{2,1,0:T(8,128)S(1)}, f32[8,16,128]{2,1,0:T(8,128)S(1)}, u32[]{:S(2)}, u32[]{:S(2)}) collective-permute-start(f32[8,16,128]{2,1,0:T(8,128)S(1)} %dynamic-slice_bitcast_fusion.2), channel_id=1, source_target_pairs={{0,1},{1,0},{2,3},{3,2},{4,5},{5,4},{6,7},{7,6},{8,9},{9,8},{10,11... | collective-permute-start | bytes 196616 | tf_op jit(solution)/shard_map/ppermute | solution.py:29
  (2 other events, 2.4 us)

commit v7 on v6

--- a/solution.py
+++ b/solution.py
@@ -109,12 +109,13 @@
     )(place, arrived, mine, other)
 
 
-def back(place, moved, gram, gram_other, early, one, two, length):
+def back(place, moved, gram, gram_other, early, one, two):
     ny, e, j, wide = moved.shape
     _, halves, q, _ = one.shape
     _, nz, half_j, full_s = two.shape
-
-    def body(place_ref, moved_ref, gram_ref, gram_other_ref, early_ref, one_ref, two_ref, late_ref, keep_ref, send_ref, sum_ref, wide_ref, sem):
+    edge, parts = e * q, full_s // wide
+
+    def body(place_ref, moved_ref, gram_ref, gram_other_ref, early_ref, one_ref, two_ref, keep_ref, send_ref, sum_ref, wide_ref):
         me = place_ref[0]
         square = gram_ref[...] + gram_other_ref[...]
         whole_two = two_ref[...].reshape(ny * j, full_s)
@@ -130,48 +131,48 @@
             spread = product(whole_two, folded, ((0,), (0,))).reshape(ny, halves, q, wide)
             for h in range(halves):
                 wide_ref[h, :, pl.ds(n * q, q)] = spread[:, h]
-        copy = pltpu.make_async_copy(wide_ref, late_ref.at[:, :, pl.ds(0, e * q)], sem)
-        copy.start()
-        keep_ref[...] = sum_ref[:, pl.ds(me, 1)].reshape(ny, half_j, full_s)
-        send_ref[...] = sum_ref[:, pl.ds(1 - me, 1)].reshape(ny, half_j, full_s)
-        copy.wait()
-
-    return pl.pallas_call(
-        body,
-        out_shape=[shape(halves, ny, length, wide), shape(ny, half_j, full_s), shape(ny, half_j, full_s)],
+        for ref, z in ((keep_ref, me), (send_ref, 1 - me)):
+            ref[:, pl.ds(0, edge)] = wide_ref[pl.ds(z, 1)].reshape(ny, edge, wide)
+            for c in range(parts):
+                piece = sum_ref[:, pl.ds(z, 1), :, pl.ds(c * wide, wide)]
+                ref[:, pl.ds(edge + c * half_j, half_j)] = piece.reshape(ny, half_j, wide)
+
+    return pl.pallas_call(
+        body,
+        out_shape=[shape(ny, edge + parts * half_j, wide)] * 2,
         in_specs=[smem] + [vmem] * 6,
-        out_specs=[hbm, vmem, vmem],
-        scratch_shapes=[
-            pltpu.VMEM((ny, nz, half_j, full_s), f32),
-            pltpu.VMEM((halves, ny, e * q, wide), f32),
-            pltpu.SemaphoreType.DMA,
-        ],
+        out_specs=[vmem] * 2,
+        scratch_shapes=[pltpu.VMEM((ny, nz, half_j, full_s), f32), pltpu.VMEM((halves, ny, edge, wide), f32)],
         compiler_params=params,
         cost_estimate=pl.CostEstimate(flops=10**9, bytes_accessed=2**21, transcendentals=0),
     )(place, moved, gram, gram_other, early, one, two)
 
 
-def put_two(late, keep, arrived, edge):
-    nz, ny, _, wide = late.shape
-    half_j = keep.shape[1]
-
-    def body(_, keep_ref, arrived_ref, late_ref, both_ref, sem):
-        both = keep_ref[...] + arrived_ref[...]
-        for z in range(nz):
-            both_ref[z] = both[:, :, z * wide : (z + 1) * wide]
-        copy = pltpu.make_async_copy(both_ref, late_ref.at[:, :, pl.ds(edge, half_j)], sem)
-        copy.start()
-        copy.wait()
-
-    return pl.pallas_call(
-        body,
-        out_shape=shape(*late.shape),
-        in_specs=[hbm, vmem, vmem],
+def put(keep, arrived, edge, length):
+    ny, rows, wide = keep.shape
+
+    def body(keep_ref, arrived_ref, late_ref, both_ref, sems):
+        copies = [
+            pltpu.make_async_copy(ref.at[:, pl.ds(0, edge)], late_ref.at[:, pl.ds(n * edge, edge)], sems.at[n])
+            for n, ref in enumerate((keep_ref, arrived_ref))
+        ]
+        for copy in copies:
+            copy.start()
+        at = pl.ds(edge, rows - edge)
+        both_ref[...] = keep_ref[:, at] + arrived_ref[:, at]
+        last = pltpu.make_async_copy(both_ref, late_ref.at[:, pl.ds(2 * edge, rows - edge)], sems.at[2])
+        last.start()
+        for copy in copies + [last]:
+            copy.wait()
+
+    return pl.pallas_call(
+        body,
+        out_shape=shape(ny, length, wide),
+        in_specs=[vmem, vmem],
         out_specs=hbm,
-        scratch_shapes=[pltpu.VMEM((nz, ny, half_j, wide), f32), pltpu.SemaphoreType.DMA],
-        input_output_aliases={0: 0},
-        compiler_params=params,
-    )(late, keep, arrived)
+        scratch_shapes=[pltpu.VMEM((ny, rows - edge, wide), f32), pltpu.SemaphoreType.DMA((3,))],
+        compiler_params=params,
+    )(keep, arrived)
 
 
 def fit(half, field, after, factor_three, before=None):
@@ -217,15 +218,13 @@
         )(half, field, after, factor_three)
 
     term, late = before
-    nz, ny, length, _ = late.shape
-    cut = k // (ny * nz)
+    ny, length, _ = late.shape
+    cut = k // ny
 
     def body(half_ref, _, after_ref, factor_ref, term_ref, __, residual_ref, late_ref, field_ref, left_ref, sems, parted_ref):
         term, outs = compute(half_ref, after_ref, factor_ref, residual_ref, field_ref, left_ref, sems)
-        parted = (term + term_ref[...]).T.reshape(ny, nz, cut, full_t)
-        for z in range(nz):
-            parted_ref[z] = parted[:, z]
-        message = pltpu.make_async_copy(parted_ref, late_ref.at[:, :, pl.ds(length - cut, cut)], sems.at[2 * pieces])
+        parted_ref[...] = (term + term_ref[...]).T.reshape(ny, cut, full_t)
+        message = pltpu.make_async_copy(parted_ref, late_ref.at[:, pl.ds(length - cut, cut)], sems.at[2 * pieces])
         message.start()
         for copy in outs:
             copy.wait()
@@ -236,20 +235,22 @@
         out_shape=[shape(rows, k), shape(*late.shape)],
         in_specs=[smem, hbm, vmem, vmem, vmem, hbm],
         out_specs=[hbm, hbm],
-        scratch_shapes=scratch + [pltpu.VMEM((nz, ny, cut, full_t), f32)],
+        scratch_shapes=scratch + [pltpu.VMEM((ny, cut, full_t), f32)],
         input_output_aliases={1: 0, 5: 1},
         compiler_params=params,
     )(half, field, after, factor_three, term, late)
 
 
 def mode_one_term(place, late, own_mine, own_other, near_mine, near_other, e):
-    n, _, wide = late.shape
+    ny, _, wide = late.shape
     q, t, r = own_mine.shape
-    i = n * e
+    edge, half = e * q, ny * e * q
+    i = 2 * ny * e
     group = min(q, 256 // t)
 
     def body(place_ref, late_ref, own_mine_ref, own_other_ref, near_mine_ref, near_other_ref, keep_ref, send_ref, rows_ref):
-        rows_ref[...] = late_ref[:, pl.ds(0, e * q)].reshape(i * q, wide)
+        for n, z in enumerate((place_ref[0], 1 - place_ref[0])):
+            rows_ref[pl.ds(pl.multiple_of(z * half, half), half), :] = late_ref[:, pl.ds(n * edge, edge)].reshape(half, wide)
         first = place_ref[0] == 0
         sum_here = jnp.zeros((i, 2 * r), f32)
         for p in range(0, q, group):
@@ -324,37 +325,35 @@
     after_one = after_one.reshape(nz, ny, e * q, full_t)
     one, two, moved = mode_two(place, after_one, mine_two, other_two, e, t)
     home = lax.all_to_all(moved, "gy", 0, 0, tiled=True).reshape(rows // nz, full_t)
-    late, keep, send = back(place, moved, gram, gram_other, early, one, two, e * q + half_j + k // (ny * nz))
-    late = put_two(late, keep, swap(send, "gz"), e * q)
-
+    edge, parts = e * q, full_s // full_t
+    keep, send = back(place, moved, gram, gram_other, early, one, two)
+    late = put(keep, swap(send, "gz"), edge, 2 * edge + parts * half_j + k // ny)
     if nx == 2:
         home, late, near_mine = lax.optimization_barrier((home, late, near_mine))
-
     field, term_three = fit(half, field, home, factor_three)
     residual, late = fit(1 - half, field, swap(home, "gz"), factor_three, (term_three, late))
-    late = lax.all_to_all(late.reshape((nz * ny,) + late.shape[2:]), ("gz", "gy"), 0, 0, tiled=True)
-    sums = total(late[:, e * q :].reshape(nz, ny, -1, full_t).sum(axis=1), "gx")
-    share_two, share_three = sums[:, :half_j], sums[:, half_j:]
+    late = lax.all_to_all(late, "gy", 0, 0, tiled=True)
+    sums = total(late[:, 2 * edge :].sum(axis=0), "gx")
+    share_two, share_three = sums[: parts * half_j], sums[parts * half_j :]
     if nx == 2:
         keep_one, send_one = mode_one_term(place, late, own_mine, own_other, near_mine, swap(own_other, "gx"), e)
         term_one = keep_one + swap(send_one, "gz")
     else:
-        share_one = late[:, : e * q].reshape(i, q, full_t)
+        share_one = in_order("gz", late[:, :edge], late[:, edge : 2 * edge]).reshape(i, q, full_t)
         every_core = gather(trade(flat, "gz"), "gx")
         term_one = dot("aqht,xhqtr->axr", share_one.reshape(i, q, nz, t), every_core)
         term_one = lax.psum_scatter(term_one.reshape(i, nz, half_r).transpose(1, 0, 2), "gz", scatter_dimension=0)
 
-    last = jnp.concatenate([term_one.reshape(-1, full_t), share_three.reshape(-1, full_t)], axis=0)
+    last = jnp.concatenate([term_one.reshape(-1, full_t), share_three], axis=0)
     last = lax.all_to_all(jnp.broadcast_to(last[None], (ny,) + last.shape), "gy", 0, 0, tiled=True)
-    share_two = gather(share_two.reshape(j, full_s // nz), "gz")
-    grad_two = jnp.concatenate([share_two[z] for z in range(nz)], axis=1) / jnp.sqrt(f32(i * nx * k * nz))
+    share_two = jnp.concatenate([share_two[c * half_j : (c + 1) * half_j] for c in range(parts)], axis=1)
+    grad_two = gather(share_two, "gz").reshape(j, full_s) / jnp.sqrt(f32(i * nx * k * nz))
     last, grad_two = lax.optimization_barrier((last, grad_two))
 
     cut = i * half_r // full_t
     grad_one = gather(last[:, :cut].sum(axis=0).reshape(i, half_r), "gz")
     grad_one = jnp.concatenate([grad_one[z] for z in range(nz)], axis=1) / jnp.sqrt(f32(j * ny * k * nz))
-    last = last[:, cut:].reshape(ny, nz, -1, full_t).transpose(1, 0, 2, 3)
-    grad_three = trade(last, "gz").transpose(1, 0, 2, 3).reshape(k, full_t) / jnp.sqrt(f32(i * nx * j * ny))
+    grad_three = last[:, cut:].reshape(k, full_t) / jnp.sqrt(f32(i * nx * j * ny))
     return (residual.reshape(i, j, k), grad_one, grad_two, grad_three)
 
 

time: 101 us -> 100 us (0.990)
    ppermute x15 -> x14, waiting for transfers between devices: 11.9 us -> 12.9 us  [swap(): return lax.ppermute(x, axis, [(0, 1), (1, 0)])]
    ppermute x15 -> x14, starting transfers between devices: 10.9 us -> 10.1 us  [swap(): return lax.ppermute(x, axis, [(0, 1), (1, 0)])]
  transfers between devices with their start and end apart: 20 -> 19, of which waited for: 13 -> 13; matrix products, arithmetic and copies ran while one was open for 5% -> 4% of each run, Pallas kernels for 12% -> 11%
where the time goes in v7:
time: 100 us; the launch traced here: 99.6 us
  waiting for transfers between devices  43.1 us (43%)
  starting transfers between devices  33.9 us (34%)
  Pallas kernels  13.7 us (14%)
  other arithmetic  3.54 us (4%)
  local copies, waits for them, and re-layouts  2.93 us (3%)
  matrix products  1.55 us (2%)
    ppermute x14, waiting for transfers between devices, swap(): return lax.ppermute(x, axis, [(0, 1), (1, 0)])  12.9 us
    all_to_all x1, waiting for transfers between devices, local(): late = lax.all_to_all(late, 'gy', 0, 0, tiled=True)  11.6 us
    ppermute x14, starting transfers between devices, swap(): return lax.ppermute(x, axis, [(0, 1), (1, 0)])  10.1 us
    all_to_all x1, waiting for transfers between devices, local(): lax.all_to_all(after_one.reshape(nz * ny, e * q, full_t), ('gz', 'gy'), 0...  7.46 us
    all_to_all x1, waiting for transfers between devices, local(): lax.all_to_all(jnp.broadcast_to(last[None], (ny,) + last.shape), 'gy', 0,...  7.36 us
    all_to_all x1, starting transfers between devices, local(): early = lax.all_to_all(early, 'gy', 0, 0, tiled=True)  6.37 us
    all_to_all x1, starting transfers between devices, local(): lax.all_to_all(jnp.broadcast_to(last[None], (ny,) + last.shape), 'gy', 0,...  5.69 us
    all_to_all x1, starting transfers between devices, local(): late = lax.all_to_all(late, 'gy', 0, 0, tiled=True)  4.46 us
  transfers between devices with their start and end apart: 19, of which 13 were waited for; matrix products, arithmetic and copies ran while one was open for 4% of the time, Pallas kernels for 11%

profile of v7, /device:TPU:0, one launch (start us, length us, event | category | flops | bytes accessed | tf_op | source)
XLA Modules:
  0.0 99.6 jit_solution(9773262127216512743)
XLA Ops:
  0.7 1.3 %copy.16 = f32[32,32,256]{2,1,0:T(8,128)S(1)} copy(f32[32,32,256]{2,1,0:T(8,128)} %param.5) | data formatting | bytes 2097152
  3.0 2.6 %collective-permute-start.1 = (f32[32,128]{1,0:T(8,128)S(1)}, f32[32,128]{1,0:T(8,128)S(1)}, u32[]{:S(2)}, u32[]{:S(2)}) collective-permute-start(f32[32,128]{1,0:T(8,128)S(1)} %get-tuple-element.55), channel_id=1, source_target_pairs={{0,16},{16,0},{1,17},{17,1},{2,18},{18,2},{3,19},{19,3},{4,20},{20... | collective-permute-start | bytes 49160 | tf_op jit(solution)/shard_map/ppermute | solution.py:29
  7.3 6.4 %all-to-all-start = ((f32[8,96,128]{2,1,0:T(8,128)}), f32[8,96,128]{2,1,0:T(8,128)S(1)}, u32[]{:S(2)}, u32[]{:S(2)}) async-start(f32[8,96,128]{2,1,0:T(8,128)} %pad_maximum_fusion), calls=%async_computation | async-start | bytes 786432 | tf_op jit(solution)/shard_map/all_to_all | solution.py:313
  14.9 1.6 %collective-permute-start.2 = (f32[32,16,128]{2,1,0:T(8,128)S(1)}, f32[32,16,128]{2,1,0:T(8,128)S(1)}, u32[]{:S(2)}, u32[]{:S(2)}) collective-permute-start(f32[32,16,128]{2,1,0:T(8,128)S(1)} %shard_map.85), channel_id=1, source_target_pairs={{0,16},{16,0},{1,17},{17,1},{2,18},{18,2},{3,19},{19,3},{4,20},{20... | collective-permute-start | bytes 786440 | tf_op jit(solution)/shard_map/ppermute | solution.py:29
  17.6 4.6 %collective-permute-done.2 = f32[32,16,128]{2,1,0:T(8,128)S(1)} collective-permute-done((f32[32,16,128]{2,1,0:T(8,128)S(1)}, f32[32,16,128]{2,1,0:T(8,128)S(1)}, u32[]{:S(2)}, u32[]{:S(2)}) %collective-permute-start.2) | collective-permute-done | bytes 262176 | tf_op jit(solution)/shard_map/ppermute | solution.py:29
  22.9 2.0 %all-to-all-done.early_ref = f32[8,96,128]{2,1,0:T(8,128)S(1)} async-done(((f32[8,96,128]{2,1,0:T(8,128)}), f32[8,96,128]{2,1,0:T(8,128)S(1)}, u32[]{:S(2)}, u32[]{:S(2)}) %all-to-all-start) | async-done | bytes 393248 | tf_op jit(solution)/shard_map/all_to_all | solution.py:313
  24.9 3.8 %all-to-all-start.1 = ((f32[16,32,128]{2,1,0:T(8,128)}), f32[16,32,128]{2,1,0:T(8,128)S(1)}, u32[]{:S(2)}, u32[]{:S(2)}) async-start(f32[16,32,128]{2,1,0:T(8,128)} %bitcast.10), calls=%async_computation.1 | async-start | bytes 524288 | tf_op jit(solution)/shard_map/all_to_all | solution.py:324
  30.1 1.4 %collective-permute-start.6 = (f32[16,64,128]{2,1,0:T(8,128)S(1)}, f32[16,64,128]{2,1,0:T(8,128)S(1)}, u32[]{:S(2)}, u32[]{:S(2)}) collective-permute-start(f32[16,64,128]{2,1,0:T(8,128)S(1)} %get-tuple-element.45.own_mine_ref), channel_id=1, source_target_pairs={{0,16},{16,0},{1,17},{17,1},{2,18},{18,2},{3,19},{19,3},{4,20},{20... | collective-permute-start | bytes 1572872 | tf_op jit(solution)/shard_map/ppermute | solution.py:29
  31.7 7.5 %all-to-all-done.1 = f32[16,32,128]{2,1,0:T(8,128)S(1)} async-done(((f32[16,32,128]{2,1,0:T(8,128)}), f32[16,32,128]{2,1,0:T(8,128)S(1)}, u32[]{:S(2)}, u32[]{:S(2)}) %all-to-all-start.1) | async-done | bytes 262176 | tf_op jit(solution)/shard_map/all_to_all | solution.py:324
  39.1 1.7 %shard_map.86 = (f32[8,2,16,256]{3,2,1,0:T(8,128)S(1)}, f32[8,2,16,256]{3,2,1,0:T(8,128)S(1)}, f32[8,2,32,128]{3,2,1,0:T(8,128)}) custom-call(s32[2]{0:T(128)S(1)} %pad_add_fusion.place_ref, f32[2,8,32,128]{3,2,1,0:T(8,128)S(1)} %bitcast.40, f32[8,2,16,128]{3,2,1,0:T(8,128)S(1)} %bitcast.44, f32[8,2,16,128]{3,2,1,0:T(8,128)S(1)} %collective-permute-done.3.other_ref), custom_call_target="tpu_custom_call" | custom-call | tf_op jit(solution)/shard_map/pallas_call | solution.py:103
  40.8 3.4 %all-to-all-start.2 = ((f32[8,2,32,128]{3,2,1,0:T(8,128)}), f32[8,2,32,128]{3,2,1,0:T(8,128)S(1)}, u32[]{:S(2)}, u32[]{:S(2)}) async-start(f32[8,2,32,128]{3,2,1,0:T(8,128)} %get-tuple-element.28.moved_ref), calls=%async_computation.2 | async-start | bytes 524288 | tf_op jit(solution)/shard_map/all_to_all | solution.py:327
  46.0 2.5 %shard_map.87 = (f32[8,64,128]{2,1,0:T(8,128)S(1)}, f32[8,64,128]{2,1,0:T(8,128)S(1)}) custom-call(s32[2]{0:T(128)S(1)} %pad_add_fusion.place_ref, f32[8,2,32,128]{3,2,1,0:T(8,128)} %get-tuple-element.28.moved_ref, f32[128,128]{1,0:T(8,128)S(1)} %fusion.9.gram_ref, f32[128,128]{1,0:T(8,128)S(1)} %collective-permute-done.4.gram_other_ref, ...), custom_call_target="tpu_custom_call" | custom-call | flops 1000000000 | bytes 2097152 | tf_op jit(solution)/shard_map/pallas_call | solution.py:140
  48.8 1.4 %collective-permute-done.5.arrived_ref = f32[8,64,128]{2,1,0:T(8,128)S(1)} collective-permute-done((f32[8,64,128]{2,1,0:T(8,128)S(1)}, f32[8,64,128]{2,1,0:T(8,128)S(1)}, u32[]{:S(2)}, u32[]{:S(2)}) %collective-permute-start.5) | collective-permute-done | bytes 262176 | tf_op jit(solution)/shard_map/ppermute | solution.py:29
  51.0 1.8 %all-to-all-done.2 = f32[8,2,32,128]{3,2,1,0:T(8,128)S(1)} async-done(((f32[8,2,32,128]{3,2,1,0:T(8,128)}), f32[8,2,32,128]{3,2,1,0:T(8,128)S(1)}, u32[]{:S(2)}, u32[]{:S(2)}) %all-to-all-start.2) | async-done | bytes 262176 | tf_op jit(solution)/shard_map/all_to_all | solution.py:327
  52.8 2.1 %shard_map.89 = (f32[1024,256]{1,0:T(8,128)}, f32[128,256]{1,0:T(8,128)S(1)}) custom-call(s32[1]{0:T(128)} %bitcast.half_ref, f32[1024,256]{1,0:T(8,128)} %bitcast.47, f32[512,128]{1,0:T(8,128)S(1)} %bitcast.42, f32[256,128]{1,0:T(8,128)S(1)} %copy-done.2), custom_call_target="tpu_custom_call", output_to_operand_aliasing={{0}: (1, {})} | custom-call | tf_op jit(solution)/shard_map/pallas_call | solution.py:210
  54.9 2.4 %shard_map.90 = (f32[1024,256]{1,0:T(8,128)}, f32[8,128,128]{2,1,0:T(8,128)}) custom-call(s32[1]{0:T(128)S(6)} %sub.10.half_ref, f32[1024,256]{1,0:T(8,128)} %get-tuple-element.34._, f32[512,128]{1,0:T(8,128)S(1)} %collective-permute-done.7.after_ref, f32[256,128]{1,0:T(8,128)S(1)} %copy-done.2, ...), custom_call_target="tpu_custom_call", output_to_operand_aliasing={{0}: (1, {}), {1}: (5, {})} | custom-call | tf_op jit(solution)/shard_map/pallas_call | solution.py:233
  57.4 4.5 %all-to-all-start.3 = ((f32[8,128,128]{2,1,0:T(8,128)}), f32[8,128,128]{2,1,0:T(8,128)S(1)}, u32[]{:S(2)}, u32[]{:S(2)}) async-start(f32[8,128,128]{2,1,0:T(8,128)} %get-tuple-element.38), calls=%async_computation.3 | async-start | bytes 1048576 | tf_op jit(solution)/shard_map/all_to_all | solution.py:335
  62.0 1.8 %collective-permute-done.8.own_other_ref = f32[16,64,128]{2,1,0:T(8,128)S(1)} collective-permute-done((f32[16,64,128]{2,1,0:T(8,128)S(1)}, f32[16,64,128]{2,1,0:T(8,128)S(1)}, u32[]{:S(2)}, u32[]{:S(2)}) %collective-permute-start.8) | collective-permute-done | bytes 524320 | tf_op jit(solution)/shard_map/ppermute | solution.py:29
  63.8 1.4 %collective-permute-start.9 = (f32[16,64,128]{2,1,0:T(8,128)S(1)}, f32[16,64,128]{2,1,0:T(8,128)S(1)}, u32[]{:S(2)}, u32[]{:S(2)}) collective-permute-start(f32[16,64,128]{2,1,0:T(8,128)S(1)} %collective-permute-done.8.own_other_ref), channel_id=1, source_target_pairs={{0,16},{16,0},{1,17},{17,1},{2,18},{18,2},{3,19},{19,3},{4,20},{20... | collective-permute-start | bytes 1572872 | tf_op jit(solution)/shard_map/ppermute | solution.py:29
  65.3 11.6 %all-to-all-done.3.late_ref = f32[8,128,128]{2,1,0:T(8,128)S(1)} async-done(((f32[8,128,128]{2,1,0:T(8,128)}), f32[8,128,128]{2,1,0:T(8,128)S(1)}, u32[]{:S(2)}, u32[]{:S(2)}) %all-to-all-start.3) | async-done | bytes 524320 | tf_op jit(solution)/shard_map/all_to_all | solution.py:335
  76.9 1.5 %collective-permute-start.11 = (f32[64,128]{1,0:T(8,128)S(1)}, f32[64,128]{1,0:T(8,128)S(1)}, u32[]{:S(2)}, u32[]{:S(2)}) collective-permute-start(f32[64,128]{1,0:T(8,128)S(1)} %slice_reduce_fusion), channel_id=1, source_target_pairs={{0,16},{16,0},{1,17},{17,1},{2,18},{18,2},{3,19},{19,3},{4,20},{20... | collective-permute-start | bytes 98312 | tf_op jit(solution)/shard_map/ppermute | solution.py:29
  78.4 1.8 %shard_map.91 = (f32[32,128]{1,0:T(8,128)S(1)}, f32[32,128]{1,0:T(8,128)S(1)}) custom-call(s32[2]{0:T(128)S(1)} %pad_add_fusion.place_ref, f32[8,128,128]{2,1,0:T(8,128)S(1)} %all-to-all-done.3.late_ref, f32[16,64,128]{2,1,0:T(8,128)S(1)} %get-tuple-element.45.own_mine_ref, f32[16,64,128]{2,1,0:T(8,128)S(1)} %collective-permute-done.8.own_other_ref, ...), custom_call_target="tpu_custom_call" | custom-call | tf_op jit(solution)/shard_map/pallas_call | solution.py:270
  82.2 5.7 %all-to-all-start.4 = ((f32[8,64,128]{2,1,0:T(8,128)}), f32[8,64,128]{2,1,0:T(8,128)S(1)}, u32[]{:S(2)}, u32[]{:S(2)}) async-start(f32[8,64,128]{2,1,0:T(8,128)} %broadcast_in_dim.5), calls=%async_computation.4 | async-start | bytes 524288 | tf_op jit(solution)/shard_map/all_to_all | solution.py:348
  89.8 7.4 %all-to-all-done.4 = f32[8,64,128]{2,1,0:T(8,128)S(1)} async-done(((f32[8,64,128]{2,1,0:T(8,128)}), f32[8,64,128]{2,1,0:T(8,128)S(1)}, u32[]{:S(2)}, u32[]{:S(2)}) %all-to-all-start.4) | async-done | bytes 262176 | tf_op jit(solution)/shard_map/all_to_all | solution.py:348
  (61 shorter events, 16.5 us)
Async XLA Ops:
  0.6 5.0 %copy-start = (f32[32,256]{1,0:T(8,128)S(1)}, f32[32,256]{1,0:T(8,128)}, u32[]{:S(2)}) copy-start(f32[32,256]{1,0:T(8,128)} %param.8) | copy-start | bytes 98308
  0.6 1.3 %copy-start.2 = (f32[256,128]{1,0:T(8,128)S(1)}, f32[256,128]{1,0:T(8,128)}, u32[]{:S(2)}) copy-start(f32[256,128]{1,0:T(8,128)} %factor_ref.3) | copy-start | bytes 393220
  1.9 3.7 %copy-start.3 = (f32[32,32,256]{2,1,0:T(8,128)}, f32[32,32,256]{2,1,0:T(8,128)S(1)}, u32[]{:S(2)}) copy-start(f32[32,32,256]{2,1,0:T(8,128)S(1)} %copy.16) | copy-start | bytes 3145732
  2.5 3.1 %collective-permute-start = (f32[512,128]{1,0:T(8,128)S(1)}, f32[512,128]{1,0:T(8,128)S(1)}, u32[]{:S(2)}, u32[]{:S(2)}) collective-permute-start(f32[512,128]{1,0:T(8,128)S(1)} %fusion.1), channel_id=1, source_target_pairs={{0,1},{1,0},{2,3},{3,2},{4,5},{5,4},{6,7},{7,6},{8,9},{9,8},{10,11... | collective-permute-start | bytes 786440 | tf_op jit(solution)/shard_map/ppermute | solution.py:29
  3.0 4.3 %collective-permute-start.1 = (f32[32,128]{1,0:T(8,128)S(1)}, f32[32,128]{1,0:T(8,128)S(1)}, u32[]{:S(2)}, u32[]{:S(2)}) collective-permute-start(f32[32,128]{1,0:T(8,128)S(1)} %get-tuple-element.55), channel_id=1, source_target_pairs={{0,16},{16,0},{1,17},{17,1},{2,18},{18,2},{3,19},{19,3},{4,20},{20... | collective-permute-start | bytes 49160 | tf_op jit(solution)/shard_map/ppermute | solution.py:29
  6.3 7.5 %copy-start.1 = (f32[128,32,64]{0,2,1:T(8,128)S(1)}, f32[128,32,64]{0,2,1:T(8,128)}, u32[]{:S(2)}) copy-start(f32[128,32,64]{0,2,1:T(8,128)} %param.6) | copy-start | bytes 3145732
  7.3 17.6 %all-to-all-start = ((f32[8,96,128]{2,1,0:T(8,128)}), f32[8,96,128]{2,1,0:T(8,128)S(1)}, u32[]{:S(2)}, u32[]{:S(2)}) async-start(f32[8,96,128]{2,1,0:T(8,128)} %pad_maximum_fusion), calls=%async_computation | async-start | bytes 786432 | tf_op jit(solution)/shard_map/all_to_all | solution.py:313
  14.9 7.3 %collective-permute-start.2 = (f32[32,16,128]{2,1,0:T(8,128)S(1)}, f32[32,16,128]{2,1,0:T(8,128)S(1)}, u32[]{:S(2)}, u32[]{:S(2)}) collective-permute-start(f32[32,16,128]{2,1,0:T(8,128)S(1)} %shard_map.85), channel_id=1, source_target_pairs={{0,16},{16,0},{1,17},{17,1},{2,18},{18,2},{3,19},{19,3},{4,20},{20... | collective-permute-start | bytes 786440 | tf_op jit(solution)/shard_map/ppermute | solution.py:29
  24.9 14.2 %all-to-all-start.1 = ((f32[16,32,128]{2,1,0:T(8,128)}), f32[16,32,128]{2,1,0:T(8,128)S(1)}, u32[]{:S(2)}, u32[]{:S(2)}) async-start(f32[16,32,128]{2,1,0:T(8,128)} %bitcast.10), calls=%async_computation.1 | async-start | bytes 524288 | tf_op jit(solution)/shard_map/all_to_all | solution.py:324
  28.8 2.9 %collective-permute-start.3 = (f32[8,2,16,128]{3,2,1,0:T(8,128)S(1)}, f32[8,2,16,128]{3,2,1,0:T(8,128)S(1)}, u32[]{:S(2)}, u32[]{:S(2)}) collective-permute-start(f32[8,2,16,128]{3,2,1,0:T(8,128)S(1)} %bitcast.43), channel_id=1, source_target_pairs={{0,1},{1,0},{2,3},{3,2},{4,5},{5,4},{6,7},{7,6},{8,9},{9,8},{10,11... | collective-permute-start | bytes 393224 | tf_op jit(solution)/shard_map/ppermute | solution.py:29
  30.1 20.8 %collective-permute-start.6 = (f32[16,64,128]{2,1,0:T(8,128)S(1)}, f32[16,64,128]{2,1,0:T(8,128)S(1)}, u32[]{:S(2)}, u32[]{:S(2)}) collective-permute-start(f32[16,64,128]{2,1,0:T(8,128)S(1)} %get-tuple-element.45.own_mine_ref), channel_id=1, source_target_pairs={{0,16},{16,0},{1,17},{17,1},{2,18},{18,2},{3,19},{19,3},{4,20},{20... | collective-permute-start | bytes 1572872 | tf_op jit(solution)/shard_map/ppermute | solution.py:29
  40.8 12.0 %all-to-all-start.2 = ((f32[8,2,32,128]{3,2,1,0:T(8,128)}), f32[8,2,32,128]{3,2,1,0:T(8,128)S(1)}, u32[]{:S(2)}, u32[]{:S(2)}) async-start(f32[8,2,32,128]{3,2,1,0:T(8,128)} %get-tuple-element.28.moved_ref), calls=%async_computation.2 | async-start | bytes 524288 | tf_op jit(solution)/shard_map/all_to_all | solution.py:327
  44.7 1.3 %collective-permute-start.4 = (f32[128,128]{1,0:T(8,128)S(1)}, f32[128,128]{1,0:T(8,128)S(1)}, u32[]{:S(2)}, u32[]{:S(2)}) collective-permute-start(f32[128,128]{1,0:T(8,128)S(1)} %fusion.9.gram_ref), channel_id=1, source_target_pairs={{0,1},{1,0},{2,3},{3,2},{4,5},{5,4},{6,7},{7,6},{8,9},{9,8},{10,11... | collective-permute-start | bytes 196616 | tf_op jit(solution)/shard_map/ppermute | solution.py:29
  48.5 1.6 %collective-permute-start.5 = (f32[8,64,128]{2,1,0:T(8,128)S(1)}, f32[8,64,128]{2,1,0:T(8,128)S(1)}, u32[]{:S(2)}, u32[]{:S(2)}) collective-permute-start(f32[8,64,128]{2,1,0:T(8,128)S(1)} %get-tuple-element.32), channel_id=1, source_target_pairs={{0,1},{1,0},{2,3},{3,2},{4,5},{5,4},{6,7},{7,6},{8,9},{9,8},{10,11... | collective-permute-start | bytes 786440 | tf_op jit(solution)/shard_map/ppermute | solution.py:29
  52.8 2.1 %collective-permute-start.7 = (f32[512,128]{1,0:T(8,128)S(1)}, f32[512,128]{1,0:T(8,128)S(1)}, u32[]{:S(2)}, u32[]{:S(2)}) collective-permute-start(f32[512,128]{1,0:T(8,128)S(1)} %bitcast.41), channel_id=1, source_target_pairs={{0,1},{1,0},{2,3},{3,2},{4,5},{5,4},{6,7},{7,6},{8,9},{9,8},{10,11... | collective-permute-start | bytes 786440 | tf_op jit(solution)/shard_map/ppermute | solution.py:29
  57.4 4.5 %copy-start.4 = (f32[16,64,128]{2,1,0:T(8,128)S(1)}, f32[16,64,128]{2,1,0:T(8,128)}, u32[]{:S(2)}) copy-start(f32[16,64,128]{2,1,0:T(8,128)} %get-tuple-element.44) | copy-start | bytes 1572868
  57.4 19.5 %all-to-all-start.3 = ((f32[8,128,128]{2,1,0:T(8,128)}), f32[8,128,128]{2,1,0:T(8,128)S(1)}, u32[]{:S(2)}, u32[]{:S(2)}) async-start(f32[8,128,128]{2,1,0:T(8,128)} %get-tuple-element.38), calls=%async_computation.3 | async-start | bytes 1048576 | tf_op jit(solution)/shard_map/all_to_all | solution.py:335
  61.8 2.0 %collective-permute-start.8 = (f32[16,64,128]{2,1,0:T(8,128)S(1)}, f32[16,64,128]{2,1,0:T(8,128)S(1)}, u32[]{:S(2)}, u32[]{:S(2)}) collective-permute-start(f32[16,64,128]{2,1,0:T(8,128)S(1)} %copy-done.4), channel_id=1, source_target_pairs={{0,1},{1,0},{2,3},{3,2},{4,5},{5,4},{6,7},{7,6},{8,9},{9,8},{10,11... | collective-permute-start | bytes 1572872 | tf_op jit(solution)/shard_map/ppermute | solution.py:29
  63.8 14.6 %collective-permute-start.9 = (f32[16,64,128]{2,1,0:T(8,128)S(1)}, f32[16,64,128]{2,1,0:T(8,128)S(1)}, u32[]{:S(2)}, u32[]{:S(2)}) collective-permute-start(f32[16,64,128]{2,1,0:T(8,128)S(1)} %collective-permute-done.8.own_other_ref), channel_id=1, source_target_pairs={{0,16},{16,0},{1,17},{17,1},{2,18},{18,2},{3,19},{19,3},{4,20},{20... | collective-permute-start | bytes 1572872 | tf_op jit(solution)/shard_map/ppermute | solution.py:29
  76.9 4.6 %collective-permute-start.11 = (f32[64,128]{1,0:T(8,128)S(1)}, f32[64,128]{1,0:T(8,128)S(1)}, u32[]{:S(2)}, u32[]{:S(2)}) collective-permute-start(f32[64,128]{1,0:T(8,128)S(1)} %slice_reduce_fusion), channel_id=1, source_target_pairs={{0,16},{16,0},{1,17},{17,1},{2,18},{18,2},{3,19},{19,3},{4,20},{20... | collective-permute-start | bytes 98312 | tf_op jit(solution)/shard_map/ppermute | solution.py:29
  80.2 1.2 %collective-permute-start.10 = (f32[32,128]{1,0:T(8,128)S(1)}, f32[32,128]{1,0:T(8,128)S(1)}, u32[]{:S(2)}, u32[]{:S(2)}) collective-permute-start(f32[32,128]{1,0:T(8,128)S(1)} %get-tuple-element.41), channel_id=1, source_target_pairs={{0,1},{1,0},{2,3},{3,2},{4,5},{5,4},{6,7},{7,6},{8,9},{9,8},{10,11... | collective-permute-start | bytes 49160 | tf_op jit(solution)/shard_map/ppermute | solution.py:29
  82.2 14.9 %all-to-all-start.4 = ((f32[8,64,128]{2,1,0:T(8,128)}), f32[8,64,128]{2,1,0:T(8,128)S(1)}, u32[]{:S(2)}, u32[]{:S(2)}) async-start(f32[8,64,128]{2,1,0:T(8,128)} %broadcast_in_dim.5), calls=%async_computation.4 | async-start | bytes 524288 | tf_op jit(solution)/shard_map/all_to_all | solution.py:348
  87.9 1.2 %collective-permute-start.12 = (f32[16,256]{1,0:T(8,128)S(1)}, f32[16,256]{1,0:T(8,128)S(1)}, u32[]{:S(2)}, u32[]{:S(2)}) collective-permute-start(f32[16,256]{1,0:T(8,128)S(1)} %pad_maximum_fusion.3), channel_id=1, source_target_pairs={{0,1},{1,0},{2,3},{3,2},{4,5},{5,4},{6,7},{7,6},{8,9},{9,8},{10,11... | collective-permute-start | bytes 49160 | tf_op jit(solution)/shard_map/ppermute | solution.py:29
  97.8 1.2 %collective-permute-start.13 = (f32[32,128]{1,0:T(8,128)S(1)}, f32[32,128]{1,0:T(8,128)S(1)}, u32[]{:S(2)}, u32[]{:S(2)}) collective-permute-start(f32[32,128]{1,0:T(8,128)S(1)} %get-tuple-element.47), channel_id=1, source_target_pairs={{0,1},{1,0},{2,3},{3,2},{4,5},{5,4},{6,7},{7,6},{8,9},{9,8},{10,11... | collective-permute-start | bytes 49160 | tf_op jit(solution)/shard_map/ppermute | solution.py:29
  (1 other events, 1.1 us)

commit v8 on v7

--- a/solution.py
+++ b/solution.py
@@ -322,6 +322,7 @@
         own_mine, own_other = part(flat, gz), swap(part(flat, 1 - gz), "gz")
         near_mine = swap(own_mine, "gx")
     after_one = lax.all_to_all(after_one.reshape(nz * ny, e * q, full_t), ("gz", "gy"), 0, 0, tiled=True)
+    after_one, gram_other = lax.optimization_barrier((after_one, gram_other))
     after_one = after_one.reshape(nz, ny, e * q, full_t)
     one, two, moved = mode_two(place, after_one, mine_two, other_two, e, t)
     home = lax.all_to_all(moved, "gy", 0, 0, tiled=True).reshape(rows // nz, full_t)

time: 100 us -> 99.5 us (level)
    all_to_all x1, waiting for transfers between devices: 1.84 us -> 3.52 us  [local(): lax.all_to_all(moved, 'gy', 0, 0, tiled=True).reshape(rows // nz, full_t)]
    ppermute x14, waiting for transfers between devices: 12.9 us -> 11.5 us  [swap(): return lax.ppermute(x, axis, [(0, 1), (1, 0)])]
  transfers between devices with their start and end apart: 19 -> 19, of which waited for: 13 -> 12; matrix products, arithmetic and copies ran while one was open for 4% -> 4% of each run, Pallas kernels for 11% -> 11%
where the time goes in v8:
time: 99.5 us; the launch traced here: 98.7 us
  waiting for transfers between devices  43.1 us (43%)
  starting transfers between devices  33 us (33%)
  Pallas kernels  13.7 us (14%)
  other arithmetic  3.54 us (4%)
  local copies, waits for them, and re-layouts  2.93 us (3%)
  matrix products  1.55 us (2%)
    all_to_all x1, waiting for transfers between devices, local(): late = lax.all_to_all(late, 'gy', 0, 0, tiled=True)  11.8 us
    ppermute x14, waiting for transfers between devices, swap(): return lax.ppermute(x, axis, [(0, 1), (1, 0)])  11.5 us
    ppermute x14, starting transfers between devices, swap(): return lax.ppermute(x, axis, [(0, 1), (1, 0)])  10.5 us
    all_to_all x1, waiting for transfers between devices, local(): lax.all_to_all(jnp.broadcast_to(last[None], (ny,) + last.shape), 'gy', 0,...  7.36 us
    all_to_all x1, waiting for transfers between devices, local(): lax.all_to_all(after_one.reshape(nz * ny, e * q, full_t), ('gz', 'gy'), 0...  6.91 us
    all_to_all x1, starting transfers between devices, local(): early = lax.all_to_all(early, 'gy', 0, 0, tiled=True)  6.37 us
    all_to_all x1, starting transfers between devices, local(): lax.all_to_all(jnp.broadcast_to(last[None], (ny,) + last.shape), 'gy', 0,...  5.25 us
    all_to_all x1, starting transfers between devices, local(): lax.all_to_all(after_one.reshape(nz * ny, e * q, full_t), ('gz', 'gy'), 0...  3.83 us
  transfers between devices with their start and end apart: 19, of which 12 were waited for; matrix products, arithmetic and copies ran while one was open for 4% of the time, Pallas kernels for 11%

profile of v8, /device:TPU:0, one launch (start us, length us, event | category | flops | bytes accessed | tf_op | source)
XLA Modules:
  0.0 98.7 jit_solution(16004761670804939243)
XLA Ops:
  0.7 1.3 %copy.16 = f32[32,32,256]{2,1,0:T(8,128)S(1)} copy(f32[32,32,256]{2,1,0:T(8,128)} %param.5) | data formatting | bytes 2097152
  3.0 2.6 %collective-permute-start.1 = (f32[32,128]{1,0:T(8,128)S(1)}, f32[32,128]{1,0:T(8,128)S(1)}, u32[]{:S(2)}, u32[]{:S(2)}) collective-permute-start(f32[32,128]{1,0:T(8,128)S(1)} %get-tuple-element.59), channel_id=1, source_target_pairs={{0,16},{16,0},{1,17},{17,1},{2,18},{18,2},{3,19},{19,3},{4,20},{20... | collective-permute-start | bytes 49160 | tf_op jit(solution)/shard_map/ppermute | solution.py:29
  7.3 6.4 %all-to-all-start = ((f32[8,96,128]{2,1,0:T(8,128)}), f32[8,96,128]{2,1,0:T(8,128)S(1)}, u32[]{:S(2)}, u32[]{:S(2)}) async-start(f32[8,96,128]{2,1,0:T(8,128)} %pad_maximum_fusion), calls=%async_computation | async-start | bytes 786432 | tf_op jit(solution)/shard_map/all_to_all | solution.py:313
  14.9 1.6 %collective-permute-start.2 = (f32[32,16,128]{2,1,0:T(8,128)S(1)}, f32[32,16,128]{2,1,0:T(8,128)S(1)}, u32[]{:S(2)}, u32[]{:S(2)}) collective-permute-start(f32[32,16,128]{2,1,0:T(8,128)S(1)} %shard_map.85), channel_id=1, source_target_pairs={{0,16},{16,0},{1,17},{17,1},{2,18},{18,2},{3,19},{19,3},{4,20},{20... | collective-permute-start | bytes 786440 | tf_op jit(solution)/shard_map/ppermute | solution.py:29
  17.6 4.6 %collective-permute-done.2 = f32[32,16,128]{2,1,0:T(8,128)S(1)} collective-permute-done((f32[32,16,128]{2,1,0:T(8,128)S(1)}, f32[32,16,128]{2,1,0:T(8,128)S(1)}, u32[]{:S(2)}, u32[]{:S(2)}) %collective-permute-start.2) | collective-permute-done | bytes 262176 | tf_op jit(solution)/shard_map/ppermute | solution.py:29
  22.9 2.0 %all-to-all-done.early_ref = f32[8,96,128]{2,1,0:T(8,128)S(1)} async-done(((f32[8,96,128]{2,1,0:T(8,128)}), f32[8,96,128]{2,1,0:T(8,128)S(1)}, u32[]{:S(2)}, u32[]{:S(2)}) %all-to-all-start) | async-done | bytes 393248 | tf_op jit(solution)/shard_map/all_to_all | solution.py:313
  24.9 3.8 %all-to-all-start.1 = ((f32[16,32,128]{2,1,0:T(8,128)}), f32[16,32,128]{2,1,0:T(8,128)S(1)}, u32[]{:S(2)}, u32[]{:S(2)}) async-start(f32[16,32,128]{2,1,0:T(8,128)} %bitcast.10), calls=%async_computation.1 | async-start | bytes 524288 | tf_op jit(solution)/shard_map/all_to_all | solution.py:324
  30.7 1.4 %collective-permute-start.6 = (f32[16,64,128]{2,1,0:T(8,128)S(1)}, f32[16,64,128]{2,1,0:T(8,128)S(1)}, u32[]{:S(2)}, u32[]{:S(2)}) collective-permute-start(f32[16,64,128]{2,1,0:T(8,128)S(1)} %get-tuple-element.49.own_mine_ref), channel_id=1, source_target_pairs={{0,16},{16,0},{1,17},{17,1},{2,18},{18,2},{3,19},{19,3},{4,20},{20... | collective-permute-start | bytes 1572872 | tf_op jit(solution)/shard_map/ppermute | solution.py:29
  32.2 6.9 %all-to-all-done.1 = f32[16,32,128]{2,1,0:T(8,128)S(1)} async-done(((f32[16,32,128]{2,1,0:T(8,128)}), f32[16,32,128]{2,1,0:T(8,128)S(1)}, u32[]{:S(2)}, u32[]{:S(2)}) %all-to-all-start.1) | async-done | bytes 262176 | tf_op jit(solution)/shard_map/all_to_all | solution.py:324
  39.1 1.7 %shard_map.86 = (f32[8,2,16,256]{3,2,1,0:T(8,128)S(1)}, f32[8,2,16,256]{3,2,1,0:T(8,128)S(1)}, f32[8,2,32,128]{3,2,1,0:T(8,128)}) custom-call(s32[2]{0:T(128)S(1)} %pad_add_fusion.place_ref, f32[2,8,32,128]{3,2,1,0:T(8,128)S(1)} %bitcast.40, f32[8,2,16,128]{3,2,1,0:T(8,128)S(1)} %bitcast.44, f32[8,2,16,128]{3,2,1,0:T(8,128)S(1)} %collective-permute-done.4.other_ref), custom_call_target="tpu_custom_call" | custom-call | tf_op jit(solution)/shard_map/pallas_call | solution.py:103
  40.9 3.4 %all-to-all-start.2 = ((f32[8,2,32,128]{3,2,1,0:T(8,128)}), f32[8,2,32,128]{3,2,1,0:T(8,128)S(1)}, u32[]{:S(2)}, u32[]{:S(2)}) async-start(f32[8,2,32,128]{3,2,1,0:T(8,128)} %get-tuple-element.31.moved_ref), calls=%async_computation.2 | async-start | bytes 524288 | tf_op jit(solution)/shard_map/all_to_all | solution.py:328
  44.3 2.6 %shard_map.87 = (f32[8,64,128]{2,1,0:T(8,128)S(1)}, f32[8,64,128]{2,1,0:T(8,128)S(1)}) custom-call(s32[2]{0:T(128)S(1)} %pad_add_fusion.place_ref, f32[8,2,32,128]{3,2,1,0:T(8,128)} %get-tuple-element.31.moved_ref, f32[128,128]{1,0:T(8,128)S(1)} %fusion.9.gram_ref, f32[128,128]{1,0:T(8,128)S(1)} %collective-permute-done.3.gram_other_ref, ...), custom_call_target="tpu_custom_call" | custom-call | flops 1000000000 | bytes 2097152 | tf_op jit(solution)/shard_map/pallas_call | solution.py:140
  46.9 1.5 %collective-permute-done.5.arrived_ref = f32[8,64,128]{2,1,0:T(8,128)S(1)} collective-permute-done((f32[8,64,128]{2,1,0:T(8,128)S(1)}, f32[8,64,128]{2,1,0:T(8,128)S(1)}, u32[]{:S(2)}, u32[]{:S(2)}) %collective-permute-start.5) | collective-permute-done | bytes 262176 | tf_op jit(solution)/shard_map/ppermute | solution.py:29
  49.3 3.5 %all-to-all-done.2 = f32[8,2,32,128]{3,2,1,0:T(8,128)S(1)} async-done(((f32[8,2,32,128]{3,2,1,0:T(8,128)}), f32[8,2,32,128]{3,2,1,0:T(8,128)S(1)}, u32[]{:S(2)}, u32[]{:S(2)}) %all-to-all-start.2) | async-done | bytes 262176 | tf_op jit(solution)/shard_map/all_to_all | solution.py:328
  52.8 2.1 %shard_map.89 = (f32[1024,256]{1,0:T(8,128)}, f32[128,256]{1,0:T(8,128)S(1)}) custom-call(s32[1]{0:T(128)} %bitcast.half_ref, f32[1024,256]{1,0:T(8,128)} %bitcast.47, f32[512,128]{1,0:T(8,128)S(1)} %bitcast.42, f32[256,128]{1,0:T(8,128)S(1)} %copy-done.2), custom_call_target="tpu_custom_call", output_to_operand_aliasing={{0}: (1, {})} | custom-call | tf_op jit(solution)/shard_map/pallas_call | solution.py:210
  54.9 2.4 %shard_map.90 = (f32[1024,256]{1,0:T(8,128)}, f32[8,128,128]{2,1,0:T(8,128)}) custom-call(s32[1]{0:T(128)S(6)} %sub.10.half_ref, f32[1024,256]{1,0:T(8,128)} %get-tuple-element.38._, f32[512,128]{1,0:T(8,128)S(1)} %collective-permute-done.7.after_ref, f32[256,128]{1,0:T(8,128)S(1)} %copy-done.2, ...), custom_call_target="tpu_custom_call", output_to_operand_aliasing={{0}: (1, {}), {1}: (5, {})} | custom-call | tf_op jit(solution)/shard_map/pallas_call | solution.py:233
  57.4 3.7 %all-to-all-start.3 = ((f32[8,128,128]{2,1,0:T(8,128)}), f32[8,128,128]{2,1,0:T(8,128)S(1)}, u32[]{:S(2)}, u32[]{:S(2)}) async-start(f32[8,128,128]{2,1,0:T(8,128)} %get-tuple-element.42), calls=%async_computation.3 | async-start | bytes 1048576 | tf_op jit(solution)/shard_map/all_to_all | solution.py:336
  61.6 1.5 %collective-permute-done.8.own_other_ref = f32[16,64,128]{2,1,0:T(8,128)S(1)} collective-permute-done((f32[16,64,128]{2,1,0:T(8,128)S(1)}, f32[16,64,128]{2,1,0:T(8,128)S(1)}, u32[]{:S(2)}, u32[]{:S(2)}) %collective-permute-start.8) | collective-permute-done | bytes 524320 | tf_op jit(solution)/shard_map/ppermute | solution.py:29
  63.1 1.5 %collective-permute-start.9 = (f32[16,64,128]{2,1,0:T(8,128)S(1)}, f32[16,64,128]{2,1,0:T(8,128)S(1)}, u32[]{:S(2)}, u32[]{:S(2)}) collective-permute-start(f32[16,64,128]{2,1,0:T(8,128)S(1)} %collective-permute-done.8.own_other_ref), channel_id=1, source_target_pairs={{0,16},{16,0},{1,17},{17,1},{2,18},{18,2},{3,19},{19,3},{4,20},{20... | collective-permute-start | bytes 1572872 | tf_op jit(solution)/shard_map/ppermute | solution.py:29
  64.6 11.8 %all-to-all-done.3.late_ref = f32[8,128,128]{2,1,0:T(8,128)S(1)} async-done(((f32[8,128,128]{2,1,0:T(8,128)}), f32[8,128,128]{2,1,0:T(8,128)S(1)}, u32[]{:S(2)}, u32[]{:S(2)}) %all-to-all-start.3) | async-done | bytes 524320 | tf_op jit(solution)/shard_map/all_to_all | solution.py:336
  76.4 1.5 %collective-permute-start.11 = (f32[64,128]{1,0:T(8,128)S(1)}, f32[64,128]{1,0:T(8,128)S(1)}, u32[]{:S(2)}, u32[]{:S(2)}) collective-permute-start(f32[64,128]{1,0:T(8,128)S(1)} %slice_reduce_fusion), channel_id=1, source_target_pairs={{0,16},{16,0},{1,17},{17,1},{2,18},{18,2},{3,19},{19,3},{4,20},{20... | collective-permute-start | bytes 98312 | tf_op jit(solution)/shard_map/ppermute | solution.py:29
  77.9 1.8 %shard_map.91 = (f32[32,128]{1,0:T(8,128)S(1)}, f32[32,128]{1,0:T(8,128)S(1)}) custom-call(s32[2]{0:T(128)S(1)} %pad_add_fusion.place_ref, f32[8,128,128]{2,1,0:T(8,128)S(1)} %all-to-all-done.3.late_ref, f32[16,64,128]{2,1,0:T(8,128)S(1)} %get-tuple-element.49.own_mine_ref, f32[16,64,128]{2,1,0:T(8,128)S(1)} %collective-permute-done.8.own_other_ref, ...), custom_call_target="tpu_custom_call" | custom-call | tf_op jit(solution)/shard_map/pallas_call | solution.py:270
  81.7 5.3 %all-to-all-start.4 = ((f32[8,64,128]{2,1,0:T(8,128)}), f32[8,64,128]{2,1,0:T(8,128)S(1)}, u32[]{:S(2)}, u32[]{:S(2)}) async-start(f32[8,64,128]{2,1,0:T(8,128)} %broadcast_in_dim.5), calls=%async_computation.4 | async-start | bytes 524288 | tf_op jit(solution)/shard_map/all_to_all | solution.py:349
  88.9 7.4 %all-to-all-done.4 = f32[8,64,128]{2,1,0:T(8,128)S(1)} async-done(((f32[8,64,128]{2,1,0:T(8,128)}), f32[8,64,128]{2,1,0:T(8,128)S(1)}, u32[]{:S(2)}, u32[]{:S(2)}) %all-to-all-start.4) | async-done | bytes 262176 | tf_op jit(solution)/shard_map/all_to_all | solution.py:349
  (61 shorter events, 15.6 us)
Async XLA Ops:
  0.6 5.0 %copy-start = (f32[32,256]{1,0:T(8,128)S(1)}, f32[32,256]{1,0:T(8,128)}, u32[]{:S(2)}) copy-start(f32[32,256]{1,0:T(8,128)} %param.8) | copy-start | bytes 98308
  0.6 1.3 %copy-start.2 = (f32[256,128]{1,0:T(8,128)S(1)}, f32[256,128]{1,0:T(8,128)}, u32[]{:S(2)}) copy-start(f32[256,128]{1,0:T(8,128)} %factor_ref.3) | copy-start | bytes 393220
  1.9 3.7 %copy-start.3 = (f32[32,32,256]{2,1,0:T(8,128)}, f32[32,32,256]{2,1,0:T(8,128)S(1)}, u32[]{:S(2)}) copy-start(f32[32,32,256]{2,1,0:T(8,128)S(1)} %copy.16) | copy-start | bytes 3145732
  2.5 3.1 %collective-permute-start = (f32[512,128]{1,0:T(8,128)S(1)}, f32[512,128]{1,0:T(8,128)S(1)}, u32[]{:S(2)}, u32[]{:S(2)}) collective-permute-start(f32[512,128]{1,0:T(8,128)S(1)} %fusion.1), channel_id=1, source_target_pairs={{0,1},{1,0},{2,3},{3,2},{4,5},{5,4},{6,7},{7,6},{8,9},{9,8},{10,11... | collective-permute-start | bytes 786440 | tf_op jit(solution)/shard_map/ppermute | solution.py:29
  3.0 4.3 %collective-permute-start.1 = (f32[32,128]{1,0:T(8,128)S(1)}, f32[32,128]{1,0:T(8,128)S(1)}, u32[]{:S(2)}, u32[]{:S(2)}) collective-permute-start(f32[32,128]{1,0:T(8,128)S(1)} %get-tuple-element.59), channel_id=1, source_target_pairs={{0,16},{16,0},{1,17},{17,1},{2,18},{18,2},{3,19},{19,3},{4,20},{20... | collective-permute-start | bytes 49160 | tf_op jit(solution)/shard_map/ppermute | solution.py:29
  6.3 7.5 %copy-start.1 = (f32[128,32,64]{0,2,1:T(8,128)S(1)}, f32[128,32,64]{0,2,1:T(8,128)}, u32[]{:S(2)}) copy-start(f32[128,32,64]{0,2,1:T(8,128)} %param.6) | copy-start | bytes 3145732
  7.3 17.6 %all-to-all-start = ((f32[8,96,128]{2,1,0:T(8,128)}), f32[8,96,128]{2,1,0:T(8,128)S(1)}, u32[]{:S(2)}, u32[]{:S(2)}) async-start(f32[8,96,128]{2,1,0:T(8,128)} %pad_maximum_fusion), calls=%async_computation | async-start | bytes 786432 | tf_op jit(solution)/shard_map/all_to_all | solution.py:313
  14.9 7.3 %collective-permute-start.2 = (f32[32,16,128]{2,1,0:T(8,128)S(1)}, f32[32,16,128]{2,1,0:T(8,128)S(1)}, u32[]{:S(2)}, u32[]{:S(2)}) collective-permute-start(f32[32,16,128]{2,1,0:T(8,128)S(1)} %shard_map.85), channel_id=1, source_target_pairs={{0,16},{16,0},{1,17},{17,1},{2,18},{18,2},{3,19},{19,3},{4,20},{20... | collective-permute-start | bytes 786440 | tf_op jit(solution)/shard_map/ppermute | solution.py:29
  24.9 14.2 %all-to-all-start.1 = ((f32[16,32,128]{2,1,0:T(8,128)}), f32[16,32,128]{2,1,0:T(8,128)S(1)}, u32[]{:S(2)}, u32[]{:S(2)}) async-start(f32[16,32,128]{2,1,0:T(8,128)} %bitcast.10), calls=%async_computation.1 | async-start | bytes 524288 | tf_op jit(solution)/shard_map/all_to_all | solution.py:324
  29.2 3.1 %collective-permute-start.3 = (f32[128,128]{1,0:T(8,128)S(1)}, f32[128,128]{1,0:T(8,128)S(1)}, u32[]{:S(2)}, u32[]{:S(2)}) collective-permute-start(f32[128,128]{1,0:T(8,128)S(1)} %fusion.9.gram_ref), channel_id=1, source_target_pairs={{0,1},{1,0},{2,3},{3,2},{4,5},{5,4},{6,7},{7,6},{8,9},{9,8},{10,11... | collective-permute-start | bytes 196616 | tf_op jit(solution)/shard_map/ppermute | solution.py:29
  29.6 9.5 %collective-permute-start.4 = (f32[8,2,16,128]{3,2,1,0:T(8,128)S(1)}, f32[8,2,16,128]{3,2,1,0:T(8,128)S(1)}, u32[]{:S(2)}, u32[]{:S(2)}) collective-permute-start(f32[8,2,16,128]{3,2,1,0:T(8,128)S(1)} %bitcast.43), channel_id=1, source_target_pairs={{0,1},{1,0},{2,3},{3,2},{4,5},{5,4},{6,7},{7,6},{8,9},{9,8},{10,11... | collective-permute-start | bytes 393224 | tf_op jit(solution)/shard_map/ppermute | solution.py:29
  30.7 18.6 %collective-permute-start.6 = (f32[16,64,128]{2,1,0:T(8,128)S(1)}, f32[16,64,128]{2,1,0:T(8,128)S(1)}, u32[]{:S(2)}, u32[]{:S(2)}) collective-permute-start(f32[16,64,128]{2,1,0:T(8,128)S(1)} %get-tuple-element.49.own_mine_ref), channel_id=1, source_target_pairs={{0,16},{16,0},{1,17},{17,1},{2,18},{18,2},{3,19},{19,3},{4,20},{20... | collective-permute-start | bytes 1572872 | tf_op jit(solution)/shard_map/ppermute | solution.py:29
  40.9 12.0 %all-to-all-start.2 = ((f32[8,2,32,128]{3,2,1,0:T(8,128)}), f32[8,2,32,128]{3,2,1,0:T(8,128)S(1)}, u32[]{:S(2)}, u32[]{:S(2)}) async-start(f32[8,2,32,128]{3,2,1,0:T(8,128)} %get-tuple-element.31.moved_ref), calls=%async_computation.2 | async-start | bytes 524288 | tf_op jit(solution)/shard_map/all_to_all | solution.py:328
  46.9 1.6 %collective-permute-start.5 = (f32[8,64,128]{2,1,0:T(8,128)S(1)}, f32[8,64,128]{2,1,0:T(8,128)S(1)}, u32[]{:S(2)}, u32[]{:S(2)}) collective-permute-start(f32[8,64,128]{2,1,0:T(8,128)S(1)} %get-tuple-element.36), channel_id=1, source_target_pairs={{0,1},{1,0},{2,3},{3,2},{4,5},{5,4},{6,7},{7,6},{8,9},{9,8},{10,11... | collective-permute-start | bytes 786440 | tf_op jit(solution)/shard_map/ppermute | solution.py:29
  52.8 2.1 %collective-permute-start.7 = (f32[512,128]{1,0:T(8,128)S(1)}, f32[512,128]{1,0:T(8,128)S(1)}, u32[]{:S(2)}, u32[]{:S(2)}) collective-permute-start(f32[512,128]{1,0:T(8,128)S(1)} %bitcast.41), channel_id=1, source_target_pairs={{0,1},{1,0},{2,3},{3,2},{4,5},{5,4},{6,7},{7,6},{8,9},{9,8},{10,11... | collective-permute-start | bytes 786440 | tf_op jit(solution)/shard_map/ppermute | solution.py:29
  57.4 3.7 %copy-start.4 = (f32[16,64,128]{2,1,0:T(8,128)S(1)}, f32[16,64,128]{2,1,0:T(8,128)}, u32[]{:S(2)}) copy-start(f32[16,64,128]{2,1,0:T(8,128)} %get-tuple-element.48) | copy-start | bytes 1572868
  57.4 19.0 %all-to-all-start.3 = ((f32[8,128,128]{2,1,0:T(8,128)}), f32[8,128,128]{2,1,0:T(8,128)S(1)}, u32[]{:S(2)}, u32[]{:S(2)}) async-start(f32[8,128,128]{2,1,0:T(8,128)} %get-tuple-element.42), calls=%async_computation.3 | async-start | bytes 1048576 | tf_op jit(solution)/shard_map/all_to_all | solution.py:336
  61.1 2.1 %collective-permute-start.8 = (f32[16,64,128]{2,1,0:T(8,128)S(1)}, f32[16,64,128]{2,1,0:T(8,128)S(1)}, u32[]{:S(2)}, u32[]{:S(2)}) collective-permute-start(f32[16,64,128]{2,1,0:T(8,128)S(1)} %copy-done.4), channel_id=1, source_target_pairs={{0,1},{1,0},{2,3},{3,2},{4,5},{5,4},{6,7},{7,6},{8,9},{9,8},{10,11... | collective-permute-start | bytes 1572872 | tf_op jit(solution)/shard_map/ppermute | solution.py:29
  63.1 14.8 %collective-permute-start.9 = (f32[16,64,128]{2,1,0:T(8,128)S(1)}, f32[16,64,128]{2,1,0:T(8,128)S(1)}, u32[]{:S(2)}, u32[]{:S(2)}) collective-permute-start(f32[16,64,128]{2,1,0:T(8,128)S(1)} %collective-permute-done.8.own_other_ref), channel_id=1, source_target_pairs={{0,16},{16,0},{1,17},{17,1},{2,18},{18,2},{3,19},{19,3},{4,20},{20... | collective-permute-start | bytes 1572872 | tf_op jit(solution)/shard_map/ppermute | solution.py:29
  76.4 4.6 %collective-permute-start.11 = (f32[64,128]{1,0:T(8,128)S(1)}, f32[64,128]{1,0:T(8,128)S(1)}, u32[]{:S(2)}, u32[]{:S(2)}) collective-permute-start(f32[64,128]{1,0:T(8,128)S(1)} %slice_reduce_fusion), channel_id=1, source_target_pairs={{0,16},{16,0},{1,17},{17,1},{2,18},{18,2},{3,19},{19,3},{4,20},{20... | collective-permute-start | bytes 98312 | tf_op jit(solution)/shard_map/ppermute | solution.py:29
  79.7 1.2 %collective-permute-start.10 = (f32[32,128]{1,0:T(8,128)S(1)}, f32[32,128]{1,0:T(8,128)S(1)}, u32[]{:S(2)}, u32[]{:S(2)}) collective-permute-start(f32[32,128]{1,0:T(8,128)S(1)} %get-tuple-element.45), channel_id=1, source_target_pairs={{0,1},{1,0},{2,3},{3,2},{4,5},{5,4},{6,7},{7,6},{8,9},{9,8},{10,11... | collective-permute-start | bytes 49160 | tf_op jit(solution)/shard_map/ppermute | solution.py:29
  81.7 14.5 %all-to-all-start.4 = ((f32[8,64,128]{2,1,0:T(8,128)}), f32[8,64,128]{2,1,0:T(8,128)S(1)}, u32[]{:S(2)}, u32[]{:S(2)}) async-start(f32[8,64,128]{2,1,0:T(8,128)} %broadcast_in_dim.5), calls=%async_computation.4 | async-start | bytes 524288 | tf_op jit(solution)/shard_map/all_to_all | solution.py:349
  87.0 1.2 %collective-permute-start.12 = (f32[16,256]{1,0:T(8,128)S(1)}, f32[16,256]{1,0:T(8,128)S(1)}, u32[]{:S(2)}, u32[]{:S(2)}) collective-permute-start(f32[16,256]{1,0:T(8,128)S(1)} %pad_maximum_fusion.3), channel_id=1, source_target_pairs={{0,1},{1,0},{2,3},{3,2},{4,5},{5,4},{6,7},{7,6},{8,9},{9,8},{10,11... | collective-permute-start | bytes 49160 | tf_op jit(solution)/shard_map/ppermute | solution.py:29
  96.9 1.2 %collective-permute-start.13 = (f32[32,128]{1,0:T(8,128)S(1)}, f32[32,128]{1,0:T(8,128)S(1)}, u32[]{:S(2)}, u32[]{:S(2)}) collective-permute-start(f32[32,128]{1,0:T(8,128)S(1)} %get-tuple-element.51), channel_id=1, source_target_pairs={{0,1},{1,0},{2,3},{3,2},{4,5},{5,4},{6,7},{7,6},{8,9},{9,8},{10,11... | collective-permute-start | bytes 49160 | tf_op jit(solution)/shard_map/ppermute | solution.py:29
  (1 other events, 1.1 us)

commit v9 on v7

--- a/solution.py
+++ b/solution.py
@@ -78,17 +78,31 @@
     )(rows, core)
 
 
-def mode_two(place, arrived, mine, other, e, t):
-    nz, ny, rows, wide = arrived.shape
-    q, halves, half_j, full_s = rows // e, wide // t, mine.shape[2], mine.shape[1] * wide
-    j = nz * half_j
-
-    def body(place_ref, arrived_ref, mine_ref, other_ref, one_ref, two_ref, moved_ref):
+def order_two(place, mine, other):
+    ny, parts, half_j, wide = mine.shape
+
+    def body(place_ref, mine_ref, other_ref, two_ref):
         me = place_ref[0]
-        for c in range(mine_ref.shape[1]):
+        for c in range(parts):
             here = pl.ds(c * wide, wide)
             two_ref[:, pl.ds(me, 1), :, here] = mine_ref[:, c][:, None]
             two_ref[:, pl.ds(1 - me, 1), :, here] = other_ref[:, c][:, None]
+
+    return pl.pallas_call(
+        body,
+        out_shape=shape(ny, 2, half_j, parts * wide),
+        in_specs=[smem, vmem, vmem],
+        out_specs=vmem,
+        compiler_params=params,
+    )(place, mine, other)
+
+
+def mode_two(arrived, two, e, t):
+    nz, ny, rows, wide = arrived.shape
+    q, halves, half_j, full_s = rows // e, wide // t, two.shape[2], two.shape[3]
+    j = nz * half_j
+
+    def body(arrived_ref, two_ref, one_ref, moved_ref):
         for n in range(e):
             for h in range(halves):
                 pieces = [arrived_ref[z, :, pl.ds(n * q, q), pl.ds(h * t, t)] for z in range(nz)]
@@ -99,14 +113,13 @@
         for n in range(e):
             moved_ref[:, n] = after[:, n * wide : (n + 1) * wide].reshape(ny, j, wide)
 
-    one, two = (ny, halves, q, e * wide), (ny, nz, half_j, full_s)
-    return pl.pallas_call(
-        body,
-        out_shape=[shape(*one), shape(*two), shape(ny, e, j, wide)],
-        in_specs=[smem, vmem, vmem, vmem],
-        out_specs=[vmem] * 3,
-        compiler_params=params,
-    )(place, arrived, mine, other)
+    return pl.pallas_call(
+        body,
+        out_shape=[shape(ny, halves, q, e * wide), shape(ny, e, j, wide)],
+        in_specs=[vmem, vmem],
+        out_specs=[vmem] * 2,
+        compiler_params=params,
+    )(arrived, two)
 
 
 def back(place, moved, gram, gram_other, early, one, two):
@@ -322,8 +335,10 @@
         own_mine, own_other = part(flat, gz), swap(part(flat, 1 - gz), "gz")
         near_mine = swap(own_mine, "gx")
     after_one = lax.all_to_all(after_one.reshape(nz * ny, e * q, full_t), ("gz", "gy"), 0, 0, tiled=True)
+    two = order_two(place, mine_two, other_two)
+    after_one, gram_other, two = lax.optimization_barrier((after_one, gram_other, two))
     after_one = after_one.reshape(nz, ny, e * q, full_t)
-    one, two, moved = mode_two(place, after_one, mine_two, other_two, e, t)
+    one, moved = mode_two(after_one, two, e, t)
     home = lax.all_to_all(moved, "gy", 0, 0, tiled=True).reshape(rows // nz, full_t)
     edge, parts = e * q, full_s // full_t
     keep, send = back(place, moved, gram, gram_other, early, one, two)

time: 100 us -> 98.8 us (0.988)
  starting transfers between devices: 33.9 us -> 32.9 us
    all_to_all x1, waiting for transfers between devices: 1.84 us -> 3.54 us  [local(): lax.all_to_all(moved, 'gy', 0, 0, tiled=True).reshape(rows // nz, full_t)]
    ppermute x14, waiting for transfers between devices: 12.9 us -> 11.5 us  [swap(): return lax.ppermute(x, axis, [(0, 1), (1, 0)])]
  transfers between devices with their start and end apart: 19 -> 19, of which waited for: 13 -> 12; matrix products, arithmetic and copies ran while one was open for 4% -> 3% of each run, Pallas kernels for 11% -> 12%
where the time goes in v9:
time: 98.8 us; the launch traced here: 98 us
  waiting for transfers between devices  43.2 us (44%)
  starting transfers between devices  32.9 us (33%)
  Pallas kernels  13.7 us (14%)
  other arithmetic  3.55 us (4%)
  local copies, waits for them, and re-layouts  2.14 us (2%)
  matrix products  1.55 us (2%)
    all_to_all x1, waiting for transfers between devices, local(): late = lax.all_to_all(late, 'gy', 0, 0, tiled=True)  11.8 us
    ppermute x14, waiting for transfers between devices, swap(): return lax.ppermute(x, axis, [(0, 1), (1, 0)])  11.5 us
    ppermute x14, starting transfers between devices, swap(): return lax.ppermute(x, axis, [(0, 1), (1, 0)])  10.5 us
    all_to_all x1, waiting for transfers between devices, local(): lax.all_to_all(jnp.broadcast_to(last[None], (ny,) + last.shape), 'gy', 0,...  7.36 us
    all_to_all x1, waiting for transfers between devices, local(): lax.all_to_all(after_one.reshape(nz * ny, e * q, full_t), ('gz', 'gy'), 0...  7.05 us
    all_to_all x1, starting transfers between devices, local(): early = lax.all_to_all(early, 'gy', 0, 0, tiled=True)  6.37 us
    all_to_all x1, starting transfers between devices, local(): lax.all_to_all(jnp.broadcast_to(last[None], (ny,) + last.shape), 'gy', 0,...  5.25 us
    all_to_all x1, starting transfers between devices, local(): lax.all_to_all(after_one.reshape(nz * ny, e * q, full_t), ('gz', 'gy'), 0...  3.83 us
  transfers between devices with their start and end apart: 19, of which 12 were waited for; matrix products, arithmetic and copies ran while one was open for 3% of the time, Pallas kernels for 12%

profile of v9, /device:TPU:0, one launch (start us, length us, event | category | flops | bytes accessed | tf_op | source)
XLA Modules:
  0.0 98.0 jit_solution(13935747014194705782)
XLA Ops:
  0.7 1.3 %copy.16 = f32[32,32,256]{2,1,0:T(8,128)S(1)} copy(f32[32,32,256]{2,1,0:T(8,128)} %param.5) | data formatting | bytes 2097152
  3.0 2.6 %collective-permute-start.1 = (f32[32,128]{1,0:T(8,128)S(1)}, f32[32,128]{1,0:T(8,128)S(1)}, u32[]{:S(2)}, u32[]{:S(2)}) collective-permute-start(f32[32,128]{1,0:T(8,128)S(1)} %get-tuple-element.59), channel_id=1, source_target_pairs={{0,16},{16,0},{1,17},{17,1},{2,18},{18,2},{3,19},{19,3},{4,20},{20... | collective-permute-start | bytes 49160 | tf_op jit(solution)/shard_map/ppermute | solution.py:29
  7.3 6.4 %all-to-all-start = ((f32[8,96,128]{2,1,0:T(8,128)}), f32[8,96,128]{2,1,0:T(8,128)S(1)}, u32[]{:S(2)}, u32[]{:S(2)}) async-start(f32[8,96,128]{2,1,0:T(8,128)} %pad_maximum_fusion), calls=%async_computation | async-start | bytes 786432 | tf_op jit(solution)/shard_map/all_to_all | solution.py:326
  14.9 1.6 %collective-permute-start.2 = (f32[32,16,128]{2,1,0:T(8,128)S(1)}, f32[32,16,128]{2,1,0:T(8,128)S(1)}, u32[]{:S(2)}, u32[]{:S(2)}) collective-permute-start(f32[32,16,128]{2,1,0:T(8,128)S(1)} %shard_map.85), channel_id=1, source_target_pairs={{0,16},{16,0},{1,17},{17,1},{2,18},{18,2},{3,19},{19,3},{4,20},{20... | collective-permute-start | bytes 786440 | tf_op jit(solution)/shard_map/ppermute | solution.py:29
  17.6 4.6 %collective-permute-done.2 = f32[32,16,128]{2,1,0:T(8,128)S(1)} collective-permute-done((f32[32,16,128]{2,1,0:T(8,128)S(1)}, f32[32,16,128]{2,1,0:T(8,128)S(1)}, u32[]{:S(2)}, u32[]{:S(2)}) %collective-permute-start.2) | collective-permute-done | bytes 262176 | tf_op jit(solution)/shard_map/ppermute | solution.py:29
  22.9 2.0 %all-to-all-done.early_ref = f32[8,96,128]{2,1,0:T(8,128)S(1)} async-done(((f32[8,96,128]{2,1,0:T(8,128)}), f32[8,96,128]{2,1,0:T(8,128)S(1)}, u32[]{:S(2)}, u32[]{:S(2)}) %all-to-all-start) | async-done | bytes 393248 | tf_op jit(solution)/shard_map/all_to_all | solution.py:326
  24.9 3.8 %all-to-all-start.1 = ((f32[16,32,128]{2,1,0:T(8,128)}), f32[16,32,128]{2,1,0:T(8,128)S(1)}, u32[]{:S(2)}, u32[]{:S(2)}) async-start(f32[16,32,128]{2,1,0:T(8,128)} %bitcast.9), calls=%async_computation.1 | async-start | bytes 524288 | tf_op jit(solution)/shard_map/all_to_all | solution.py:337
  29.9 1.5 %collective-permute-start.6 = (f32[16,64,128]{2,1,0:T(8,128)S(1)}, f32[16,64,128]{2,1,0:T(8,128)S(1)}, u32[]{:S(2)}, u32[]{:S(2)}) collective-permute-start(f32[16,64,128]{2,1,0:T(8,128)S(1)} %get-tuple-element.49.own_mine_ref), channel_id=1, source_target_pairs={{0,16},{16,0},{1,17},{17,1},{2,18},{18,2},{3,19},{19,3},{4,20},{20... | collective-permute-start | bytes 1572872 | tf_op jit(solution)/shard_map/ppermute | solution.py:29
  32.1 7.1 %all-to-all-done.1 = f32[16,32,128]{2,1,0:T(8,128)S(1)} async-done(((f32[16,32,128]{2,1,0:T(8,128)}), f32[16,32,128]{2,1,0:T(8,128)S(1)}, u32[]{:S(2)}, u32[]{:S(2)}) %all-to-all-start.1) | async-done | bytes 262176 | tf_op jit(solution)/shard_map/all_to_all | solution.py:337
  40.3 3.4 %all-to-all-start.2 = ((f32[8,2,32,128]{3,2,1,0:T(8,128)}), f32[8,2,32,128]{3,2,1,0:T(8,128)S(1)}, u32[]{:S(2)}, u32[]{:S(2)}) async-start(f32[8,2,32,128]{3,2,1,0:T(8,128)} %get-tuple-element.32.moved_ref), calls=%async_computation.2 | async-start | bytes 524288 | tf_op jit(solution)/shard_map/all_to_all | solution.py:342
  43.7 2.6 %shard_map.88 = (f32[8,64,128]{2,1,0:T(8,128)S(1)}, f32[8,64,128]{2,1,0:T(8,128)S(1)}) custom-call(s32[2]{0:T(128)S(1)} %pad_add_fusion.place_ref, f32[8,2,32,128]{3,2,1,0:T(8,128)} %get-tuple-element.32.moved_ref, f32[128,128]{1,0:T(8,128)S(1)} %fusion.9.gram_ref, f32[128,128]{1,0:T(8,128)S(1)} %collective-permute-done.3.gram_other_ref, ...), custom_call_target="tpu_custom_call" | custom-call | flops 1000000000 | bytes 2097152 | tf_op jit(solution)/shard_map/pallas_call | solution.py:153
  46.4 1.5 %collective-permute-done.5.arrived_ref = f32[8,64,128]{2,1,0:T(8,128)S(1)} collective-permute-done((f32[8,64,128]{2,1,0:T(8,128)S(1)}, f32[8,64,128]{2,1,0:T(8,128)S(1)}, u32[]{:S(2)}, u32[]{:S(2)}) %collective-permute-start.5) | collective-permute-done | bytes 262176 | tf_op jit(solution)/shard_map/ppermute | solution.py:29
  48.7 3.5 %all-to-all-done.2 = f32[8,2,32,128]{3,2,1,0:T(8,128)S(1)} async-done(((f32[8,2,32,128]{3,2,1,0:T(8,128)}), f32[8,2,32,128]{3,2,1,0:T(8,128)S(1)}, u32[]{:S(2)}, u32[]{:S(2)}) %all-to-all-start.2) | async-done | bytes 262176 | tf_op jit(solution)/shard_map/all_to_all | solution.py:342
  52.3 2.1 %shard_map.90 = (f32[1024,256]{1,0:T(8,128)}, f32[128,256]{1,0:T(8,128)S(1)}) custom-call(s32[1]{0:T(128)} %bitcast.half_ref, f32[1024,256]{1,0:T(8,128)} %bitcast.47, f32[512,128]{1,0:T(8,128)S(1)} %bitcast.42, f32[256,128]{1,0:T(8,128)S(1)} %copy-done.2), custom_call_target="tpu_custom_call", output_to_operand_aliasing={{0}: (1, {})} | custom-call | tf_op jit(solution)/shard_map/pallas_call | solution.py:223
  54.4 2.4 %shard_map.91 = (f32[1024,256]{1,0:T(8,128)}, f32[8,128,128]{2,1,0:T(8,128)}) custom-call(s32[1]{0:T(128)S(6)} %sub.10.half_ref, f32[1024,256]{1,0:T(8,128)} %get-tuple-element.38._, f32[512,128]{1,0:T(8,128)S(1)} %collective-permute-done.7.after_ref, f32[256,128]{1,0:T(8,128)S(1)} %copy-done.2, ...), custom_call_target="tpu_custom_call", output_to_operand_aliasing={{0}: (1, {}), {1}: (5, {})} | custom-call | tf_op jit(solution)/shard_map/pallas_call | solution.py:246
  56.8 3.6 %all-to-all-start.3 = ((f32[8,128,128]{2,1,0:T(8,128)}), f32[8,128,128]{2,1,0:T(8,128)S(1)}, u32[]{:S(2)}, u32[]{:S(2)}) async-start(f32[8,128,128]{2,1,0:T(8,128)} %get-tuple-element.42), calls=%async_computation.3 | async-start | bytes 1048576 | tf_op jit(solution)/shard_map/all_to_all | solution.py:350
  60.9 1.5 %collective-permute-done.8.own_other_ref = f32[16,64,128]{2,1,0:T(8,128)S(1)} collective-permute-done((f32[16,64,128]{2,1,0:T(8,128)S(1)}, f32[16,64,128]{2,1,0:T(8,128)S(1)}, u32[]{:S(2)}, u32[]{:S(2)}) %collective-permute-start.8) | collective-permute-done | bytes 524320 | tf_op jit(solution)/shard_map/ppermute | solution.py:29
  62.4 1.5 %collective-permute-start.9 = (f32[16,64,128]{2,1,0:T(8,128)S(1)}, f32[16,64,128]{2,1,0:T(8,128)S(1)}, u32[]{:S(2)}, u32[]{:S(2)}) collective-permute-start(f32[16,64,128]{2,1,0:T(8,128)S(1)} %collective-permute-done.8.own_other_ref), channel_id=1, source_target_pairs={{0,16},{16,0},{1,17},{17,1},{2,18},{18,2},{3,19},{19,3},{4,20},{20... | collective-permute-start | bytes 1572872 | tf_op jit(solution)/shard_map/ppermute | solution.py:29
  63.9 11.8 %all-to-all-done.3.late_ref = f32[8,128,128]{2,1,0:T(8,128)S(1)} async-done(((f32[8,128,128]{2,1,0:T(8,128)}), f32[8,128,128]{2,1,0:T(8,128)S(1)}, u32[]{:S(2)}, u32[]{:S(2)}) %all-to-all-start.3) | async-done | bytes 524320 | tf_op jit(solution)/shard_map/all_to_all | solution.py:350
  75.7 1.5 %collective-permute-start.11 = (f32[64,128]{1,0:T(8,128)S(1)}, f32[64,128]{1,0:T(8,128)S(1)}, u32[]{:S(2)}, u32[]{:S(2)}) collective-permute-start(f32[64,128]{1,0:T(8,128)S(1)} %slice_reduce_fusion), channel_id=1, source_target_pairs={{0,16},{16,0},{1,17},{17,1},{2,18},{18,2},{3,19},{19,3},{4,20},{20... | collective-permute-start | bytes 98312 | tf_op jit(solution)/shard_map/ppermute | solution.py:29
  77.2 1.8 %shard_map.92 = (f32[32,128]{1,0:T(8,128)S(1)}, f32[32,128]{1,0:T(8,128)S(1)}) custom-call(s32[2]{0:T(128)S(1)} %pad_add_fusion.place_ref, f32[8,128,128]{2,1,0:T(8,128)S(1)} %all-to-all-done.3.late_ref, f32[16,64,128]{2,1,0:T(8,128)S(1)} %get-tuple-element.49.own_mine_ref, f32[16,64,128]{2,1,0:T(8,128)S(1)} %collective-permute-done.8.own_other_ref, ...), custom_call_target="tpu_custom_call" | custom-call | tf_op jit(solution)/shard_map/pallas_call | solution.py:283
  81.0 5.3 %all-to-all-start.4 = ((f32[8,64,128]{2,1,0:T(8,128)}), f32[8,64,128]{2,1,0:T(8,128)S(1)}, u32[]{:S(2)}, u32[]{:S(2)}) async-start(f32[8,64,128]{2,1,0:T(8,128)} %broadcast_in_dim.5), calls=%async_computation.4 | async-start | bytes 524288 | tf_op jit(solution)/shard_map/all_to_all | solution.py:363
  88.2 7.4 %all-to-all-done.4 = f32[8,64,128]{2,1,0:T(8,128)S(1)} async-done(((f32[8,64,128]{2,1,0:T(8,128)}), f32[8,64,128]{2,1,0:T(8,128)S(1)}, u32[]{:S(2)}, u32[]{:S(2)}) %all-to-all-start.4) | async-done | bytes 262176 | tf_op jit(solution)/shard_map/all_to_all | solution.py:363
  96.2 1.2 %collective-permute-done.13 = f32[32,128]{1,0:T(8,128)S(1)} collective-permute-done((f32[32,128]{1,0:T(8,128)S(1)}, f32[32,128]{1,0:T(8,128)S(1)}, u32[]{:S(2)}, u32[]{:S(2)}) %collective-permute-start.13) | collective-permute-done | bytes 16416 | tf_op jit(solution)/shard_map/ppermute | solution.py:29
  (60 shorter events, 15.3 us)
Async XLA Ops:
  0.6 5.0 %copy-start = (f32[32,256]{1,0:T(8,128)S(1)}, f32[32,256]{1,0:T(8,128)}, u32[]{:S(2)}) copy-start(f32[32,256]{1,0:T(8,128)} %param.8) | copy-start | bytes 98308
  0.6 1.3 %copy-start.2 = (f32[256,128]{1,0:T(8,128)S(1)}, f32[256,128]{1,0:T(8,128)}, u32[]{:S(2)}) copy-start(f32[256,128]{1,0:T(8,128)} %factor_ref.3) | copy-start | bytes 393220
  1.9 3.7 %copy-start.3 = (f32[32,32,256]{2,1,0:T(8,128)}, f32[32,32,256]{2,1,0:T(8,128)S(1)}, u32[]{:S(2)}) copy-start(f32[32,32,256]{2,1,0:T(8,128)S(1)} %copy.16) | copy-start | bytes 3145732
  1.9 1.1 %copy-start.4 = (f32[32,256]{1,0:T(8,128)S(1)}, f32[32,256]{1,0:T(8,128)}, u32[]{:S(2)}) copy-start(f32[32,256]{1,0:T(8,128)} %param.7) | copy-start | bytes 98308
  2.5 3.1 %collective-permute-start = (f32[512,128]{1,0:T(8,128)S(1)}, f32[512,128]{1,0:T(8,128)S(1)}, u32[]{:S(2)}, u32[]{:S(2)}) collective-permute-start(f32[512,128]{1,0:T(8,128)S(1)} %fusion.1), channel_id=1, source_target_pairs={{0,1},{1,0},{2,3},{3,2},{4,5},{5,4},{6,7},{7,6},{8,9},{9,8},{10,11... | collective-permute-start | bytes 786440 | tf_op jit(solution)/shard_map/ppermute | solution.py:29
  3.0 4.3 %collective-permute-start.1 = (f32[32,128]{1,0:T(8,128)S(1)}, f32[32,128]{1,0:T(8,128)S(1)}, u32[]{:S(2)}, u32[]{:S(2)}) collective-permute-start(f32[32,128]{1,0:T(8,128)S(1)} %get-tuple-element.59), channel_id=1, source_target_pairs={{0,16},{16,0},{1,17},{17,1},{2,18},{18,2},{3,19},{19,3},{4,20},{20... | collective-permute-start | bytes 49160 | tf_op jit(solution)/shard_map/ppermute | solution.py:29
  6.3 7.5 %copy-start.1 = (f32[128,32,64]{0,2,1:T(8,128)S(1)}, f32[128,32,64]{0,2,1:T(8,128)}, u32[]{:S(2)}) copy-start(f32[128,32,64]{0,2,1:T(8,128)} %param.6) | copy-start | bytes 3145732
  7.3 17.6 %all-to-all-start = ((f32[8,96,128]{2,1,0:T(8,128)}), f32[8,96,128]{2,1,0:T(8,128)S(1)}, u32[]{:S(2)}, u32[]{:S(2)}) async-start(f32[8,96,128]{2,1,0:T(8,128)} %pad_maximum_fusion), calls=%async_computation | async-start | bytes 786432 | tf_op jit(solution)/shard_map/all_to_all | solution.py:326
  14.9 7.3 %collective-permute-start.2 = (f32[32,16,128]{2,1,0:T(8,128)S(1)}, f32[32,16,128]{2,1,0:T(8,128)S(1)}, u32[]{:S(2)}, u32[]{:S(2)}) collective-permute-start(f32[32,16,128]{2,1,0:T(8,128)S(1)} %shard_map.85), channel_id=1, source_target_pairs={{0,16},{16,0},{1,17},{17,1},{2,18},{18,2},{3,19},{19,3},{4,20},{20... | collective-permute-start | bytes 786440 | tf_op jit(solution)/shard_map/ppermute | solution.py:29
  24.9 14.2 %all-to-all-start.1 = ((f32[16,32,128]{2,1,0:T(8,128)}), f32[16,32,128]{2,1,0:T(8,128)S(1)}, u32[]{:S(2)}, u32[]{:S(2)}) async-start(f32[16,32,128]{2,1,0:T(8,128)} %bitcast.9), calls=%async_computation.1 | async-start | bytes 524288 | tf_op jit(solution)/shard_map/all_to_all | solution.py:337
  29.2 2.9 %collective-permute-start.3 = (f32[128,128]{1,0:T(8,128)S(1)}, f32[128,128]{1,0:T(8,128)S(1)}, u32[]{:S(2)}, u32[]{:S(2)}) collective-permute-start(f32[128,128]{1,0:T(8,128)S(1)} %fusion.9.gram_ref), channel_id=1, source_target_pairs={{0,1},{1,0},{2,3},{3,2},{4,5},{5,4},{6,7},{7,6},{8,9},{9,8},{10,11... | collective-permute-start | bytes 196616 | tf_op jit(solution)/shard_map/ppermute | solution.py:29
  29.6 1.9 %collective-permute-start.4 = (f32[8,2,16,128]{3,2,1,0:T(8,128)S(1)}, f32[8,2,16,128]{3,2,1,0:T(8,128)S(1)}, u32[]{:S(2)}, u32[]{:S(2)}) collective-permute-start(f32[8,2,16,128]{3,2,1,0:T(8,128)S(1)} %bitcast.43), channel_id=1, source_target_pairs={{0,1},{1,0},{2,3},{3,2},{4,5},{5,4},{6,7},{7,6},{8,9},{9,8},{10,11... | collective-permute-start | bytes 393224 | tf_op jit(solution)/shard_map/ppermute | solution.py:29
  29.9 18.8 %collective-permute-start.6 = (f32[16,64,128]{2,1,0:T(8,128)S(1)}, f32[16,64,128]{2,1,0:T(8,128)S(1)}, u32[]{:S(2)}, u32[]{:S(2)}) collective-permute-start(f32[16,64,128]{2,1,0:T(8,128)S(1)} %get-tuple-element.49.own_mine_ref), channel_id=1, source_target_pairs={{0,16},{16,0},{1,17},{17,1},{2,18},{18,2},{3,19},{19,3},{4,20},{20... | collective-permute-start | bytes 1572872 | tf_op jit(solution)/shard_map/ppermute | solution.py:29
  40.3 12.0 %all-to-all-start.2 = ((f32[8,2,32,128]{3,2,1,0:T(8,128)}), f32[8,2,32,128]{3,2,1,0:T(8,128)S(1)}, u32[]{:S(2)}, u32[]{:S(2)}) async-start(f32[8,2,32,128]{3,2,1,0:T(8,128)} %get-tuple-element.32.moved_ref), calls=%async_computation.2 | async-start | bytes 524288 | tf_op jit(solution)/shard_map/all_to_all | solution.py:342
  46.3 1.6 %collective-permute-start.5 = (f32[8,64,128]{2,1,0:T(8,128)S(1)}, f32[8,64,128]{2,1,0:T(8,128)S(1)}, u32[]{:S(2)}, u32[]{:S(2)}) collective-permute-start(f32[8,64,128]{2,1,0:T(8,128)S(1)} %get-tuple-element.36), channel_id=1, source_target_pairs={{0,1},{1,0},{2,3},{3,2},{4,5},{5,4},{6,7},{7,6},{8,9},{9,8},{10,11... | collective-permute-start | bytes 786440 | tf_op jit(solution)/shard_map/ppermute | solution.py:29
  52.3 2.1 %collective-permute-start.7 = (f32[512,128]{1,0:T(8,128)S(1)}, f32[512,128]{1,0:T(8,128)S(1)}, u32[]{:S(2)}, u32[]{:S(2)}) collective-permute-start(f32[512,128]{1,0:T(8,128)S(1)} %bitcast.41), channel_id=1, source_target_pairs={{0,1},{1,0},{2,3},{3,2},{4,5},{5,4},{6,7},{7,6},{8,9},{9,8},{10,11... | collective-permute-start | bytes 786440 | tf_op jit(solution)/shard_map/ppermute | solution.py:29
  56.8 18.9 %all-to-all-start.3 = ((f32[8,128,128]{2,1,0:T(8,128)}), f32[8,128,128]{2,1,0:T(8,128)S(1)}, u32[]{:S(2)}, u32[]{:S(2)}) async-start(f32[8,128,128]{2,1,0:T(8,128)} %get-tuple-element.42), calls=%async_computation.3 | async-start | bytes 1048576 | tf_op jit(solution)/shard_map/all_to_all | solution.py:350
  60.4 2.1 %collective-permute-start.8 = (f32[16,64,128]{2,1,0:T(8,128)S(1)}, f32[16,64,128]{2,1,0:T(8,128)S(1)}, u32[]{:S(2)}, u32[]{:S(2)}) collective-permute-start(f32[16,64,128]{2,1,0:T(8,128)S(1)} %get-tuple-element.48), channel_id=1, source_target_pairs={{0,1},{1,0},{2,3},{3,2},{4,5},{5,4},{6,7},{7,6},{8,9},{9,8},{10,11... | collective-permute-start | bytes 1572872 | tf_op jit(solution)/shard_map/ppermute | solution.py:29
  62.4 14.8 %collective-permute-start.9 = (f32[16,64,128]{2,1,0:T(8,128)S(1)}, f32[16,64,128]{2,1,0:T(8,128)S(1)}, u32[]{:S(2)}, u32[]{:S(2)}) collective-permute-start(f32[16,64,128]{2,1,0:T(8,128)S(1)} %collective-permute-done.8.own_other_ref), channel_id=1, source_target_pairs={{0,16},{16,0},{1,17},{17,1},{2,18},{18,2},{3,19},{19,3},{4,20},{20... | collective-permute-start | bytes 1572872 | tf_op jit(solution)/shard_map/ppermute | solution.py:29
  75.7 4.6 %collective-permute-start.11 = (f32[64,128]{1,0:T(8,128)S(1)}, f32[64,128]{1,0:T(8,128)S(1)}, u32[]{:S(2)}, u32[]{:S(2)}) collective-permute-start(f32[64,128]{1,0:T(8,128)S(1)} %slice_reduce_fusion), channel_id=1, source_target_pairs={{0,16},{16,0},{1,17},{17,1},{2,18},{18,2},{3,19},{19,3},{4,20},{20... | collective-permute-start | bytes 98312 | tf_op jit(solution)/shard_map/ppermute | solution.py:29
  79.0 1.2 %collective-permute-start.10 = (f32[32,128]{1,0:T(8,128)S(1)}, f32[32,128]{1,0:T(8,128)S(1)}, u32[]{:S(2)}, u32[]{:S(2)}) collective-permute-start(f32[32,128]{1,0:T(8,128)S(1)} %get-tuple-element.45), channel_id=1, source_target_pairs={{0,1},{1,0},{2,3},{3,2},{4,5},{5,4},{6,7},{7,6},{8,9},{9,8},{10,11... | collective-permute-start | bytes 49160 | tf_op jit(solution)/shard_map/ppermute | solution.py:29
  81.0 14.5 %all-to-all-start.4 = ((f32[8,64,128]{2,1,0:T(8,128)}), f32[8,64,128]{2,1,0:T(8,128)S(1)}, u32[]{:S(2)}, u32[]{:S(2)}) async-start(f32[8,64,128]{2,1,0:T(8,128)} %broadcast_in_dim.5), calls=%async_computation.4 | async-start | bytes 524288 | tf_op jit(solution)/shard_map/all_to_all | solution.py:363
  86.3 1.2 %collective-permute-start.12 = (f32[16,256]{1,0:T(8,128)S(1)}, f32[16,256]{1,0:T(8,128)S(1)}, u32[]{:S(2)}, u32[]{:S(2)}) collective-permute-start(f32[16,256]{1,0:T(8,128)S(1)} %pad_maximum_fusion.3), channel_id=1, source_target_pairs={{0,1},{1,0},{2,3},{3,2},{4,5},{5,4},{6,7},{7,6},{8,9},{9,8},{10,11... | collective-permute-start | bytes 49160 | tf_op jit(solution)/shard_map/ppermute | solution.py:29
  96.2 1.2 %collective-permute-start.13 = (f32[32,128]{1,0:T(8,128)S(1)}, f32[32,128]{1,0:T(8,128)S(1)}, u32[]{:S(2)}, u32[]{:S(2)}) collective-permute-start(f32[32,128]{1,0:T(8,128)S(1)} %get-tuple-element.51), channel_id=1, source_target_pairs={{0,1},{1,0},{2,3},{3,2},{4,5},{5,4},{6,7},{7,6},{8,9},{9,8},{10,11... | collective-permute-start | bytes 49160 | tf_op jit(solution)/shard_map/ppermute | solution.py:29

commit v10 on v9

--- a/solution.py
+++ b/solution.py
@@ -347,6 +347,8 @@
         home, late, near_mine = lax.optimization_barrier((home, late, near_mine))
     field, term_three = fit(half, field, home, factor_three)
     residual, late = fit(1 - half, field, swap(home, "gz"), factor_three, (term_three, late))
+    if nx == 2:
+        late, own_other = lax.optimization_barrier((late, own_other))
     late = lax.all_to_all(late, "gy", 0, 0, tiled=True)
     sums = total(late[:, 2 * edge :].sum(axis=0), "gx")
     share_two, share_three = sums[: parts * half_j], sums[parts * half_j :]

time: 98.8 us -> 98.1 us (level)
  starting transfers between devices: 32.9 us -> 27.1 us
  waiting for transfers between devices: 43.2 us -> 47.5 us
    ppermute x14, starting transfers between devices: 10.5 us -> 6.73 us  [swap(): return lax.ppermute(x, axis, [(0, 1), (1, 0)])]
    all_to_all x1, waiting for transfers between devices: 11.8 us -> 14.7 us  [local(): late = lax.all_to_all(late, 'gy', 0, 0, tiled=True)]
    all_to_all x1, starting transfers between devices: 5.25 us -> 3.72 us  [local(): lax.all_to_all(jnp.broadcast_to(last[None], (ny,) + last.shape), 'gy', 0,...]
    ppermute x14, waiting for transfers between devices: 11.5 us -> 12.7 us  [swap(): return lax.ppermute(x, axis, [(0, 1), (1, 0)])]
  transfers between devices with their start and end apart: 19 -> 19, of which waited for: 12 -> 12; matrix products, arithmetic and copies ran while one was open for 3% -> 5% of each run, Pallas kernels for 12% -> 14%
where the time goes in v10:
time: 98.1 us; the launch traced here: 97.4 us
  waiting for transfers between devices  47.5 us (48%)
  starting transfers between devices  27.1 us (28%)
  Pallas kernels  13.7 us (14%)
  other arithmetic  3.55 us (4%)
  local copies, waits for them, and re-layouts  2.92 us (3%)
  matrix products  1.54 us (2%)
    all_to_all x1, waiting for transfers between devices, local(): late = lax.all_to_all(late, 'gy', 0, 0, tiled=True)  14.7 us
    ppermute x14, waiting for transfers between devices, swap(): return lax.ppermute(x, axis, [(0, 1), (1, 0)])  12.7 us
    all_to_all x1, waiting for transfers between devices, local(): lax.all_to_all(jnp.broadcast_to(last[None], (ny,) + last.shape), 'gy', 0,...  7.36 us
    all_to_all x1, waiting for transfers between devices, local(): lax.all_to_all(after_one.reshape(nz * ny, e * q, full_t), ('gz', 'gy'), 0...  7.25 us
    ppermute x14, starting transfers between devices, swap(): return lax.ppermute(x, axis, [(0, 1), (1, 0)])  6.73 us
    all_to_all x1, starting transfers between devices, local(): early = lax.all_to_all(early, 'gy', 0, 0, tiled=True)  5.84 us
    all_to_all x1, starting transfers between devices, local(): lax.all_to_all(after_one.reshape(nz * ny, e * q, full_t), ('gz', 'gy'), 0...  3.87 us
    all_to_all x1, starting transfers between devices, local(): lax.all_to_all(jnp.broadcast_to(last[None], (ny,) + last.shape), 'gy', 0,...  3.72 us
  transfers between devices with their start and end apart: 19, of which 12 were waited for; matrix products, arithmetic and copies ran while one was open for 5% of the time, Pallas kernels for 14%

profile of v10, /device:TPU:0, one launch (start us, length us, event | category | flops | bytes accessed | tf_op | source)
XLA Modules:
  0.0 97.4 jit_solution(2645327467514919824)
XLA Ops:
  0.7 1.3 %copy.16 = f32[32,32,256]{2,1,0:T(8,128)S(1)} copy(f32[32,32,256]{2,1,0:T(8,128)} %param.5) | data formatting | bytes 2097152
  1.9 3.0 %collective-permute-start.1 = (f32[32,128]{1,0:T(8,128)S(1)}, f32[32,128]{1,0:T(8,128)S(1)}, u32[]{:S(2)}, u32[]{:S(2)}) collective-permute-start(f32[32,128]{1,0:T(8,128)S(1)} %get-tuple-element.63), channel_id=1, source_target_pairs={{0,16},{16,0},{1,17},{17,1},{2,18},{18,2},{3,19},{19,3},{4,20},{20... | collective-permute-start | bytes 49160 | tf_op jit(solution)/shard_map/ppermute | solution.py:29
  5.7 1.5 %collective-permute-done = f32[512,128]{1,0:T(8,128)S(1)} collective-permute-done((f32[512,128]{1,0:T(8,128)S(1)}, f32[512,128]{1,0:T(8,128)S(1)}, u32[]{:S(2)}, u32[]{:S(2)}) %collective-permute-start) | collective-permute-done | bytes 262176 | tf_op jit(solution)/shard_map/ppermute | solution.py:29
  8.5 5.8 %all-to-all-start = ((f32[8,96,128]{2,1,0:T(8,128)}), f32[8,96,128]{2,1,0:T(8,128)S(1)}, u32[]{:S(2)}, u32[]{:S(2)}) async-start(f32[8,96,128]{2,1,0:T(8,128)} %pad_maximum_fusion), calls=%async_computation | async-start | bytes 786432 | tf_op jit(solution)/shard_map/all_to_all | solution.py:326
  14.4 1.2 %shard_map.85 = f32[32,16,128]{2,1,0:T(8,128)S(1)} custom-call(f32[32,128]{1,0:T(8,128)S(1)} %collective-permute-done.1.rows_ref, f32[32,64,128]{2,1,0:T(8,128)S(1)} %bitcast.37), custom_call_target="tpu_custom_call" | custom-call | flops 100663296 | bytes 1048576 | tf_op jit(solution)/shard_map/pallas_call | solution.py:71
  16.1 1.1 %shard_map.84 = f32[32,16,128]{2,1,0:T(8,128)S(1)} custom-call(f32[32,128]{1,0:T(8,128)S(1)} %get-tuple-element.62.rows_ref, f32[32,64,128]{2,1,0:T(8,128)S(1)} %bitcast.38), custom_call_target="tpu_custom_call" | custom-call | flops 100663296 | bytes 1048576 | tf_op jit(solution)/shard_map/pallas_call | solution.py:71
  17.3 6.4 %collective-permute-done.2 = f32[32,16,128]{2,1,0:T(8,128)S(1)} collective-permute-done((f32[32,16,128]{2,1,0:T(8,128)S(1)}, f32[32,16,128]{2,1,0:T(8,128)S(1)}, u32[]{:S(2)}, u32[]{:S(2)}) %collective-permute-start.2) | collective-permute-done | bytes 262176 | tf_op jit(solution)/shard_map/ppermute | solution.py:29
  24.4 1.9 %all-to-all-done.early_ref = f32[8,96,128]{2,1,0:T(8,128)S(1)} async-done(((f32[8,96,128]{2,1,0:T(8,128)}), f32[8,96,128]{2,1,0:T(8,128)S(1)}, u32[]{:S(2)}, u32[]{:S(2)}) %all-to-all-start) | async-done | bytes 393248 | tf_op jit(solution)/shard_map/all_to_all | solution.py:326
  26.3 3.9 %all-to-all-start.1 = ((f32[16,32,128]{2,1,0:T(8,128)}), f32[16,32,128]{2,1,0:T(8,128)S(1)}, u32[]{:S(2)}, u32[]{:S(2)}) async-start(f32[16,32,128]{2,1,0:T(8,128)} %bitcast.9), calls=%async_computation.1 | async-start | bytes 524288 | tf_op jit(solution)/shard_map/all_to_all | solution.py:337
  33.3 7.3 %all-to-all-done.1 = f32[16,32,128]{2,1,0:T(8,128)S(1)} async-done(((f32[16,32,128]{2,1,0:T(8,128)}), f32[16,32,128]{2,1,0:T(8,128)S(1)}, u32[]{:S(2)}, u32[]{:S(2)}) %all-to-all-start.1) | async-done | bytes 262176 | tf_op jit(solution)/shard_map/all_to_all | solution.py:337
  40.6 1.2 %shard_map.87 = (f32[8,2,16,256]{3,2,1,0:T(8,128)S(1)}, f32[8,2,32,128]{3,2,1,0:T(8,128)}) custom-call(f32[2,8,32,128]{3,2,1,0:T(8,128)S(1)} %bitcast.40, f32[8,2,16,256]{3,2,1,0:T(8,128)S(1)} %shard_map.86.two_ref), custom_call_target="tpu_custom_call" | custom-call | tf_op jit(solution)/shard_map/pallas_call | solution.py:116
  41.8 3.4 %all-to-all-start.2 = ((f32[8,2,32,128]{3,2,1,0:T(8,128)}), f32[8,2,32,128]{3,2,1,0:T(8,128)S(1)}, u32[]{:S(2)}, u32[]{:S(2)}) async-start(f32[8,2,32,128]{3,2,1,0:T(8,128)} %get-tuple-element.34.moved_ref), calls=%async_computation.2 | async-start | bytes 524288 | tf_op jit(solution)/shard_map/all_to_all | solution.py:342
  45.2 2.6 %shard_map.88 = (f32[8,64,128]{2,1,0:T(8,128)S(1)}, f32[8,64,128]{2,1,0:T(8,128)S(1)}) custom-call(s32[2]{0:T(128)S(1)} %pad_add_fusion.place_ref, f32[8,2,32,128]{3,2,1,0:T(8,128)} %get-tuple-element.34.moved_ref, f32[128,128]{1,0:T(8,128)S(1)} %fusion.9.gram_ref, f32[128,128]{1,0:T(8,128)S(1)} %collective-permute-done.3.gram_other_ref, ...), custom_call_target="tpu_custom_call" | custom-call | flops 1000000000 | bytes 2097152 | tf_op jit(solution)/shard_map/pallas_call | solution.py:153
  50.2 3.5 %all-to-all-done.2 = f32[8,2,32,128]{3,2,1,0:T(8,128)S(1)} async-done(((f32[8,2,32,128]{3,2,1,0:T(8,128)}), f32[8,2,32,128]{3,2,1,0:T(8,128)S(1)}, u32[]{:S(2)}, u32[]{:S(2)}) %all-to-all-start.2) | async-done | bytes 262176 | tf_op jit(solution)/shard_map/all_to_all | solution.py:342
  53.7 2.1 %shard_map.90 = (f32[1024,256]{1,0:T(8,128)}, f32[128,256]{1,0:T(8,128)S(1)}) custom-call(s32[1]{0:T(128)} %bitcast.half_ref, f32[1024,256]{1,0:T(8,128)} %bitcast.47, f32[512,128]{1,0:T(8,128)S(1)} %bitcast.42, f32[256,128]{1,0:T(8,128)S(1)} %copy-done.2), custom_call_target="tpu_custom_call", output_to_operand_aliasing={{0}: (1, {})} | custom-call | tf_op jit(solution)/shard_map/pallas_call | solution.py:223
  55.8 2.4 %shard_map.91 = (f32[1024,256]{1,0:T(8,128)}, f32[8,128,128]{2,1,0:T(8,128)}) custom-call(s32[1]{0:T(128)S(6)} %sub.10.half_ref, f32[1024,256]{1,0:T(8,128)} %get-tuple-element.40._, f32[512,128]{1,0:T(8,128)S(1)} %collective-permute-done.7.after_ref, f32[256,128]{1,0:T(8,128)S(1)} %copy-done.2, ...), custom_call_target="tpu_custom_call", output_to_operand_aliasing={{0}: (1, {}), {1}: (5, {})} | custom-call | tf_op jit(solution)/shard_map/pallas_call | solution.py:246
  58.3 3.6 %all-to-all-start.3 = ((f32[8,128,128]{2,1,0:T(8,128)}), f32[8,128,128]{2,1,0:T(8,128)S(1)}, u32[]{:S(2)}, u32[]{:S(2)}) async-start(f32[8,128,128]{2,1,0:T(8,128)} %get-tuple-element.45), calls=%async_computation.3 | async-start | bytes 1048576 | tf_op jit(solution)/shard_map/all_to_all | solution.py:352
  62.4 14.7 %all-to-all-done.3.late_ref = f32[8,128,128]{2,1,0:T(8,128)S(1)} async-done(((f32[8,128,128]{2,1,0:T(8,128)}), f32[8,128,128]{2,1,0:T(8,128)S(1)}, u32[]{:S(2)}, u32[]{:S(2)}) %all-to-all-start.3) | async-done | bytes 524320 | tf_op jit(solution)/shard_map/all_to_all | solution.py:352
  77.8 1.8 %shard_map.92 = (f32[32,128]{1,0:T(8,128)S(1)}, f32[32,128]{1,0:T(8,128)S(1)}) custom-call(s32[2]{0:T(128)S(1)} %pad_add_fusion.place_ref, f32[8,128,128]{2,1,0:T(8,128)S(1)} %all-to-all-done.3.late_ref, f32[16,64,128]{2,1,0:T(8,128)S(1)} %get-tuple-element.53.own_mine_ref, f32[16,64,128]{2,1,0:T(8,128)S(1)} %collective-permute-done.8.own_other_ref, ...), custom_call_target="tpu_custom_call" | custom-call | tf_op jit(solution)/shard_map/pallas_call | solution.py:283
  79.7 1.2 %collective-permute-done.10 = f32[32,128]{1,0:T(8,128)S(1)} collective-permute-done((f32[32,128]{1,0:T(8,128)S(1)}, f32[32,128]{1,0:T(8,128)S(1)}, u32[]{:S(2)}, u32[]{:S(2)}) %collective-permute-start.10) | collective-permute-done | bytes 16416 | tf_op jit(solution)/shard_map/ppermute | solution.py:29
  81.9 3.7 %all-to-all-start.4 = ((f32[8,64,128]{2,1,0:T(8,128)}), f32[8,64,128]{2,1,0:T(8,128)S(1)}, u32[]{:S(2)}, u32[]{:S(2)}) async-start(f32[8,64,128]{2,1,0:T(8,128)} %broadcast_in_dim.5), calls=%async_computation.4 | async-start | bytes 524288 | tf_op jit(solution)/shard_map/all_to_all | solution.py:365
  85.7 1.2 %collective-permute-done.12 = f32[16,256]{1,0:T(8,128)S(1)} collective-permute-done((f32[16,256]{1,0:T(8,128)S(1)}, f32[16,256]{1,0:T(8,128)S(1)}, u32[]{:S(2)}, u32[]{:S(2)}) %collective-permute-start.12) | collective-permute-done | bytes 16416 | tf_op jit(solution)/shard_map/ppermute | solution.py:29
  87.5 7.4 %all-to-all-done.4 = f32[8,64,128]{2,1,0:T(8,128)S(1)} async-done(((f32[8,64,128]{2,1,0:T(8,128)}), f32[8,64,128]{2,1,0:T(8,128)S(1)}, u32[]{:S(2)}, u32[]{:S(2)}) %all-to-all-start.4) | async-done | bytes 262176 | tf_op jit(solution)/shard_map/all_to_all | solution.py:365
  95.5 1.2 %collective-permute-done.13 = f32[32,128]{1,0:T(8,128)S(1)} collective-permute-done((f32[32,128]{1,0:T(8,128)S(1)}, f32[32,128]{1,0:T(8,128)S(1)}, u32[]{:S(2)}, u32[]{:S(2)}) %collective-permute-start.13) | collective-permute-done | bytes 16416 | tf_op jit(solution)/shard_map/ppermute | solution.py:29
  (60 shorter events, 13.2 us)
Async XLA Ops:
  0.6 5.0 %copy-start = (f32[32,256]{1,0:T(8,128)S(1)}, f32[32,256]{1,0:T(8,128)}, u32[]{:S(2)}) copy-start(f32[32,256]{1,0:T(8,128)} %param.8) | copy-start | bytes 98308
  0.6 1.3 %copy-start.4 = (f32[32,256]{1,0:T(8,128)S(1)}, f32[32,256]{1,0:T(8,128)}, u32[]{:S(2)}) copy-start(f32[32,256]{1,0:T(8,128)} %param.7) | copy-start | bytes 98308
  0.7 4.3 %copy-start.2 = (f32[256,128]{1,0:T(8,128)S(1)}, f32[256,128]{1,0:T(8,128)}, u32[]{:S(2)}) copy-start(f32[256,128]{1,0:T(8,128)} %factor_ref.3) | copy-start | bytes 393220
  1.9 5.2 %copy-start.3 = (f32[32,32,256]{2,1,0:T(8,128)}, f32[32,32,256]{2,1,0:T(8,128)S(1)}, u32[]{:S(2)}) copy-start(f32[32,32,256]{2,1,0:T(8,128)S(1)} %copy.16) | copy-start | bytes 3145732
  1.9 6.6 %collective-permute-start.1 = (f32[32,128]{1,0:T(8,128)S(1)}, f32[32,128]{1,0:T(8,128)S(1)}, u32[]{:S(2)}, u32[]{:S(2)}) collective-permute-start(f32[32,128]{1,0:T(8,128)S(1)} %get-tuple-element.63), channel_id=1, source_target_pairs={{0,16},{16,0},{1,17},{17,1},{2,18},{18,2},{3,19},{19,3},{4,20},{20... | collective-permute-start | bytes 49160 | tf_op jit(solution)/shard_map/ppermute | solution.py:29
  5.5 1.6 %collective-permute-start = (f32[512,128]{1,0:T(8,128)S(1)}, f32[512,128]{1,0:T(8,128)S(1)}, u32[]{:S(2)}, u32[]{:S(2)}) collective-permute-start(f32[512,128]{1,0:T(8,128)S(1)} %fusion.1), channel_id=1, source_target_pairs={{0,1},{1,0},{2,3},{3,2},{4,5},{5,4},{6,7},{7,6},{8,9},{9,8},{10,11... | collective-permute-start | bytes 786440 | tf_op jit(solution)/shard_map/ppermute | solution.py:29
  7.7 6.7 %copy-start.1 = (f32[128,32,64]{0,2,1:T(8,128)S(1)}, f32[128,32,64]{0,2,1:T(8,128)}, u32[]{:S(2)}) copy-start(f32[128,32,64]{0,2,1:T(8,128)} %param.6) | copy-start | bytes 3145732
  8.5 17.8 %all-to-all-start = ((f32[8,96,128]{2,1,0:T(8,128)}), f32[8,96,128]{2,1,0:T(8,128)S(1)}, u32[]{:S(2)}, u32[]{:S(2)}) async-start(f32[8,96,128]{2,1,0:T(8,128)} %pad_maximum_fusion), calls=%async_computation | async-start | bytes 786432 | tf_op jit(solution)/shard_map/all_to_all | solution.py:326
  15.5 8.1 %collective-permute-start.2 = (f32[32,16,128]{2,1,0:T(8,128)S(1)}, f32[32,16,128]{2,1,0:T(8,128)S(1)}, u32[]{:S(2)}, u32[]{:S(2)}) collective-permute-start(f32[32,16,128]{2,1,0:T(8,128)S(1)} %shard_map.85), channel_id=1, source_target_pairs={{0,16},{16,0},{1,17},{17,1},{2,18},{18,2},{3,19},{19,3},{4,20},{20... | collective-permute-start | bytes 786440 | tf_op jit(solution)/shard_map/ppermute | solution.py:29
  26.3 14.2 %all-to-all-start.1 = ((f32[16,32,128]{2,1,0:T(8,128)}), f32[16,32,128]{2,1,0:T(8,128)S(1)}, u32[]{:S(2)}, u32[]{:S(2)}) async-start(f32[16,32,128]{2,1,0:T(8,128)} %bitcast.9), calls=%async_computation.1 | async-start | bytes 524288 | tf_op jit(solution)/shard_map/all_to_all | solution.py:337
  30.6 2.7 %collective-permute-start.3 = (f32[128,128]{1,0:T(8,128)S(1)}, f32[128,128]{1,0:T(8,128)S(1)}, u32[]{:S(2)}, u32[]{:S(2)}) collective-permute-start(f32[128,128]{1,0:T(8,128)S(1)} %fusion.9.gram_ref), channel_id=1, source_target_pairs={{0,1},{1,0},{2,3},{3,2},{4,5},{5,4},{6,7},{7,6},{8,9},{9,8},{10,11... | collective-permute-start | bytes 196616 | tf_op jit(solution)/shard_map/ppermute | solution.py:29
  31.1 1.7 %collective-permute-start.4 = (f32[8,2,16,128]{3,2,1,0:T(8,128)S(1)}, f32[8,2,16,128]{3,2,1,0:T(8,128)S(1)}, u32[]{:S(2)}, u32[]{:S(2)}) collective-permute-start(f32[8,2,16,128]{3,2,1,0:T(8,128)S(1)} %bitcast.43), channel_id=1, source_target_pairs={{0,1},{1,0},{2,3},{3,2},{4,5},{5,4},{6,7},{7,6},{8,9},{9,8},{10,11... | collective-permute-start | bytes 393224 | tf_op jit(solution)/shard_map/ppermute | solution.py:29
  32.1 18.0 %collective-permute-start.6 = (f32[16,64,128]{2,1,0:T(8,128)S(1)}, f32[16,64,128]{2,1,0:T(8,128)S(1)}, u32[]{:S(2)}, u32[]{:S(2)}) collective-permute-start(f32[16,64,128]{2,1,0:T(8,128)S(1)} %get-tuple-element.53.own_mine_ref), channel_id=1, source_target_pairs={{0,16},{16,0},{1,17},{17,1},{2,18},{18,2},{3,19},{19,3},{4,20},{20... | collective-permute-start | bytes 1572872 | tf_op jit(solution)/shard_map/ppermute | solution.py:29
  41.8 12.0 %all-to-all-start.2 = ((f32[8,2,32,128]{3,2,1,0:T(8,128)}), f32[8,2,32,128]{3,2,1,0:T(8,128)S(1)}, u32[]{:S(2)}, u32[]{:S(2)}) async-start(f32[8,2,32,128]{3,2,1,0:T(8,128)} %get-tuple-element.34.moved_ref), calls=%async_computation.2 | async-start | bytes 524288 | tf_op jit(solution)/shard_map/all_to_all | solution.py:342
  47.8 1.6 %collective-permute-start.5 = (f32[8,64,128]{2,1,0:T(8,128)S(1)}, f32[8,64,128]{2,1,0:T(8,128)S(1)}, u32[]{:S(2)}, u32[]{:S(2)}) collective-permute-start(f32[8,64,128]{2,1,0:T(8,128)S(1)} %get-tuple-element.38), channel_id=1, source_target_pairs={{0,1},{1,0},{2,3},{3,2},{4,5},{5,4},{6,7},{7,6},{8,9},{9,8},{10,11... | collective-permute-start | bytes 786440 | tf_op jit(solution)/shard_map/ppermute | solution.py:29
  47.9 10.4 %collective-permute-start.8 = (f32[16,64,128]{2,1,0:T(8,128)}, f32[16,64,128]{2,1,0:T(8,128)S(1)}, u32[]{:S(2)}, u32[]{:S(2)}) collective-permute-start(f32[16,64,128]{2,1,0:T(8,128)} %get-tuple-element.52), channel_id=1, source_target_pairs={{0,1},{1,0},{2,3},{3,2},{4,5},{5,4},{6,7},{7,6},{8,9},{9,8},{10,11... | collective-permute-start | bytes 1572872 | tf_op jit(solution)/shard_map/ppermute | solution.py:29
  53.7 2.1 %collective-permute-start.7 = (f32[512,128]{1,0:T(8,128)S(1)}, f32[512,128]{1,0:T(8,128)S(1)}, u32[]{:S(2)}, u32[]{:S(2)}) collective-permute-start(f32[512,128]{1,0:T(8,128)S(1)} %bitcast.41), channel_id=1, source_target_pairs={{0,1},{1,0},{2,3},{3,2},{4,5},{5,4},{6,7},{7,6},{8,9},{9,8},{10,11... | collective-permute-start | bytes 786440 | tf_op jit(solution)/shard_map/ppermute | solution.py:29
  58.3 18.9 %all-to-all-start.3 = ((f32[8,128,128]{2,1,0:T(8,128)}), f32[8,128,128]{2,1,0:T(8,128)S(1)}, u32[]{:S(2)}, u32[]{:S(2)}) async-start(f32[8,128,128]{2,1,0:T(8,128)} %get-tuple-element.45), calls=%async_computation.3 | async-start | bytes 1048576 | tf_op jit(solution)/shard_map/all_to_all | solution.py:352
  61.9 15.9 %collective-permute-start.9 = (f32[16,64,128]{2,1,0:T(8,128)S(1)}, f32[16,64,128]{2,1,0:T(8,128)S(1)}, u32[]{:S(2)}, u32[]{:S(2)}) collective-permute-start(f32[16,64,128]{2,1,0:T(8,128)S(1)} %collective-permute-done.8.own_other_ref), channel_id=1, source_target_pairs={{0,16},{16,0},{1,17},{17,1},{2,18},{18,2},{3,19},{19,3},{4,20},{20... | collective-permute-start | bytes 1572872 | tf_op jit(solution)/shard_map/ppermute | solution.py:29
  77.2 4.0 %collective-permute-start.11 = (f32[64,128]{1,0:T(8,128)S(1)}, f32[64,128]{1,0:T(8,128)S(1)}, u32[]{:S(2)}, u32[]{:S(2)}) collective-permute-start(f32[64,128]{1,0:T(8,128)S(1)} %slice_reduce_fusion), channel_id=1, source_target_pairs={{0,16},{16,0},{1,17},{17,1},{2,18},{18,2},{3,19},{19,3},{4,20},{20... | collective-permute-start | bytes 98312 | tf_op jit(solution)/shard_map/ppermute | solution.py:29
  79.6 1.2 %collective-permute-start.10 = (f32[32,128]{1,0:T(8,128)S(1)}, f32[32,128]{1,0:T(8,128)S(1)}, u32[]{:S(2)}, u32[]{:S(2)}) collective-permute-start(f32[32,128]{1,0:T(8,128)S(1)} %get-tuple-element.49), channel_id=1, source_target_pairs={{0,1},{1,0},{2,3},{3,2},{4,5},{5,4},{6,7},{7,6},{8,9},{9,8},{10,11... | collective-permute-start | bytes 49160 | tf_op jit(solution)/shard_map/ppermute | solution.py:29
  81.9 13.0 %all-to-all-start.4 = ((f32[8,64,128]{2,1,0:T(8,128)}), f32[8,64,128]{2,1,0:T(8,128)S(1)}, u32[]{:S(2)}, u32[]{:S(2)}) async-start(f32[8,64,128]{2,1,0:T(8,128)} %broadcast_in_dim.5), calls=%async_computation.4 | async-start | bytes 524288 | tf_op jit(solution)/shard_map/all_to_all | solution.py:365
  85.6 1.2 %collective-permute-start.12 = (f32[16,256]{1,0:T(8,128)S(1)}, f32[16,256]{1,0:T(8,128)S(1)}, u32[]{:S(2)}, u32[]{:S(2)}) collective-permute-start(f32[16,256]{1,0:T(8,128)S(1)} %pad_maximum_fusion.3), channel_id=1, source_target_pairs={{0,1},{1,0},{2,3},{3,2},{4,5},{5,4},{6,7},{7,6},{8,9},{9,8},{10,11... | collective-permute-start | bytes 49160 | tf_op jit(solution)/shard_map/ppermute | solution.py:29
  95.5 1.2 %collective-permute-start.13 = (f32[32,128]{1,0:T(8,128)S(1)}, f32[32,128]{1,0:T(8,128)S(1)}, u32[]{:S(2)}, u32[]{:S(2)}) collective-permute-start(f32[32,128]{1,0:T(8,128)S(1)} %get-tuple-element.55), channel_id=1, source_target_pairs={{0,1},{1,0},{2,3},{3,2},{4,5},{5,4},{6,7},{7,6},{8,9},{9,8},{10,11... | collective-permute-start | bytes 49160 | tf_op jit(solution)/shard_map/ppermute | solution.py:29
